TPU v7x, 32 devices: a whole 2x2x4 slice. The times are simulated.
32 devices in a mesh: groups: 2 (over x), graph: 4 (over y, core), chan: 4 (over z).
Axes of the slice: x: 2, y: 2, z: 4, core: 2. Of those that a mesh axis runs over, the one named last changes fastest.
Arguments:
- node_embed: bfloat16 [256, 2048], P(None, ('groups', 'graph')), parts along dimension 1, may hold values from -6 to 6
- edge_embed: bfloat16 [256, 16384], P(None, ('groups', 'graph')), parts along dimension 1, may hold values from -6 to 6
- edge_vector: float32 [3, 16384], P(None, ('groups', 'graph')), parts along dimension 1, may hold values from -6 to 6
- triplet_basis: bfloat16 [16, 65536], P(None, ('groups', 'graph')), parts along dimension 1, may hold values from -6 to 6
- w_source: bfloat16 [256, 256], P(None, 'chan'), may hold values from -0.375 to 0.375
- w_target: bfloat16 [256, 256], P(None, 'chan'), may hold values from -0.375 to 0.375
- w_edge: bfloat16 [256, 256], P(None, 'chan'), may hold values from -0.375 to 0.375
- w_radial: bfloat16 [128, 256], P(None, 'chan'), may hold values from -2 to 2
- w_angle: bfloat16 [16, 256], P(None, 'chan'), may hold values from -1.5 to 1.5
- w_energy: float32 [256], P('chan'), may hold values from -0.12 to 0.12
- node_send: int32 [8, 4, 64], P('groups'), parts along dimension 0, may hold values from -1 to 255, as said below
- edge_send: int32 [8, 4, 256], P('groups'), parts along dimension 0, may hold values from -1 to 2047, as said below
- edge_target: int32 [16384], P(('groups', 'graph')), parts along dimension 0, may hold values from 0 to 255
- edge_source: int32 [16384], P(('groups', 'graph')), parts along dimension 0, may hold values from 0 to 255, as said below
- triplet_in: int32 [65536], P(('groups', 'graph')), parts along dimension 0, may hold values from 0 to 1023, as said below
- triplet_out: int32 [65536], P(('groups', 'graph')), parts along dimension 0, may hold values from 0 to 2047
Outputs:
- node_out: bfloat16 [256, 2048], P('chan', ('groups', 'graph')), parts along dimension 1
- edge_out: bfloat16 [256, 16384], P('chan', ('groups', 'graph')), parts along dimension 1
- forces: float32 [3, 2048], P(None, ('groups', 'graph')), parts along dimension 1
There are 2 independent parts, one for each index of `groups`. A program takes and returns all parts, laid end to end along the dimension named above; an argument that names none is the same for every part. Nothing has to cross between parts.
Inputs may be any that keep to these rules, and one draw needn't show every extreme that they name: node_send[q, p] lists distinct atoms of shard q (indices within that shard) sent to shard p: its first n entries, n from about 64 / 4 to 64, the rest -1. n = 64 when q = p, and for every q toward one shard p drawn anew. edge_send[q, p] lists distinct edges of shard q (indices within that shard) sent to shard p, laid out as node_send with 256 in place of 64. `edge_source`: each value is q * 64 + k where k is below the number of listed entries of node_send[q, p], p the edge's shard. `triplet_in`: each value is q * 256 + k where k is below the number of listed entries of edge_send[q, p], p the triplet's shard.
All inputs are finite; a program needn't handle non-finite values.
Results may differ from a plain program's by a relative error of at most 0.0075.
Values may be sent and summed in bfloat16 or wider, within the bound.
No kernel may reach another device: no remote copies, remote signals or barrier semaphores. Data moves between devices by JAX's collectives and lax.ppermute only.
A program may use at most 64 MiB of HBM per device.

v0:
```python
import math

import jax
import jax.numpy as jnp
from jax import lax
from jax.sharding import PartitionSpec as P

NODE_DEV = 256
EDGE_DEV = 2048


radius_max = 8.0


def silu_slope(values):
    sig = jax.nn.sigmoid(values)
    return sig * (1.0 + values * (1.0 - sig))


def radial_terms(lengths, basis_count):
    centers = jnp.arange(basis_count).astype(jnp.float32) * (radius_max / (basis_count - 1))
    spread = 4.0 * radius_max / (basis_count - 1)
    offset = (lengths[None, :] - centers[:, None]) / spread
    values = jnp.exp(-offset * offset)
    slopes = values * (-2.0 * offset / spread)
    return (values.astype(jnp.bfloat16), slopes.astype(jnp.bfloat16))


def project(weight, data):
    return jnp.einsum("dc,dn->cn", weight, data, preferred_element_type=jnp.float32)


def one_hot(index, count, dtype):
    return (index[:, None] == jnp.arange(count, dtype=jnp.int32)[None, :]).astype(dtype)


def take_cols(data, index):
    table = one_hot(index, data.shape[1], data.dtype)
    return jnp.einsum(
        "cm,nm->cn",
        data,
        table,
        preferred_element_type=jnp.float32,
        precision=lax.Precision.HIGHEST,
    )


def put_cols(values, index, count):
    table = one_hot(index, count, jnp.float32)
    return jnp.einsum(
        "cn,nm->cm",
        values,
        table,
        preferred_element_type=jnp.float32,
        precision=lax.Precision.HIGHEST,
    )


def pick_peers(data, chosen, width):
    blocks = data.reshape(data.shape[0], chosen.shape[0], width).transpose(1, 0, 2)
    picked = lax.map(lambda pair: take_cols(pair[0], pair[1]), (blocks, chosen))
    return picked.transpose(1, 0, 2).reshape(data.shape[0], -1)


def spread_peers(values, chosen, count):
    parts = values.reshape(values.shape[0], chosen.shape[0], chosen.shape[1]).transpose(1, 0, 2)
    spread = lax.map(lambda pair: put_cols(pair[0], pair[1], count), (parts, chosen))
    return spread.transpose(1, 0, 2).reshape(values.shape[0], -1)


def shards(
    node_embed,
    edge_embed,
    edge_vector,
    triplet_basis,
    w_source,
    w_target,
    w_edge,
    w_radial,
    w_angle,
    w_energy,
    node_send,
    edge_send,
    edge_target,
    edge_source,
    triplet_in,
    triplet_out,
):
    peer_count = lax.axis_size("graph")
    device = lax.axis_index("graph")
    channels = w_source.shape[1]
    first_chan = lax.axis_index("chan") * channels
    node_count = node_embed.shape[1]
    edge_count = edge_embed.shape[1]
    trip_count = triplet_basis.shape[1]
    block = math.gcd(trip_count, 256)
    turns = trip_count // block
    proj_src = project(w_source, node_embed).astype(jnp.bfloat16)
    proj_dst = project(w_target, node_embed)
    proj_edge = project(w_edge, edge_embed)
    node_shards = lax.all_gather(proj_src, "graph", axis=1, tiled=True)
    node_slots = pick_peers(node_shards, node_send[:, device], node_count).astype(jnp.bfloat16)
    src_rows = take_cols(node_slots, edge_source)
    lengths = jnp.sqrt(1.0 + jnp.sum(edge_vector * edge_vector, axis=0))
    basis, slope = radial_terms(lengths, w_radial.shape[0])
    radial = project(w_radial, basis)
    radial_rate = project(w_radial, slope)
    preact = src_rows + take_cols(proj_dst, edge_target) + proj_edge
    activated = jax.nn.silu(preact)
    message = (activated * radial).astype(jnp.bfloat16)
    edge_shards = lax.all_gather(message, "graph", axis=1, tiled=True)
    edge_slots = pick_peers(edge_shards, edge_send[:, device], edge_count).astype(jnp.bfloat16)
    slot_count = edge_slots.shape[1]

    def forward_turn(turn, total):
        start = turn * block
        in_part = lax.dynamic_slice_in_dim(triplet_in, start, block, 0)
        out_part = lax.dynamic_slice_in_dim(triplet_out, start, block, 0)
        angular = project(w_angle, lax.dynamic_slice_in_dim(triplet_basis, start, block, 1))
        term = take_cols(edge_slots, in_part) * angular
        return total + put_cols(term, out_part, edge_count)

    gathered = lax.fori_loop(0, turns, forward_turn, jnp.zeros((channels, edge_count), jnp.float32))
    own_edge = lax.dynamic_slice_in_dim(edge_embed, first_chan, channels, 0).astype(jnp.float32)
    edge_new = own_edge + message.astype(jnp.float32) + jax.nn.silu(gathered)
    scale = (NODE_DEV / EDGE_DEV) ** 0.5
    own_node = lax.dynamic_slice_in_dim(node_embed, first_chan, channels, 0).astype(jnp.float32)
    node_new = own_node + scale * put_cols(edge_new, edge_target, node_count)
    grad_node = w_energy[:, None] * silu_slope(node_new)
    grad_edge = scale * take_cols(grad_node, edge_target)
    grad_gated = grad_edge * silu_slope(gathered)

    def backward_turn(turn, total):
        start = turn * block
        in_part = lax.dynamic_slice_in_dim(triplet_in, start, block, 0)
        out_part = lax.dynamic_slice_in_dim(triplet_out, start, block, 0)
        angular = project(w_angle, lax.dynamic_slice_in_dim(triplet_basis, start, block, 1))
        term = take_cols(grad_gated, out_part) * angular
        return total + put_cols(term, in_part, slot_count)

    slot_grad = lax.fori_loop(
        0, turns, backward_turn, jnp.zeros((channels, slot_count), jnp.float32)
    )
    spread_grad = spread_peers(slot_grad, edge_send[:, device], edge_count)
    returned = lax.psum_scatter(
        spread_grad.astype(jnp.bfloat16), "graph", scatter_dimension=1, tiled=True
    ).astype(jnp.float32)
    grad_msg = grad_edge + returned
    partial_len = jnp.sum(grad_msg * activated * radial_rate, axis=0)
    grad_len = lax.psum(partial_len, "chan")
    push = grad_len[None, :] * edge_vector / lengths[None, :]
    at_target = jnp.zeros((3, node_count), jnp.float32).at[:, edge_target].add(push)
    node_cap = node_send.shape[2]
    slot_push = jnp.zeros((3, peer_count * node_cap), jnp.float32).at[:, edge_source].add(push)
    pushed_back = lax.all_to_all(slot_push, "graph", split_axis=1, concat_axis=1, tiled=True)
    own_slots = jnp.maximum(node_send[device], 0).reshape(-1)
    at_source = jnp.zeros((3, node_count), jnp.float32).at[:, own_slots].add(pushed_back)
    return (node_new.astype(jnp.bfloat16), edge_new.astype(jnp.bfloat16), at_source - at_target)


def solution(mesh):
    placed = (
        P(None, ("groups", "graph")),
        P(None, ("groups", "graph")),
        P(None, ("groups", "graph")),
        P(None, ("groups", "graph")),
        P(None, "chan"),
        P(None, "chan"),
        P(None, "chan"),
        P(None, "chan"),
        P(None, "chan"),
        P("chan"),
        P("groups", None, None),
        P("groups", None, None),
        P(("groups", "graph")),
        P(("groups", "graph")),
        P(("groups", "graph")),
        P(("groups", "graph")),
    )
    return jax.shard_map(
        shards,
        mesh=mesh,
        in_specs=placed,
        out_specs=(
            P("chan", ("groups", "graph")),
            P("chan", ("groups", "graph")),
            P(None, ("groups", "graph")),
        ),
        check_vma=False,
    )
```

profile of v0, /device:TPU:0, one launch (start us, length us, event | category | flops | bytes accessed | tf_op | source)
XLA Modules:
  0.0 395.3 jit_solution(15915088212630788051)
XLA Ops:
  8.4 6.6 %all_gather.6 = bf16[64,1024]{1,0:T(8,128)(2,1)S(1)} all-gather(bf16[64,256]{1,0:T(8,128)(2,1)S(1)} %convolution_convert_fusion), channel_id=1, replica_groups=mesh['groups'=2,'graph'=4,'chan'=4] {'graph'}, dimensions={1}, use_global_device_ids=true | all-gather | bytes 163840 | tf_op jit(solution)/shard_map/all_gather | solution.py:101
  17.9 1.4 convolution_add_fusion.3
  22.5 17.7 %all-gather.2.cloned.1.call-done = bf16[64,8192]{1,0:T(8,128)(2,1)} async-done(((bf16[64,2048]{1,0:T(8,128)(2,1)}), bf16[64,8192]{1,0:T(8,128)(2,1)}) %all-gather.2.cloned.1.call-update) | async-done | bytes 1048592 | tf_op jit(solution)/shard_map/all_gather | solution.py:111
  40.2 1.3 copy.68
  41.5 2.3 while.59
  43.9 124.7 %while.61 = (s32[]{:T(128)}, f32[64,2048]{1,0:T(8,128)S(1)}, s32[8192]{0:T(1024)}, bf16[64,1024]{1,0:T(8,128)(2,1)S(1)}, bf16[16,8192]{1,0:T(8,128)(2,1)}, /*ind...) while((s32[]{:T(128)}, f32[64,2048]{1,0:T(8,128)S(1)}, ...), condition=%wide.region_6.7_spmd.clone, body=%wide.region_5.6_spmd.clone.sunk | while | flops 437796864 | bytes 1458353 | solution.py:123
  168.6 1.8 fusion.74
  170.5 1.5 fusion.75
  172.0 2.2 multiply_multiply_fusion
  174.2 138.5 %while.62 = (s32[]{:T(128)}, f32[64,1024]{1,0:T(8,128)S(1)}, s32[8192]{0:T(1024)}, f32[64,2048]{1,0:T(8,128)S(1)}, bf16[16,8192]{1,0:T(8,128)(2,1)}, /*index=5*/...) while((s32[]{:T(128)}, f32[64,1024]{1,0:T(8,128)S(1)}, ...), condition=%wide.region_8.9_spmd.clone, body=%wide.region_7.8_spmd.clone.sunk | while | flops 605437952 | bytes 1327281 | solution.py:141
  175.0 1.3 fusion.127
  179.3 1.3 fusion.127
  183.6 1.3 fusion.127
  187.9 1.3 fusion.127
  192.3 1.3 fusion.127
  196.6 1.3 fusion.127
  200.9 1.3 fusion.127
  205.3 1.3 fusion.127
  209.6 1.3 fusion.127
  213.9 1.3 fusion.127
  218.2 1.3 fusion.127
  222.6 1.3 fusion.127
  226.9 1.3 fusion.127
  231.2 1.3 fusion.127
  244.2 1.3 fusion.127
  248.5 1.3 fusion.127
  252.9 1.3 fusion.127
  257.2 1.3 fusion.127
  261.5 1.3 fusion.127
  265.9 1.3 fusion.127
  270.2 1.3 fusion.127
  274.5 1.3 fusion.127
  278.8 1.3 fusion.127
  283.2 1.3 fusion.127
  287.5 1.3 fusion.127
  291.8 1.3 fusion.127
  296.2 1.3 fusion.127
  300.5 1.3 fusion.127
  304.8 1.3 fusion.127
  309.1 1.3 fusion.127
  312.7 4.0 %while.60 = (s32[]{:T(128)}, bf16[4,64,2048]{2,1,0:T(8,128)(2,1)S(1)}, f32[4,64,256]{2,1,0:T(8,128)S(1)}, s32[4,256]{1,0:T(4,128)S(1)}, s32[]{:T(128)}) while((s32[]{:T(128)}, bf16[4,64,2048]{2,1,0:T(8,128)(2,1)S(1)}, f32[4,64,256]{2,1,0:T(8,128)S(1)}, s32[4,256]{1,0:T(4,128)S(1)}, s32[]{:T(128)}) %tuple.135), condition=%wide.region_10.11_spmd, body=%wide.region_9.10_spmd.sunk | while | flops 403177472 | bytes 593985 | solution.py:67
  317.8 25.0 %reduce-scatter.2.cloned.1.call-done = bf16[64,2048]{1,0:T(8,128)(2,1)} async-done(((bf16[64,8192]{1,0:T(8,128)(2,1)}), bf16[64,2048]{1,0:T(8,128)(2,1)}) %reduce-scatter.2.cloned.1.call-update) | async-done | bytes 262160 | tf_op jit(solution)/shard_map/reduce_scatter | solution.py:145
  342.8 1.5 fusion.33
  344.3 11.9 %psum.7 = f32[2048]{0:T(1024)S(1)} all-reduce(f32[2048]{0:T(1024)S(1)} %fusion.33), channel_id=1, replica_groups=mesh['groups'=2,'graph'=4,'chan'=4] {'chan'}, use_global_device_ids=true, to_apply=%region_13.14 | all-reduce | flops 2048 | bytes 16384 | tf_op jit(solution)/shard_map/psum | solution.py:150
  356.6 11.5 %scatter_custom_fusion = f32[3,256]{0,1:T(8,128)S(1)} fusion(s32[2048]{0:T(1024)S(1)} %compare_select_fusion.1, f32[2048,3]{1,0:T(8,128)S(1)} %copy.52, f32[]{:T(128)} %constant.129.clone.1), kind=kCustom, calls=%fused_computation.103 | custom fusion | flops 6144 | bytes 3076 | tf_op jit(solution)/shard_map/scatter-add | solution.py:154
  368.9 3.4 all-to-all-start
  373.1 11.5 %scatter_custom_fusion.2 = f32[3,256]{0,1:T(8,128)S(1)} fusion(s32[2048]{0:T(1024)S(1)} %compare_select_fusion, f32[2048,3]{1,0:T(8,128)S(1)} %copy.52, f32[]{:T(128)} %constant.129.clone.1), kind=kCustom, calls=%fused_computation.99 | custom fusion | flops 6144 | bytes 3076 | tf_op jit(solution)/shard_map/scatter-add | solution.py:152
  386.1 1.7 scatter_custom_fusion.1
  (386 shorter events, 242.2 us)
Async XLA Ops:
  7.2 12.1 %copy-start = (bf16[256,64]{0,1:T(8,128)(2,1)S(1)}, bf16[256,64]{0,1:T(8,128)(2,1)}, u32[]{:S(2)}) copy-start(bf16[256,64]{0,1:T(8,128)(2,1)} %param.32) | copy-start | bytes 98308
  7.2 9.7 %copy-start.2 = (bf16[256,256]{1,0:T(8,128)(2,1)S(1)}, bf16[256,256]{1,0:T(8,128)(2,1)}, u32[]{:S(2)}) copy-start(bf16[256,256]{1,0:T(8,128)(2,1)} %param.26) | copy-start | bytes 393220
  7.2 9.6 %copy-start.7 = (bf16[256,64]{0,1:T(8,128)(2,1)S(1)}, bf16[256,64]{0,1:T(8,128)(2,1)}, u32[]{:S(2)}) copy-start(bf16[256,64]{0,1:T(8,128)(2,1)} %param.31) | copy-start | bytes 98308
  7.2 9.8 %copy-start.4 = (f32[3,2048]{1,0:T(4,128)S(1)}, f32[3,2048]{1,0:T(4,128)}, u32[]{:S(2)}) copy-start(f32[3,2048]{1,0:T(4,128)} %param.28) | copy-start | bytes 73732
  7.2 9.8 %copy-start.8 = (s32[2048]{0:T(1024)S(1)}, s32[2048]{0:T(1024)}, u32[]{:S(2)}) copy-start(s32[2048]{0:T(1024)} %param.39) | copy-start | bytes 24580
  7.2 33.0 %all-gather.2.cloned.1.call-start = ((), (), s32[]{:S(2)}) async-start(), calls=%async_computation.2 | async-start | bytes 1310720 | tf_op jit(solution)/shard_map/all_gather | solution.py:111
  8.4 9.5 %copy-start.6 = (s32[2048]{0:T(1024)S(1)}, s32[2048]{0:T(1024)}, u32[]{:S(2)}) copy-start(s32[2048]{0:T(1024)} %param.38) | copy-start | bytes 24580
  16.8 2.5 copy-start.5
  19.3 1.2 copy-start.9
  19.7 0.8 copy-start.11
  21.7 321.1 %reduce-scatter.2.cloned.1.call-start = ((), (), s32[]{:S(2)}) async-start(), calls=%async_computation.3 | async-start | bytes 1310720 | tf_op jit(solution)/shard_map/reduce_scatter | solution.py:145
  41.5 2.4 copy-start.3
  43.9 124.8 %copy-start.1 = (bf16[64,2048]{1,0:T(8,128)(2,1)S(1)}, bf16[64,2048]{1,0:T(8,128)(2,1)}, u32[]{:S(2)}) copy-start(bf16[64,2048]{1,0:T(8,128)(2,1)} %fusion.30) | copy-start | bytes 786436
  168.6 3.3 copy-start.10
  317.7 25.1 %copy-start.12 = (f32[64,2048]{1,0:T(8,128)S(1)}, f32[64,2048]{1,0:T(8,128)}, u32[]{:S(2)}) copy-start(f32[64,2048]{1,0:T(8,128)} %copy-done.11) | copy-start | bytes 1572868
  317.7 25.1 %copy-start.13 = (f32[64,2048]{1,0:T(8,128)S(1)}, f32[64,2048]{1,0:T(8,128)}, u32[]{:S(2)}) copy-start(f32[64,2048]{1,0:T(8,128)} %get-tuple-element.439) | copy-start | bytes 1572868
  368.9 15.7 %all-to-all-start = ((f32[4,1,192]{2,1,0:T(1,128)}), f32[4,1,192]{2,1,0:T(1,128)S(1)}, u32[]{:S(2)}, u32[]{:S(2)}) async-start(f32[4,1,192]{2,1,0:T(1,128)} %reshape.96), calls=%async_computation.1 | async-start | bytes 8192 | tf_op jit(solution)/shard_map/all_to_all | solution.py:155
Sparse Core Ops, SparseCore 0:
  21.8 18.3 all-gather.1
  317.9 24.8 reduce-scatter.1
where the time goes:
time: 402 us; the launch traced here: 395 us
  matrix products  180 us (45%)
  local copies, waits for them, and re-layouts  106 us (26%)
  waiting for transfers between devices  42.7 us (11%)
  other arithmetic  27.9 us (7%)
  blocking collectives  18.5 us (5%)
  between operations  14.5 us (4%)
    dot_general x69, matrix products, project(): jnp.einsum('dc,dn->cn', weight, data, preferred_element_type=jnp.float32)  61.9 us
    dot_general x75, matrix products, take_cols(): jnp.einsum('cm,nm->cn', data, table, preferred_element_type=jnp.float32,...  59.6 us
    dot_general x69, matrix products, put_cols(): jnp.einsum('cn,nm->cm', values, table, preferred_element_type=jnp.float32...  58.5 us
    reduce_scatter x1, waiting for transfers between devices, shards(): lax.psum_scatter(spread_grad.astype(jnp.bfloat16), 'graph', scatter_dimen...  25 us
    dynamic_slice x32, local copies, waits for them, and re-layouts, forward_turn(): out_part = lax.dynamic_slice_in_dim(triplet_out, start, block, 0)  24.5 us
    dynamic_slice x32, local copies, waits for them, and re-layouts, backward_turn(): in_part = lax.dynamic_slice_in_dim(triplet_in, start, block, 0)  24.5 us
    dynamic_slice x32, local copies, waits for them, and re-layouts, forward_turn(): in_part = lax.dynamic_slice_in_dim(triplet_in, start, block, 0)  24.5 us
    dynamic_slice x32, local copies, waits for them, and re-layouts, backward_turn(): out_part = lax.dynamic_slice_in_dim(triplet_out, start, block, 0)  24.4 us
  transfers between devices with their start and end apart: 3, of which 2 were waited for; matrix products, arithmetic and copies ran while one was open for 3% of the time, Pallas kernels for 0%

commit v1 on v0

v1 whole, which is shorter than its diff:
```python
import functools
import math

import jax
import jax.numpy as jnp
from jax import lax
from jax.experimental import pallas as pl
from jax.experimental.pallas import tpu as pltpu
from jax.sharding import PartitionSpec as P

NODE_DEV = 256
EDGE_DEV = 2048

radius_max = 8.0
MISC = 16
TERM = 8
BF = jnp.bfloat16
F32 = jnp.float32
VMEM_LIMIT = 40 * 1024 * 1024


def sigmoid(values):
    return 1.0 / (1.0 + jnp.exp(-values))


def dot_tn(weight, data):
    return lax.dot_general(weight, data, (((0,), (0,)), ((), ())), preferred_element_type=F32)


def dot_nn(left, right):
    return lax.dot_general(left, right, (((1,), (0,)), ((), ())), preferred_element_type=F32)


def dot_nt(left, right):
    return lax.dot_general(left, right, (((1,), (1,)), ((), ())), preferred_element_type=F32)


def one_hot(row, count):
    lines = lax.broadcasted_iota(jnp.int32, (count, row.shape[1]), 0)
    return jnp.where(lines == row, 1.0, 0.0).astype(BF)


def choose(stacked, group, groups):
    rows = stacked.shape[0] // groups
    out = jnp.where(group == 0, stacked[:rows], 0.0)
    for g in range(1, groups):
        out = jnp.where(group == g, stacked[g * rows : (g + 1) * rows], out)
    return out


def expand(values, group, groups):
    zero = jnp.zeros_like(values)
    return jnp.concatenate([jnp.where(group == g, values, zero) for g in range(groups)], axis=0)


def halves(values):
    high = values.astype(BF)
    return high, (values - high.astype(F32)).astype(BF)


def radial_terms(squared, weight):
    count = weight.shape[0]
    lengths = jnp.sqrt(1.0 + squared)
    spread = 4.0 * radius_max / (count - 1)
    lines = lax.broadcasted_iota(jnp.int32, (count, 1), 0).astype(F32)
    centers = lines * (radius_max / (count - 1))
    offset = (lengths - centers) * (1.0 / spread)
    values = jnp.exp(-offset * offset)
    slopes = values * (offset * (-2.0 / spread))
    return dot_tn(weight, values.astype(BF)), dot_tn(weight, slopes.astype(BF)), lengths


def squared_length(vector):
    return vector[0:1] * vector[0:1] + vector[1:2] * vector[1:2] + vector[2:3] * vector[2:3]


def prep_kernel(
    node, edge, vector, w_source, w_target, w_edge, node_send, edge_send, target, source, part_out, misc_out, *sends
):
    me = lax.axis_index("graph")
    peers = len(sends)
    channels = w_source.shape[1]
    edges = edge.shape[1]
    cap = node_send.shape[2]
    high_count = 4
    low_count = edges // high_count
    atoms = node[...]
    proj_src = dot_tn(w_source[...], atoms).astype(BF)
    dst_high, dst_low = halves(dot_tn(w_target[...], atoms))
    dst_table = jnp.concatenate([dst_high, dst_low], axis=0)
    own_nodes = jnp.concatenate([node_send[q, pl.ds(me, 1), :] for q in range(peers)], axis=0)
    own_nodes = own_nodes.astype(F32).astype(BF)
    parts = []
    for h in range(high_count):
        cols = slice(h * low_count, (h + 1) * low_count)
        dst = target[:, cols]
        src = source[:, cols]
        rows = dot_nn(dst_table, one_hot(dst, atoms.shape[1]))
        part = rows[:channels] + rows[channels:] + dot_tn(w_edge[...], edge[:, cols])
        part_out[:, cols] = part
        src_peer = src // cap
        by_peer = dot_nn(own_nodes, one_hot(src - src_peer * cap, cap))
        src_node = choose(by_peer, src_peer, peers)
        vec = vector[:, cols]
        first = vec.astype(BF).astype(F32)
        second = (vec - first).astype(BF).astype(F32)
        third = vec - first - second
        misc = jnp.concatenate(
            [
                first,
                second,
                third,
                dst.astype(F32),
                src_node,
                src_peer.astype(F32),
                jnp.zeros((MISC - 12, low_count), F32),
            ],
            axis=0,
        )
        misc_out[:, cols] = misc
        parts.append(jnp.concatenate([part.astype(BF), misc.astype(BF)], axis=0))
    table = jnp.concatenate(parts, axis=0)
    for d in range(peers):
        chosen = edge_send[me, pl.ds(jnp.bitwise_xor(me, d), 1), :]
        high = jnp.where(chosen < 0, -1, chosen // low_count)
        picked = choose(dot_nn(table, one_hot(chosen % low_count, low_count)), high, high_count)
        sends[d][:channels] = proj_src
        sends[d][channels:] = picked.astype(BF)


def local_kernel(vector, w_radial, radial_out, rate_out):
    edges = vector.shape[1]
    width = min(512, edges)
    for start in range(0, edges, width):
        cols = slice(start, start + width)
        radial, rate, _ = radial_terms(squared_length(vector[:, cols]), w_radial[...])
        radial_out[:, cols] = radial
        rate_out[:, cols] = rate


def main_kernel(
    peers,
    ecap,
    scale,
    part,
    misc,
    radial,
    rate,
    vector,
    node,
    edge,
    basis,
    w_radial,
    w_angle,
    w_energy,
    trip_in,
    trip_out,
    target,
    *refs,
):
    received = refs[:peers]
    node_out, edge_out, force_out = refs[peers : peers + 3]
    message, own_rate, slot_rate, slot_table, angular, gather_sum, grad_table, edge_grad, slot_sum, moves = refs[peers + 3 :]
    me = lax.axis_index("graph")
    channels, edges = part.shape
    nodes = node.shape[1]
    trips = basis.shape[1]
    first_chan = pl.multiple_of(lax.axis_index("chan") * channels, channels)
    groups = slot_table.shape[0] // channels
    low_in = slot_table.shape[1]
    low_out = edges // groups
    step = 512
    width = 256

    src_table = jnp.concatenate([received[d][:channels] for d in range(peers)], axis=0)

    def src_rows(src_node, src_peer):
        rows = dot_nn(src_table, one_hot(src_node, nodes))
        return choose(rows, jnp.bitwise_xor(src_peer, me), peers)

    for start in range(0, edges, step):
        cols = slice(start, start + step)
        rows = src_rows(misc[10:11, cols].astype(jnp.int32), misc[11:12, cols].astype(jnp.int32))
        preact = rows + part[:, cols]
        active = preact * sigmoid(preact)
        message[:, cols] = (active * radial[:, cols]).astype(BF)
        own_rate[:, cols] = active * rate[:, cols]
    slots = []
    for d in range(peers):
        cols = slice(d * ecap, (d + 1) * ecap)
        extra = received[d][channels:].astype(F32)
        rest = extra[channels:]
        vec = rest[0:3] + rest[3:6] + rest[6:9]
        src_node = rest[10:11].astype(jnp.int32)
        src_peer = rest[11:12].astype(jnp.int32)
        slot_radial, slot_slope, lengths = radial_terms(squared_length(vec), w_radial[...])
        preact = src_rows(src_node, src_peer) + extra[:channels]
        active = preact * sigmoid(preact)
        place = d * ecap
        low = place % low_in
        slot_table[(place // low_in) * channels : (place // low_in + 1) * channels, low : low + ecap] = (
            active * slot_radial
        ).astype(BF)
        slot_rate[:, cols] = active * slot_slope
        slots.append((vec / lengths, src_node, src_peer, rest[9:10].astype(jnp.int32)))

    def split_in(cols):
        place = jnp.bitwise_xor(trip_in[:, cols], me * ecap)
        high = place // low_in
        return high, one_hot(place - high * low_in, low_in)

    def split_out(cols):
        place = trip_out[:, cols]
        high = place // low_out
        return high, one_hot(place - high * low_out, low_out)

    gather_sum[...] = jnp.zeros_like(gather_sum)
    weight = w_angle[...]

    def forward(turn, carry):
        total = None
        for sub in range(step // width):
            cols = pl.ds(pl.multiple_of(turn * step + sub * width, width), width)
            high_in, hot_in = split_in(cols)
            high_out, hot_out = split_out(cols)
            angle = dot_tn(weight, basis[:, cols])
            angular[:, cols] = angle
            term = (choose(dot_nn(slot_table[...], hot_in), high_in, groups) * angle).astype(BF)
            more = dot_nt(hot_out, expand(term, high_out, groups))
            total = more if total is None else total + more
        gather_sum[...] += total
        return carry

    lax.fori_loop(0, trips // step, forward, 0)

    gathered = gather_sum[...].T
    atom_sum = jnp.zeros((channels, nodes), F32)
    for g in range(groups):
        cols = slice(g * low_out, (g + 1) * low_out)
        value = gathered[g * channels : (g + 1) * channels]
        own_edge = edge[pl.ds(first_chan, channels), cols].astype(F32)
        fresh = own_edge + message[:, cols].astype(F32) + value * sigmoid(value)
        edge_out[:, cols] = fresh.astype(BF)
        high, low = halves(fresh)
        sums = dot_nt(jnp.concatenate([high, low], axis=0), one_hot(target[:, cols], nodes))
        atom_sum += sums[:channels] + sums[channels:]
    node_new = node[pl.ds(first_chan, channels), :].astype(F32) + scale * atom_sum
    node_out[...] = node_new.astype(BF)
    sig = sigmoid(node_new)
    grad_node = w_energy[...] * (sig * (1.0 + node_new * (1.0 - sig))) * scale
    high, low = halves(grad_node)
    grad_pair = jnp.concatenate([high, low], axis=0)
    pushes = []
    for g in range(groups):
        cols = slice(g * low_out, (g + 1) * low_out)
        value = gathered[g * channels : (g + 1) * channels]
        rows = dot_nn(grad_pair, one_hot(target[:, cols], nodes))
        grad_edge = rows[:channels] + rows[channels:]
        sig = sigmoid(value)
        grad_table[g * channels : (g + 1) * channels, :] = (
            grad_edge * (sig * (1.0 + value * (1.0 - sig)))
        ).astype(BF)
        edge_grad[:, cols] = jnp.sum(grad_edge * own_rate[:, cols], axis=0, keepdims=True)

    slot_sum[...] = jnp.zeros_like(slot_sum)

    def backward(turn, carry):
        total = None
        for sub in range(step // width):
            cols = pl.ds(pl.multiple_of(turn * step + sub * width, width), width)
            high_in, hot_in = split_in(cols)
            high_out, hot_out = split_out(cols)
            term = (choose(dot_nn(grad_table[...], hot_out), high_out, groups) * angular[:, cols]).astype(BF)
            more = dot_nt(hot_in, expand(term, high_in, groups))
            total = more if total is None else total + more
        slot_sum[...] += total
        return carry

    lax.fori_loop(0, trips // step, backward, 0)

    moves[...] = jnp.zeros_like(moves)

    def push_terms(push):
        high = push.astype(BF).astype(F32)
        return jnp.concatenate([high, push - high, jnp.zeros((TERM - 6, push.shape[1]), F32)], axis=0)

    for start in range(0, edges, step):
        cols = slice(start, start + step)
        vec = vector[:, cols]
        terms = push_terms(vec * (edge_grad[:, cols] / jnp.sqrt(1.0 + squared_length(vec))))
        src_peer = jnp.bitwise_xor(misc[11:12, cols].astype(jnp.int32), me)
        moves[...] += dot_nt(
            expand(terms, src_peer, peers).astype(BF), one_hot(misc[10:11, cols].astype(jnp.int32), nodes)
        )
        moves[:TERM] -= dot_nt(
            jnp.concatenate([terms, jnp.zeros_like(terms)], axis=0).astype(BF), one_hot(target[:, cols], nodes)
        )[:TERM]
    slot_grad = slot_sum[...].T
    for d in range(peers):
        cols = slice(d * ecap, (d + 1) * ecap)
        place = d * ecap
        low = place % low_in
        grads = slot_grad[(place // low_in) * channels : (place // low_in + 1) * channels, low : low + ecap]
        unit, src_node, src_peer, dst_node = slots[d]
        terms = push_terms(unit * jnp.sum(grads * slot_rate[:, cols], axis=0, keepdims=True))
        moves[...] += dot_nt(
            expand(terms, jnp.bitwise_xor(src_peer, me), peers).astype(BF), one_hot(src_node, nodes)
        )
        moves[d * TERM : (d + 1) * TERM] -= dot_nt(
            jnp.concatenate([terms, jnp.zeros_like(terms)], axis=0).astype(BF), one_hot(dst_node, nodes)
        )[:TERM]
    force_out[...] = moves[...].reshape(force_out.shape)


def exchange(values, axis, distance):
    count = lax.axis_size(axis)
    return lax.ppermute(values, axis, [(i, i ^ distance) for i in range(count)])


def add_over(values, axis):
    count = lax.axis_size(axis)
    if count <= 4:
        others = [exchange(values, axis, d) for d in range(1, count)]
        return functools.reduce(jnp.add, others, values)
    for bit in range(count.bit_length() - 1):
        values = values + exchange(values, axis, 1 << bit)
    return values


def shards(
    node_embed,
    edge_embed,
    edge_vector,
    triplet_basis,
    w_source,
    w_target,
    w_edge,
    w_radial,
    w_angle,
    w_energy,
    node_send,
    edge_send,
    edge_target,
    edge_source,
    triplet_in,
    triplet_out,
):
    peers = lax.axis_size("graph")
    channels = w_source.shape[1]
    nodes = node_embed.shape[1]
    edges = edge_embed.shape[1]
    trips = triplet_basis.shape[1]
    ecap = edge_send.shape[2]
    groups = 256 // channels
    low_in = peers * ecap // groups
    low_out = edges // groups
    target = edge_target.reshape(1, edges)
    source = edge_source.reshape(1, edges)
    params = pltpu.CompilerParams(vmem_limit_bytes=VMEM_LIMIT)
    part, misc, *sends = pl.pallas_call(
        prep_kernel,
        name="prep",
        out_shape=[
            jax.ShapeDtypeStruct((channels, edges), F32),
            jax.ShapeDtypeStruct((MISC, edges), F32),
        ]
        + [jax.ShapeDtypeStruct((2 * channels + MISC, ecap), BF)] * peers,
        compiler_params=params,
    )(node_embed, edge_embed, edge_vector, w_source, w_target, w_edge, node_send, edge_send, target, source)
    received = [sends[0]] + [exchange(sends[d], "graph", d) for d in range(1, peers)]
    radial, rate = pl.pallas_call(
        local_kernel,
        name="local",
        out_shape=[jax.ShapeDtypeStruct((channels, edges), F32)] * 2,
        compiler_params=params,
        cost_estimate=pl.CostEstimate(flops=2**28, bytes_accessed=2**21, transcendentals=2**18),
    )(edge_vector, w_radial)
    node_out, edge_out, force = pl.pallas_call(
        functools.partial(main_kernel, peers, ecap, math.sqrt(NODE_DEV / EDGE_DEV)),
        name="main",
        out_shape=[
            jax.ShapeDtypeStruct((channels, nodes), BF),
            jax.ShapeDtypeStruct((channels, edges), BF),
            jax.ShapeDtypeStruct((peers, TERM, nodes), F32),
        ],
        scratch_shapes=[
            pltpu.VMEM((channels, edges), BF),
            pltpu.VMEM((channels, edges), F32),
            pltpu.VMEM((channels, peers * ecap), F32),
            pltpu.VMEM((groups * channels, low_in), BF),
            pltpu.VMEM((channels, trips), F32),
            pltpu.VMEM((low_out, groups * channels), F32),
            pltpu.VMEM((groups * channels, low_out), BF),
            pltpu.VMEM((1, edges), F32),
            pltpu.VMEM((low_in, groups * channels), F32),
            pltpu.VMEM((peers * TERM, nodes), F32),
        ],
        compiler_params=params,
    )(
        part,
        misc,
        radial,
        rate,
        edge_vector,
        node_embed,
        edge_embed,
        triplet_basis,
        w_radial,
        w_angle,
        w_energy.reshape(channels, 1),
        triplet_in.reshape(1, trips),
        triplet_out.reshape(1, trips),
        target,
        *received,
    )
    mine = force[0]
    for d in range(1, peers):
        mine = mine + exchange(force[d], "graph", d)
    mine = add_over(mine, "chan")
    return node_out, edge_out, mine[0:3] + mine[3:6]


def solution(mesh):
    placed = (
        P(None, ("groups", "graph")),
        P(None, ("groups", "graph")),
        P(None, ("groups", "graph")),
        P(None, ("groups", "graph")),
        P(None, "chan"),
        P(None, "chan"),
        P(None, "chan"),
        P(None, "chan"),
        P(None, "chan"),
        P("chan"),
        P("groups", None, None),
        P("groups", None, None),
        P(("groups", "graph")),
        P(("groups", "graph")),
        P(("groups", "graph")),
        P(("groups", "graph")),
    )
    return jax.shard_map(
        shards,
        mesh=mesh,
        in_specs=placed,
        out_specs=(
            P("chan", ("groups", "graph")),
            P("chan", ("groups", "graph")),
            P(None, ("groups", "graph")),
        ),
        check_vma=False,
    )
```

time: 402 us -> 52.5 us (0.13); the launches traced: 395 us -> 52.1 us
  matrix products: 180 us -> 0 us
  local copies, waits for them, and re-layouts: 106 us -> 5.18 us
  waiting for transfers between devices: 42.7 us -> 9.52 us
  other arithmetic: 27.9 us -> 0.61 us
  Pallas kernels: 0 us -> 26.3 us
  blocking collectives: 18.5 us -> 0 us
  between operations: 14.5 us -> 0.78 us
  starting transfers between devices: 3.51 us -> 9.71 us
    dot_general x213 -> x0, matrix products: 180 us -> none  [the longest x69 61.9 us: project(): jnp.einsum('dc,dn->cn', weight, data, preferred_element_type=jnp.float32)]
    dynamic_slice x138 -> x0, local copies, waits for them, and re-layouts: 99.5 us -> none  [the longest x32 24.5 us: forward_turn(): out_part = lax.dynamic_slice_in_dim(triplet_out, start, block, 0)]
    pallas_call x0 -> x3, Pallas kernels: none -> 26.3 us  [the longest x1 24.5 us: shards(): pl.pallas_call(functools.partial(main_kernel, peers, ecap, math.sqrt(NODE...]
    reduce_scatter x1 -> x0, waiting for transfers between devices: 25 us -> none  [shards(): lax.psum_scatter(spread_grad.astype(jnp.bfloat16), 'graph', scatter_dimen...]
    scatter-add x3 -> x0, other arithmetic: 24.6 us -> none  [the longest x1 11.5 us: shards(): jnp.zeros((3, peer_count * node_cap), jnp.float32).at[:, edge_source]]
    all_gather x1 -> x0, waiting for transfers between devices: 17.7 us -> none  [shards(): edge_shards = lax.all_gather(message, 'graph', axis=1, tiled=True)]
    psum x1 -> x0, blocking collectives: 11.9 us -> none  [shards(): grad_len = lax.psum(partial_len, 'chan')]
    ppermute x0 -> x9, starting transfers between devices: none -> 9.71 us  [exchange(): return lax.ppermute(values, axis, [(i, i ^ distance) for i in range(count)])]
  transfers between devices with their start and end apart: 3 -> 9, of which waited for: 2 -> 6; matrix products, arithmetic and copies ran while one was open for 3% -> 0% of each run, Pallas kernels for 0% -> 1%
where the time goes in v1:
time: 52.5 us; the launch traced here: 52.1 us
  Pallas kernels  26.3 us (50%)
  starting transfers between devices  9.71 us (18%)
  waiting for transfers between devices  9.52 us (18%)
  local copies, waits for them, and re-layouts  5.18 us (10%)
  between operations  0.78 us (1%)
  other arithmetic  0.61 us (1%)
    pallas_call x1, Pallas kernels, shards(): pl.pallas_call(functools.partial(main_kernel, peers, ecap, math.sqrt(NODE...  24.5 us
    ppermute x9, starting transfers between devices, exchange(): return lax.ppermute(values, axis, [(i, i ^ distance) for i in range(count)])  9.71 us
    ppermute x9, waiting for transfers between devices, exchange(): return lax.ppermute(values, axis, [(i, i ^ distance) for i in range(count)])  9.52 us
    unnamed x36, local copies, waits for them, and re-layouts  5.08 us
    pallas_call x1, Pallas kernels, shards(): pl.pallas_call(prep_kernel, name='prep', out_shape=[jax.ShapeDtypeStruct(...  1.19 us
  transfers between devices with their start and end apart: 9, of which 6 were waited for; matrix products, arithmetic and copies ran while one was open for 0% of the time, Pallas kernels for 1%

profile of v1, /device:TPU:0, one launch (start us, length us, event | category | flops | bytes accessed | tf_op | source)
XLA Modules:
  0.0 52.1 jit_solution(9488310908442507773)
XLA Ops:
  0.6 0.0 copy-start.12
  0.6 0.0 copy-start.2
  0.7 0.9 %copy.19.w_source = bf16[256,64]{1,0:T(8,128)(2,1)S(1)} copy(bf16[256,64]{0,1:T(8,128)(2,1)} %param.20) | data formatting | bytes 65536 | tf_op args[4]
  1.6 0.0 copy-done.12
  1.6 0.0 copy-start.13
  1.6 0.1 copy.20.w_target
  1.7 0.6 %copy-done.13 = bf16[256,64]{0,1:T(8,128)(2,1)S(1)} copy-done((bf16[256,64]{0,1:T(8,128)(2,1)S(1)}, bf16[256,64]{0,1:T(8,128)(2,1)}, u32[]{:S(2)}) %copy-start.13) | copy-done | bytes 32792
  2.3 0.0 copy-start.10
  2.4 0.1 copy.21.w_edge
  2.5 0.0 copy-done.2
  2.5 0.6 %copy-done.4 = f32[3,2048]{1,0:T(4,128)S(1)} copy-done((f32[3,2048]{1,0:T(4,128)S(1)}, f32[3,2048]{1,0:T(4,128)}, u32[]{:S(2)}) %copy-start.4) | copy-done | bytes 24600
  3.1 0.0 copy-done.7
  3.1 0.0 copy-done.8
  3.1 0.0 copy-done.9
  3.1 0.0 copy-done.10
  3.1 0.0 copy-start
  3.1 1.2 %copy-done = bf16[256,2048]{1,0:T(8,128)(2,1)S(1)} copy-done((bf16[256,2048]{1,0:T(8,128)(2,1)S(1)}, bf16[256,2048]{1,0:T(8,128)(2,1)}, u32[]{:S(2)}) %copy-start) | copy-done | bytes 1048600
  4.3 1.2 %prep.1 = (f32[64,2048]{1,0:T(8,128)S(1)}, f32[16,2048]{1,0:T(8,128)S(1)}, bf16[144,256]{1,0:T(8,128)(2,1)S(1)}, bf16[144,256]{1,0:T(8,128)(2,1)S(1)}, bf16[144,...) custom-call(bf16[256,256]{1,0:T(8,128)(2,1)S(1)} %copy-done.2, bf16[256,2048]{1,0:T(8,128)(2,1)S(1)} %copy-done, ...), custom_call_target="tpu_custom_call" | custom-call | tf_op jit(solution)/shard_map/prep/pallas_call | solution.py:360
  5.5 0.5 collective-permute-start
  6.1 2.6 %collective-permute-start.1 = (bf16[144,256]{1,0:T(8,128)(2,1)S(1)}, bf16[144,256]{1,0:T(8,128)(2,1)S(1)}, u32[]{:S(2)}, u32[]{:S(2)}) collective-permute-start(bf16[144,256]{1,0:T(8,128)(2,1)S(1)} %get-tuple-element.20), channel_id=1, source_target_pairs={{0,8},{4,12},{8,0},{12,4},{1,9},{5,13},{9,1},{13,5},{2,10},{6,14},... | collective-permute-start | bytes 221192 | tf_op jit(solution)/shard_map/ppermute | solution.py:317
  8.6 0.1 collective-permute-start.2
  8.7 0.0 copy-done.14
  8.7 0.1 copy.22.w_radial
  8.8 0.0 copy-start.15
  8.8 0.7 %copy-done.15 = f32[64]{0:T(128)S(1)} copy-done((f32[64]{0:T(128)S(1)}, f32[64]{0:T(128)}, u32[]{:S(2)}) %copy-start.15) | copy-done | bytes 280
  9.5 0.1 copy.24.w_energy
  9.6 0.0 copy-start.6
  9.6 0.6 %local.1 = (f32[64,2048]{1,0:T(8,128)S(1)}, f32[64,2048]{1,0:T(8,128)S(1)}) custom-call(f32[3,2048]{1,0:T(4,128)S(1)} %copy-done.4, bf16[128,64]{1,0:T(8,128)(2,1)S(1)} %copy.22.w_radial), custom_call_target="tpu_custom_call" | custom-call | flops 268435456 | bytes 2097152 | tf_op jit(solution)/shard_map/local/pallas_call | solution.py:371
  10.3 0.0 collective-permute-done.refs_1_
  10.3 1.2 %collective-permute-done.1.refs_2_ = bf16[144,256]{1,0:T(8,128)(2,1)S(1)} collective-permute-done((bf16[144,256]{1,0:T(8,128)(2,1)S(1)}, bf16[144,256]{1,0:T(8,128)(2,1)S(1)}, u32[]{:S(2)}, u32[]{:S(2)}) %collective-permute-start.1) | collective-permute-done | bytes 73760 | tf_op jit(solution)/shard_map/ppermute | solution.py:317
  11.5 1.4 %collective-permute-done.2.refs_3_ = bf16[144,256]{1,0:T(8,128)(2,1)S(1)} collective-permute-done((bf16[144,256]{1,0:T(8,128)(2,1)S(1)}, bf16[144,256]{1,0:T(8,128)(2,1)S(1)}, u32[]{:S(2)}, u32[]{:S(2)}) %collective-permute-start.2) | collective-permute-done | bytes 73760 | tf_op jit(solution)/shard_map/ppermute | solution.py:317
  12.9 0.0 copy-done.1
  12.9 0.0 copy-done.6
  12.9 0.7 %copy-done.11 = bf16[16,64]{1,0:T(8,128)(2,1)S(1)} copy-done((bf16[16,64]{1,0:T(8,128)(2,1)S(1)}, bf16[16,64]{1,0:T(8,128)(2,1)}, u32[]{:S(2)}) %copy-start.11) | copy-done | bytes 2072
  13.6 24.5 %main.1 = (bf16[64,256]{1,0:T(8,128)(2,1)}, bf16[64,2048]{1,0:T(8,128)(2,1)}, f32[4,8,256]{2,1,0:T(8,128)S(1)}) custom-call(f32[64,2048]{1,0:T(8,128)S(1)} %get-tuple-element.14.part, f32[16,2048]{1,0:T(8,128)S(1)} %get-tuple-element.15.misc, f32[64,2048]{1,0:T(8,128)S(1)} %get-tuple-element.16.radial, f32[64,2048]{1,0:T(8,128)S(1)} %get-tuple-element.17.rate, ...), custom_call_target="tpu_custom_call" | custom-call | tf_op jit(solution)/shard_map/main/pallas_call | solution.py:378
  38.1 0.2 collective-permute-start.3
  38.2 1.5 %collective-permute-start.5 = (f32[8,256]{1,0:T(8,128)S(1)}, f32[8,256]{1,0:T(8,128)S(1)}, u32[]{:S(2)}, u32[]{:S(2)}) collective-permute-start(f32[8,256]{1,0:T(8,128)S(1)} %get-tuple-element.26), channel_id=1, source_target_pairs={{0,12},{4,8},{8,4},{12,0},{1,13},{5,9},{9,5},{13,1},{2,14},{6,10},... | collective-permute-start | bytes 24584 | tf_op jit(solution)/shard_map/ppermute | solution.py:317
  39.7 0.5 collective-permute-start.4
  40.2 0.0 collective-permute-done.3
  40.2 1.1 %collective-permute-done.5 = f32[8,256]{1,0:T(8,128)S(1)} collective-permute-done((f32[8,256]{1,0:T(8,128)S(1)}, f32[8,256]{1,0:T(8,128)S(1)}, u32[]{:S(2)}, u32[]{:S(2)}) %collective-permute-start.5) | collective-permute-done | bytes 8224 | tf_op jit(solution)/shard_map/ppermute | solution.py:317
  41.3 2.0 %collective-permute-done.4 = f32[8,256]{1,0:T(8,128)S(1)} collective-permute-done((f32[8,256]{1,0:T(8,128)S(1)}, f32[8,256]{1,0:T(8,128)S(1)}, u32[]{:S(2)}, u32[]{:S(2)}) %collective-permute-start.4) | collective-permute-done | bytes 8224 | tf_op jit(solution)/shard_map/ppermute | solution.py:317
  43.4 3.6 %collective-permute-start.8 = (f32[8,256]{1,0:T(8,128)S(1)}, f32[8,256]{1,0:T(8,128)S(1)}, u32[]{:S(2)}, u32[]{:S(2)}) collective-permute-start(f32[8,256]{1,0:T(8,128)S(1)} %fusion.1), channel_id=1, source_target_pairs={{0,3},{1,2},{2,1},{3,0},{4,7},{5,6},{6,5},{7,4},{8,11},{9,10},{10,... | collective-permute-start | bytes 24584 | tf_op jit(solution)/shard_map/ppermute | solution.py:317
  47.0 0.0 collective-permute-start.7
  47.0 0.8 %collective-permute-start.6 = (f32[8,256]{1,0:T(8,128)S(1)}, f32[8,256]{1,0:T(8,128)S(1)}, u32[]{:S(2)}, u32[]{:S(2)}) collective-permute-start(f32[8,256]{1,0:T(8,128)S(1)} %fusion.1), channel_id=1, source_target_pairs={{0,1},{1,0},{2,3},{3,2},{4,5},{5,4},{6,7},{7,6},{8,9},{9,8},{10,11... | collective-permute-start | bytes 24584 | tf_op jit(solution)/shard_map/ppermute | solution.py:317
  47.8 1.1 %collective-permute-done.8 = f32[8,256]{1,0:T(8,128)S(1)} collective-permute-done((f32[8,256]{1,0:T(8,128)S(1)}, f32[8,256]{1,0:T(8,128)S(1)}, u32[]{:S(2)}, u32[]{:S(2)}) %collective-permute-start.8) | collective-permute-done | bytes 8224 | tf_op jit(solution)/shard_map/ppermute | solution.py:317
  48.8 2.7 %collective-permute-done.7 = f32[8,256]{1,0:T(8,128)S(1)} collective-permute-done((f32[8,256]{1,0:T(8,128)S(1)}, f32[8,256]{1,0:T(8,128)S(1)}, u32[]{:S(2)}, u32[]{:S(2)}) %collective-permute-start.7) | collective-permute-done | bytes 8224 | tf_op jit(solution)/shard_map/ppermute | solution.py:317
  51.5 0.0 collective-permute-done.6
  51.5 0.6 %slice_add_fusion = f32[3,256]{1,0:T(4,128)} fusion(f32[8,256]{1,0:T(8,128)S(1)} %add_add_fusion), kind=kLoop, calls=%fused_computation.7 | loop fusion | flops 768 | bytes 9216 | tf_op jit(solution)/shard_map/add | solution.py:420
  (14 shorter events, 0.0 us)
Async XLA Ops:
  0.6 0.9 %copy-start.12 = (bf16[256,64]{0,1:T(8,128)(2,1)S(1)}, bf16[256,64]{0,1:T(8,128)(2,1)}, u32[]{:S(2)}) copy-start(bf16[256,64]{0,1:T(8,128)(2,1)} %param.21) | copy-start | bytes 98308
  0.6 1.8 %copy-start.2 = (bf16[256,256]{1,0:T(8,128)(2,1)S(1)}, bf16[256,256]{1,0:T(8,128)(2,1)}, u32[]{:S(2)}) copy-start(bf16[256,256]{1,0:T(8,128)(2,1)} %node.3) | copy-start | bytes 393220
  1.6 0.8 %copy-start.13 = (bf16[256,64]{0,1:T(8,128)(2,1)S(1)}, bf16[256,64]{0,1:T(8,128)(2,1)}, u32[]{:S(2)}) copy-start(bf16[256,64]{0,1:T(8,128)(2,1)} %param.22) | copy-start | bytes 98308
  2.3 0.8 %copy-start.4 = (f32[3,2048]{1,0:T(4,128)S(1)}, f32[3,2048]{1,0:T(4,128)}, u32[]{:S(2)}) copy-start(f32[3,2048]{1,0:T(4,128)} %vector.5) | copy-start | bytes 73732
  2.3 0.8 %copy-start.7 = (s32[2048]{0:T(1024)S(1)}, s32[2048]{0:T(1024)}, u32[]{:S(2)}) copy-start(s32[2048]{0:T(1024)} %param.28) | copy-start | bytes 24580
  2.3 0.8 %copy-start.8 = (s32[4,4,256]{2,1,0:T(4,128)S(1)}, s32[4,4,256]{2,1,0:T(4,128)}, u32[]{:S(2)}) copy-start(s32[4,4,256]{2,1,0:T(4,128)} %edge_send.1) | copy-start | bytes 49156
  2.3 0.8 %copy-start.9 = (s32[4,4,64]{2,1,0:T(4,128)S(1)}, s32[4,4,64]{2,1,0:T(4,128)}, u32[]{:S(2)}) copy-start(s32[4,4,64]{2,1,0:T(4,128)} %node_send.1) | copy-start | bytes 12292
  2.3 0.8 %copy-start.10 = (s32[2048]{0:T(1024)S(1)}, s32[2048]{0:T(1024)}, u32[]{:S(2)}) copy-start(s32[2048]{0:T(1024)} %param.29) | copy-start | bytes 24580
  3.1 1.2 %copy-start = (bf16[256,2048]{1,0:T(8,128)(2,1)S(1)}, bf16[256,2048]{1,0:T(8,128)(2,1)}, u32[]{:S(2)}) copy-start(bf16[256,2048]{1,0:T(8,128)(2,1)} %edge.3) | copy-start | bytes 3145732
  4.3 4.4 %copy-start.14 = (bf16[128,64]{0,1:T(8,128)(2,1)S(1)}, bf16[128,64]{0,1:T(8,128)(2,1)}, u32[]{:S(2)}) copy-start(bf16[128,64]{0,1:T(8,128)(2,1)} %param.23) | copy-start | bytes 49156
  4.3 8.5 %copy-start.1 = (bf16[256,2048]{1,0:T(8,128)(2,1)S(1)}, bf16[256,2048]{1,0:T(8,128)(2,1)}, u32[]{:S(2)}) copy-start(bf16[256,2048]{1,0:T(8,128)(2,1)} %edge.3) | copy-start | bytes 3145732
  5.5 4.7 %collective-permute-start = (bf16[144,256]{1,0:T(8,128)(2,1)S(1)}, bf16[144,256]{1,0:T(8,128)(2,1)S(1)}, u32[]{:S(2)}, u32[]{:S(2)}) collective-permute-start(bf16[144,256]{1,0:T(8,128)(2,1)S(1)} %get-tuple-element.19), channel_id=1, source_target_pairs={{0,4},{4,0},{8,12},{12,8},{1,5},{5,1},{9,13},{13,9},{2,6},{6,2},{1... | collective-permute-start | bytes 221192 | tf_op jit(solution)/shard_map/ppermute | solution.py:317
  6.1 5.5 %collective-permute-start.1 = (bf16[144,256]{1,0:T(8,128)(2,1)S(1)}, bf16[144,256]{1,0:T(8,128)(2,1)S(1)}, u32[]{:S(2)}, u32[]{:S(2)}) collective-permute-start(bf16[144,256]{1,0:T(8,128)(2,1)S(1)} %get-tuple-element.20), channel_id=1, source_target_pairs={{0,8},{4,12},{8,0},{12,4},{1,9},{5,13},{9,1},{13,5},{2,10},{6,14},... | collective-permute-start | bytes 221192 | tf_op jit(solution)/shard_map/ppermute | solution.py:317
  8.6 4.2 %collective-permute-start.2 = (bf16[144,256]{1,0:T(8,128)(2,1)S(1)}, bf16[144,256]{1,0:T(8,128)(2,1)S(1)}, u32[]{:S(2)}, u32[]{:S(2)}) collective-permute-start(bf16[144,256]{1,0:T(8,128)(2,1)S(1)} %get-tuple-element.21), channel_id=1, source_target_pairs={{0,12},{4,8},{8,4},{12,0},{1,13},{5,9},{9,5},{13,1},{2,14},{6,10},... | collective-permute-start | bytes 221192 | tf_op jit(solution)/shard_map/ppermute | solution.py:317
  8.8 0.7 %copy-start.15 = (f32[64]{0:T(128)S(1)}, f32[64]{0:T(128)}, u32[]{:S(2)}) copy-start(f32[64]{0:T(128)} %param.25) | copy-start | bytes 772
  9.6 3.3 %copy-start.3 = (bf16[16,8192]{1,0:T(8,128)(2,1)S(1)}, bf16[16,8192]{1,0:T(8,128)(2,1)}, u32[]{:S(2)}) copy-start(bf16[16,8192]{1,0:T(8,128)(2,1)} %basis.1) | copy-start | bytes 786436
  9.6 3.3 %copy-start.5 = (s32[8192]{0:T(1024)S(1)}, s32[8192]{0:T(1024)}, u32[]{:S(2)}) copy-start(s32[8192]{0:T(1024)} %param.30) | copy-start | bytes 98308
  9.6 3.3 %copy-start.6 = (s32[8192]{0:T(1024)S(1)}, s32[8192]{0:T(1024)}, u32[]{:S(2)}) copy-start(s32[8192]{0:T(1024)} %param.31) | copy-start | bytes 98308
  12.9 0.7 %copy-start.11 = (bf16[16,64]{1,0:T(8,128)(2,1)S(1)}, bf16[16,64]{1,0:T(8,128)(2,1)}, u32[]{:S(2)}) copy-start(bf16[16,64]{1,0:T(8,128)(2,1)} %w_angle.1) | copy-start | bytes 6148
  38.1 2.1 %collective-permute-start.3 = (f32[8,256]{1,0:T(8,128)S(1)}, f32[8,256]{1,0:T(8,128)S(1)}, u32[]{:S(2)}, u32[]{:S(2)}) collective-permute-start(f32[8,256]{1,0:T(8,128)S(1)} %get-tuple-element.25), channel_id=1, source_target_pairs={{0,4},{4,0},{8,12},{12,8},{1,5},{5,1},{9,13},{13,9},{2,6},{6,2},{1... | collective-permute-start | bytes 24584 | tf_op jit(solution)/shard_map/ppermute | solution.py:317
  38.2 3.1 %collective-permute-start.5 = (f32[8,256]{1,0:T(8,128)S(1)}, f32[8,256]{1,0:T(8,128)S(1)}, u32[]{:S(2)}, u32[]{:S(2)}) collective-permute-start(f32[8,256]{1,0:T(8,128)S(1)} %get-tuple-element.26), channel_id=1, source_target_pairs={{0,12},{4,8},{8,4},{12,0},{1,13},{5,9},{9,5},{13,1},{2,14},{6,10},... | collective-permute-start | bytes 24584 | tf_op jit(solution)/shard_map/ppermute | solution.py:317
  39.7 3.7 %collective-permute-start.4 = (f32[8,256]{1,0:T(8,128)S(1)}, f32[8,256]{1,0:T(8,128)S(1)}, u32[]{:S(2)}, u32[]{:S(2)}) collective-permute-start(f32[8,256]{1,0:T(8,128)S(1)} %get-tuple-element.27), channel_id=1, source_target_pairs={{0,8},{4,12},{8,0},{12,4},{1,9},{5,13},{9,1},{13,5},{2,10},{6,14},... | collective-permute-start | bytes 24584 | tf_op jit(solution)/shard_map/ppermute | solution.py:317
  43.4 5.4 %collective-permute-start.8 = (f32[8,256]{1,0:T(8,128)S(1)}, f32[8,256]{1,0:T(8,128)S(1)}, u32[]{:S(2)}, u32[]{:S(2)}) collective-permute-start(f32[8,256]{1,0:T(8,128)S(1)} %fusion.1), channel_id=1, source_target_pairs={{0,3},{1,2},{2,1},{3,0},{4,7},{5,6},{6,5},{7,4},{8,11},{9,10},{10,... | collective-permute-start | bytes 24584 | tf_op jit(solution)/shard_map/ppermute | solution.py:317
  47.0 4.5 %collective-permute-start.7 = (f32[8,256]{1,0:T(8,128)S(1)}, f32[8,256]{1,0:T(8,128)S(1)}, u32[]{:S(2)}, u32[]{:S(2)}) collective-permute-start(f32[8,256]{1,0:T(8,128)S(1)} %fusion.1), channel_id=1, source_target_pairs={{0,2},{1,3},{2,0},{3,1},{4,6},{5,7},{6,4},{7,5},{8,10},{9,11},{10,... | collective-permute-start | bytes 24584 | tf_op jit(solution)/shard_map/ppermute | solution.py:317
  47.0 4.5 %collective-permute-start.6 = (f32[8,256]{1,0:T(8,128)S(1)}, f32[8,256]{1,0:T(8,128)S(1)}, u32[]{:S(2)}, u32[]{:S(2)}) collective-permute-start(f32[8,256]{1,0:T(8,128)S(1)} %fusion.1), channel_id=1, source_target_pairs={{0,1},{1,0},{2,3},{3,2},{4,5},{5,4},{6,7},{7,6},{8,9},{9,8},{10,11... | collective-permute-start | bytes 24584 | tf_op jit(solution)/shard_map/ppermute | solution.py:317

commit v2 on v1

--- a/solution.py
+++ b/solution.py
@@ -59,7 +59,7 @@
 
 
 def radial_terms(squared, weight):
-    count = weight.shape[0]
+    count = weight.shape[1]
     lengths = jnp.sqrt(1.0 + squared)
     spread = 4.0 * radius_max / (count - 1)
     lines = lax.broadcasted_iota(jnp.int32, (count, 1), 0).astype(F32)
@@ -67,7 +67,7 @@
     offset = (lengths - centers) * (1.0 / spread)
     values = jnp.exp(-offset * offset)
     slopes = values * (offset * (-2.0 / spread))
-    return dot_tn(weight, values.astype(BF)), dot_tn(weight, slopes.astype(BF)), lengths
+    return dot_nn(weight, values.astype(BF)), dot_nn(weight, slopes.astype(BF)), lengths
 
 
 def squared_length(vector):
@@ -75,18 +75,35 @@
 
 
 def prep_kernel(
-    node, edge, vector, w_source, w_target, w_edge, node_send, edge_send, target, source, part_out, misc_out, *sends
+    node,
+    edge,
+    vector,
+    w_source,
+    w_target,
+    w_edge,
+    node_send,
+    edge_send,
+    target,
+    source,
+    part_out,
+    misc_out,
+    own_node_out,
+    own_edge_out,
+    *sends,
 ):
     me = lax.axis_index("graph")
     peers = len(sends)
-    channels = w_source.shape[1]
+    channels = w_source.shape[0]
+    first_chan = pl.multiple_of(lax.axis_index("chan") * channels, channels)
     edges = edge.shape[1]
     cap = node_send.shape[2]
     high_count = 4
     low_count = edges // high_count
     atoms = node[...]
-    proj_src = dot_tn(w_source[...], atoms).astype(BF)
-    dst_high, dst_low = halves(dot_tn(w_target[...], atoms))
+    own_node_out[...] = node[pl.ds(first_chan, channels), :]
+    own_edge_out[...] = edge[pl.ds(first_chan, channels), :]
+    proj_src = dot_nn(w_source[...], atoms).astype(BF)
+    dst_high, dst_low = halves(dot_nn(w_target[...], atoms))
     dst_table = jnp.concatenate([dst_high, dst_low], axis=0)
     own_nodes = jnp.concatenate([node_send[q, pl.ds(me, 1), :] for q in range(peers)], axis=0)
     own_nodes = own_nodes.astype(F32).astype(BF)
@@ -96,7 +113,7 @@
         dst = target[:, cols]
         src = source[:, cols]
         rows = dot_nn(dst_table, one_hot(dst, atoms.shape[1]))
-        part = rows[:channels] + rows[channels:] + dot_tn(w_edge[...], edge[:, cols])
+        part = rows[:channels] + rows[channels:] + dot_nn(w_edge[...], edge[:, cols])
         part_out[:, cols] = part
         src_peer = src // cap
         by_peer = dot_nn(own_nodes, one_hot(src - src_peer * cap, cap))
@@ -165,12 +182,12 @@
     channels, edges = part.shape
     nodes = node.shape[1]
     trips = basis.shape[1]
-    first_chan = pl.multiple_of(lax.axis_index("chan") * channels, channels)
     groups = slot_table.shape[0] // channels
     low_in = slot_table.shape[1]
     low_out = edges // groups
     step = 512
-    width = 256
+    width = min(1024, trips)
+    turn_width = min(4096, trips)
 
     src_table = jnp.concatenate([received[d][:channels] for d in range(peers)], axis=0)
 
@@ -219,8 +236,8 @@
 
     def forward(turn, carry):
         total = None
-        for sub in range(step // width):
-            cols = pl.ds(pl.multiple_of(turn * step + sub * width, width), width)
+        for sub in range(turn_width // width):
+            cols = pl.ds(pl.multiple_of(turn * turn_width + sub * width, width), width)
             high_in, hot_in = split_in(cols)
             high_out, hot_out = split_out(cols)
             angle = dot_tn(weight, basis[:, cols])
@@ -231,23 +248,26 @@
         gather_sum[...] += total
         return carry
 
-    lax.fori_loop(0, trips // step, forward, 0)
+    lax.fori_loop(0, trips // turn_width, forward, 0)
 
     gathered = gather_sum[...].T
     atom_sum = jnp.zeros((channels, nodes), F32)
     for g in range(groups):
         cols = slice(g * low_out, (g + 1) * low_out)
         value = gathered[g * channels : (g + 1) * channels]
-        own_edge = edge[pl.ds(first_chan, channels), cols].astype(F32)
+        own_edge = edge[:, cols].astype(F32)
         fresh = own_edge + message[:, cols].astype(F32) + value * sigmoid(value)
         edge_out[:, cols] = fresh.astype(BF)
         high, low = halves(fresh)
         sums = dot_nt(jnp.concatenate([high, low], axis=0), one_hot(target[:, cols], nodes))
         atom_sum += sums[:channels] + sums[channels:]
-    node_new = node[pl.ds(first_chan, channels), :].astype(F32) + scale * atom_sum
+    lines = lax.broadcasted_iota(jnp.int32, (channels, channels), 0)
+    diagonal = lines == lax.broadcasted_iota(jnp.int32, (channels, channels), 1)
+    energy = jnp.sum(jnp.where(diagonal, w_energy[...], 0.0), axis=1, keepdims=True)
+    node_new = node[...].astype(F32) + scale * atom_sum
     node_out[...] = node_new.astype(BF)
     sig = sigmoid(node_new)
-    grad_node = w_energy[...] * (sig * (1.0 + node_new * (1.0 - sig))) * scale
+    grad_node = energy * (sig * (1.0 + node_new * (1.0 - sig))) * scale
     high, low = halves(grad_node)
     grad_pair = jnp.concatenate([high, low], axis=0)
     pushes = []
@@ -266,8 +286,8 @@
 
     def backward(turn, carry):
         total = None
-        for sub in range(step // width):
-            cols = pl.ds(pl.multiple_of(turn * step + sub * width, width), width)
+        for sub in range(turn_width // width):
+            cols = pl.ds(pl.multiple_of(turn * turn_width + sub * width, width), width)
             high_in, hot_in = split_in(cols)
             high_out, hot_out = split_out(cols)
             term = (choose(dot_nn(grad_table[...], hot_out), high_out, groups) * angular[:, cols]).astype(BF)
@@ -276,7 +296,7 @@
         slot_sum[...] += total
         return carry
 
-    lax.fori_loop(0, trips // step, backward, 0)
+    lax.fori_loop(0, trips // turn_width, backward, 0)
 
     moves[...] = jnp.zeros_like(moves)
 
@@ -357,16 +377,18 @@
     target = edge_target.reshape(1, edges)
     source = edge_source.reshape(1, edges)
     params = pltpu.CompilerParams(vmem_limit_bytes=VMEM_LIMIT)
-    part, misc, *sends = pl.pallas_call(
+    part, misc, own_node, own_edge, *sends = pl.pallas_call(
         prep_kernel,
         name="prep",
         out_shape=[
             jax.ShapeDtypeStruct((channels, edges), F32),
             jax.ShapeDtypeStruct((MISC, edges), F32),
+            jax.ShapeDtypeStruct((channels, nodes), BF),
+            jax.ShapeDtypeStruct((channels, edges), BF),
         ]
         + [jax.ShapeDtypeStruct((2 * channels + MISC, ecap), BF)] * peers,
         compiler_params=params,
-    )(node_embed, edge_embed, edge_vector, w_source, w_target, w_edge, node_send, edge_send, target, source)
+    )(node_embed, edge_embed, edge_vector, w_source.T, w_target.T, w_edge.T, node_send, edge_send, target, source)
     received = [sends[0]] + [exchange(sends[d], "graph", d) for d in range(1, peers)]
     radial, rate = pl.pallas_call(
         local_kernel,
@@ -374,7 +396,7 @@
         out_shape=[jax.ShapeDtypeStruct((channels, edges), F32)] * 2,
         compiler_params=params,
         cost_estimate=pl.CostEstimate(flops=2**28, bytes_accessed=2**21, transcendentals=2**18),
-    )(edge_vector, w_radial)
+    )(edge_vector, w_radial.T)
     node_out, edge_out, force = pl.pallas_call(
         functools.partial(main_kernel, peers, ecap, math.sqrt(NODE_DEV / EDGE_DEV)),
         name="main",
@@ -402,21 +424,21 @@
         radial,
         rate,
         edge_vector,
-        node_embed,
-        edge_embed,
+        own_node,
+        own_edge,
         triplet_basis,
-        w_radial,
+        w_radial.T,
         w_angle,
-        w_energy.reshape(channels, 1),
+        w_energy.reshape(1, channels),
         triplet_in.reshape(1, trips),
         triplet_out.reshape(1, trips),
         target,
         *received,
     )
+    force = add_over(force, "chan")
     mine = force[0]
     for d in range(1, peers):
         mine = mine + exchange(force[d], "graph", d)
-    mine = add_over(mine, "chan")
     return node_out, edge_out, mine[0:3] + mine[3:6]
 
 

time: 52.5 us -> 46 us (0.88)
  Pallas kernels: 26.3 us -> 14.9 us
  local copies, waits for them, and re-layouts: 5.18 us -> 8.65 us
  waiting for transfers between devices: 9.52 us -> 10.6 us
    pallas_call x1, Pallas kernels: 24.5 us -> 13.1 us  [shards(): pl.pallas_call(functools.partial(main_kernel, peers, ecap, math.sqrt(NODE...]
    unnamed x36 -> x34, local copies, waits for them, and re-layouts: 5.08 us -> 8.65 us
    ppermute x9, waiting for transfers between devices: 9.52 us -> 10.6 us  [exchange(): return lax.ppermute(values, axis, [(i, i ^ distance) for i in range(count)])]
where the time goes in v2:
time: 46 us; the launch traced here: 45.3 us
  Pallas kernels  14.9 us (32%)
  waiting for transfers between devices  10.6 us (23%)
  starting transfers between devices  9.8 us (21%)
  local copies, waits for them, and re-layouts  8.65 us (19%)
  between operations  0.72 us (2%)
  other arithmetic  0.62 us (1%)
    pallas_call x1, Pallas kernels, shards(): pl.pallas_call(functools.partial(main_kernel, peers, ecap, math.sqrt(NODE...  13.1 us
    ppermute x9, waiting for transfers between devices, exchange(): return lax.ppermute(values, axis, [(i, i ^ distance) for i in range(count)])  10.6 us
    ppermute x9, starting transfers between devices, exchange(): return lax.ppermute(values, axis, [(i, i ^ distance) for i in range(count)])  9.8 us
    unnamed x34, local copies, waits for them, and re-layouts  8.65 us
    pallas_call x1, Pallas kernels, shards(): pl.pallas_call(prep_kernel, name='prep', out_shape=[jax.ShapeDtypeStruct(...  1.17 us
  transfers between devices with their start and end apart: 9, of which 6 were waited for; matrix products, arithmetic and copies ran while one was open for 0% of the time, Pallas kernels for 1%

profile of v2, /device:TPU:0, one launch (start us, length us, event | category | flops | bytes accessed | tf_op | source)
XLA Modules:
  0.0 45.3 jit_solution(17808619949877858030)
XLA Ops:
  0.6 0.0 copy-start.7
  0.6 0.7 %copy-done.7 = s32[2048]{0:T(1024)S(1)} copy-done((s32[2048]{0:T(1024)S(1)}, s32[2048]{0:T(1024)}, u32[]{:S(2)}) %copy-start.7) | copy-done | bytes 8216
  1.3 0.0 copy-start
  1.3 1.2 %copy-done = bf16[256,2048]{1,0:T(8,128)(2,1)S(1)} copy-done((bf16[256,2048]{1,0:T(8,128)(2,1)S(1)}, bf16[256,2048]{1,0:T(8,128)(2,1)}, u32[]{:S(2)}) %copy-start) | copy-done | bytes 1048600
  2.6 0.0 copy-start.2
  2.6 0.8 %copy-done.2 = f32[3,2048]{1,0:T(4,128)S(1)} copy-done((f32[3,2048]{1,0:T(4,128)S(1)}, f32[3,2048]{1,0:T(4,128)}, u32[]{:S(2)}) %copy-start.2) | copy-done | bytes 24600
  3.3 0.0 copy-start.4
  3.3 0.9 %copy-done.4 = bf16[256,256]{1,0:T(8,128)(2,1)S(1)} copy-done((bf16[256,256]{1,0:T(8,128)(2,1)S(1)}, bf16[256,256]{1,0:T(8,128)(2,1)}, u32[]{:S(2)}) %copy-start.4) | copy-done | bytes 131096
  4.2 0.0 copy-start.8
  4.2 0.8 %copy-done.8 = bf16[256,64]{0,1:T(8,128)(2,1)S(1)} copy-done((bf16[256,64]{0,1:T(8,128)(2,1)S(1)}, bf16[256,64]{0,1:T(8,128)(2,1)}, u32[]{:S(2)}) %copy-start.8) | copy-done | bytes 32792
  5.0 0.0 copy-start.9
  5.0 0.8 %copy-done.9 = bf16[256,64]{0,1:T(8,128)(2,1)S(1)} copy-done((bf16[256,64]{0,1:T(8,128)(2,1)S(1)}, bf16[256,64]{0,1:T(8,128)(2,1)}, u32[]{:S(2)}) %copy-start.9) | copy-done | bytes 32792
  5.7 0.0 copy-start.10
  5.7 0.8 %copy-done.10 = bf16[256,64]{0,1:T(8,128)(2,1)S(1)} copy-done((bf16[256,64]{0,1:T(8,128)(2,1)S(1)}, bf16[256,64]{0,1:T(8,128)(2,1)}, u32[]{:S(2)}) %copy-start.10) | copy-done | bytes 32792
  6.5 0.0 copy-start.11
  6.5 0.7 %copy-done.11 = s32[4,4,256]{2,1,0:T(4,128)S(1)} copy-done((s32[4,4,256]{2,1,0:T(4,128)S(1)}, s32[4,4,256]{2,1,0:T(4,128)}, u32[]{:S(2)}) %copy-start.11) | copy-done | bytes 16408
  7.2 0.7 %copy-done.13 = s32[4,4,64]{2,1,0:T(4,128)S(1)} copy-done((s32[4,4,64]{2,1,0:T(4,128)S(1)}, s32[4,4,64]{2,1,0:T(4,128)}, u32[]{:S(2)}) %copy-start.13) | copy-done | bytes 4120
  7.9 0.7 %copy-done.14 = s32[2048]{0:T(1024)S(1)} copy-done((s32[2048]{0:T(1024)S(1)}, s32[2048]{0:T(1024)}, u32[]{:S(2)}) %copy-start.14) | copy-done | bytes 8216
  8.6 1.2 %prep.1 = (f32[64,2048]{1,0:T(8,128)S(1)}, f32[16,2048]{1,0:T(8,128)S(1)}, bf16[64,256]{1,0:T(8,128)(2,1)S(1)}, bf16[64,2048]{1,0:T(8,128)(2,1)S(1)}, bf16[144,2...) custom-call(bf16[256,256]{1,0:T(8,128)(2,1)S(1)} %copy-done.4, ...), custom_call_target="tpu_custom_call" | custom-call | tf_op jit(solution)/shard_map/prep/pallas_call | solution.py:380
  9.8 0.5 %collective-permute-start = (bf16[144,256]{1,0:T(8,128)(2,1)S(1)}, bf16[144,256]{1,0:T(8,128)(2,1)S(1)}, u32[]{:S(2)}, u32[]{:S(2)}) collective-permute-start(bf16[144,256]{1,0:T(8,128)(2,1)S(1)} %get-tuple-element.23), channel_id=1, source_target_pairs={{0,4},{4,0},{8,12},{12,8},{1,5},{5,1},{9,13},{13,9},{2,6},{6,2},{1... | collective-permute-start | bytes 221192 | tf_op jit(solution)/shard_map/ppermute | solution.py:337
  10.3 2.6 %collective-permute-start.1 = (bf16[144,256]{1,0:T(8,128)(2,1)S(1)}, bf16[144,256]{1,0:T(8,128)(2,1)S(1)}, u32[]{:S(2)}, u32[]{:S(2)}) collective-permute-start(bf16[144,256]{1,0:T(8,128)(2,1)S(1)} %get-tuple-element.24), channel_id=1, source_target_pairs={{0,8},{4,12},{8,0},{12,4},{1,9},{5,13},{9,1},{13,5},{2,10},{6,14},... | collective-permute-start | bytes 221192 | tf_op jit(solution)/shard_map/ppermute | solution.py:337
  12.9 0.1 collective-permute-start.2
  13.0 0.0 copy-done.3
  13.0 0.0 copy-done.12
  13.0 0.0 copy-start.6
  13.0 0.6 %local.1 = (f32[64,2048]{1,0:T(8,128)S(1)}, f32[64,2048]{1,0:T(8,128)S(1)}) custom-call(f32[3,2048]{1,0:T(4,128)S(1)} %copy-done.3, bf16[64,128]{1,0:T(8,128)(2,1)S(1)} %bitcast.30), custom_call_target="tpu_custom_call" | custom-call | flops 268435456 | bytes 2097152 | tf_op jit(solution)/shard_map/local/pallas_call | solution.py:393
  13.6 0.0 collective-permute-done.refs_1_
  13.6 2.1 %collective-permute-done.1.refs_2_ = bf16[144,256]{1,0:T(8,128)(2,1)S(1)} collective-permute-done((bf16[144,256]{1,0:T(8,128)(2,1)S(1)}, bf16[144,256]{1,0:T(8,128)(2,1)S(1)}, u32[]{:S(2)}, u32[]{:S(2)}) %collective-permute-start.1) | collective-permute-done | bytes 73760 | tf_op jit(solution)/shard_map/ppermute | solution.py:337
  15.8 1.4 %collective-permute-done.2.refs_3_ = bf16[144,256]{1,0:T(8,128)(2,1)S(1)} collective-permute-done((bf16[144,256]{1,0:T(8,128)(2,1)S(1)}, bf16[144,256]{1,0:T(8,128)(2,1)S(1)}, u32[]{:S(2)}, u32[]{:S(2)}) %collective-permute-start.2) | collective-permute-done | bytes 73760 | tf_op jit(solution)/shard_map/ppermute | solution.py:337
  17.1 0.0 copy-done.1
  17.1 0.0 copy-done.5
  17.1 0.0 copy-done.6
  17.2 0.7 %copy-done.15 = bf16[16,64]{1,0:T(8,128)(2,1)S(1)} copy-done((bf16[16,64]{1,0:T(8,128)(2,1)S(1)}, bf16[16,64]{1,0:T(8,128)(2,1)}, u32[]{:S(2)}) %copy-start.15) | copy-done | bytes 2072
  17.8 0.0 copy-done.16
  17.8 13.1 %main.1 = (bf16[64,256]{1,0:T(8,128)(2,1)}, bf16[64,2048]{1,0:T(8,128)(2,1)}, f32[4,8,256]{2,1,0:T(8,128)S(1)}) custom-call(f32[64,2048]{1,0:T(8,128)S(1)} %get-tuple-element.16.part, f32[16,2048]{1,0:T(8,128)S(1)} %get-tuple-element.17.misc, f32[64,2048]{1,0:T(8,128)S(1)} %get-tuple-element.18.radial, f32[64,2048]{1,0:T(8,128)S(1)} %get-tuple-element.19.rate, ...), custom_call_target="tpu_custom_call" | custom-call | tf_op jit(solution)/shard_map/main/pallas_call | solution.py:400
  30.9 3.8 %collective-permute-start.5 = (f32[4,8,256]{2,1,0:T(8,128)S(1)}, f32[4,8,256]{2,1,0:T(8,128)S(1)}, u32[]{:S(2)}, u32[]{:S(2)}) collective-permute-start(f32[4,8,256]{2,1,0:T(8,128)S(1)} %get-tuple-element.28), channel_id=1, source_target_pairs={{0,3},{1,2},{2,1},{3,0},{4,7},{5,6},{6,5},{7,4},{8,11},{9,10},{10,... | collective-permute-start | bytes 98312 | tf_op jit(solution)/shard_map/ppermute | solution.py:337
  34.7 0.0 collective-permute-start.4
  34.7 0.6 %collective-permute-start.3 = (f32[4,8,256]{2,1,0:T(8,128)S(1)}, f32[4,8,256]{2,1,0:T(8,128)S(1)}, u32[]{:S(2)}, u32[]{:S(2)}) collective-permute-start(f32[4,8,256]{2,1,0:T(8,128)S(1)} %get-tuple-element.28), channel_id=1, source_target_pairs={{0,1},{1,0},{2,3},{3,2},{4,5},{5,4},{6,7},{7,6},{8,9},{9,8},{10,11... | collective-permute-start | bytes 98312 | tf_op jit(solution)/shard_map/ppermute | solution.py:337
  35.3 1.3 %collective-permute-done.5 = f32[4,8,256]{2,1,0:T(8,128)S(1)} collective-permute-done((f32[4,8,256]{2,1,0:T(8,128)S(1)}, f32[4,8,256]{2,1,0:T(8,128)S(1)}, u32[]{:S(2)}, u32[]{:S(2)}) %collective-permute-start.5) | collective-permute-done | bytes 32800 | tf_op jit(solution)/shard_map/ppermute | solution.py:337
  36.7 2.9 %collective-permute-done.4 = f32[4,8,256]{2,1,0:T(8,128)S(1)} collective-permute-done((f32[4,8,256]{2,1,0:T(8,128)S(1)}, f32[4,8,256]{2,1,0:T(8,128)S(1)}, u32[]{:S(2)}, u32[]{:S(2)}) %collective-permute-start.4) | collective-permute-done | bytes 32800 | tf_op jit(solution)/shard_map/ppermute | solution.py:337
  39.6 0.0 collective-permute-done.3
  39.6 0.1 collective-permute-start.6
  39.7 1.4 %collective-permute-start.8 = (f32[8,256]{1,0:T(8,128)S(1)}, f32[8,256]{1,0:T(8,128)S(1)}, u32[]{:S(2)}, u32[]{:S(2)}) collective-permute-start(f32[8,256]{1,0:T(8,128)S(1)} %get-tuple-element.30), channel_id=1, source_target_pairs={{0,12},{4,8},{8,4},{12,0},{1,13},{5,9},{9,5},{13,1},{2,14},{6,10},... | collective-permute-start | bytes 24584 | tf_op jit(solution)/shard_map/ppermute | solution.py:337
  41.1 0.7 %collective-permute-start.7 = (f32[8,256]{1,0:T(8,128)S(1)}, f32[8,256]{1,0:T(8,128)S(1)}, u32[]{:S(2)}, u32[]{:S(2)}) collective-permute-start(f32[8,256]{1,0:T(8,128)S(1)} %get-tuple-element.31), channel_id=1, source_target_pairs={{0,8},{4,12},{8,0},{12,4},{1,9},{5,13},{9,1},{13,5},{2,10},{6,14},... | collective-permute-start | bytes 24584 | tf_op jit(solution)/shard_map/ppermute | solution.py:337
  41.8 0.0 collective-permute-done.6
  41.8 1.0 %collective-permute-done.8 = f32[8,256]{1,0:T(8,128)S(1)} collective-permute-done((f32[8,256]{1,0:T(8,128)S(1)}, f32[8,256]{1,0:T(8,128)S(1)}, u32[]{:S(2)}, u32[]{:S(2)}) %collective-permute-start.8) | collective-permute-done | bytes 8224 | tf_op jit(solution)/shard_map/ppermute | solution.py:337
  42.8 1.9 %collective-permute-done.7 = f32[8,256]{1,0:T(8,128)S(1)} collective-permute-done((f32[8,256]{1,0:T(8,128)S(1)}, f32[8,256]{1,0:T(8,128)S(1)}, u32[]{:S(2)}, u32[]{:S(2)}) %collective-permute-start.7) | collective-permute-done | bytes 8224 | tf_op jit(solution)/shard_map/ppermute | solution.py:337
  44.7 0.6 %slice_add_fusion = f32[3,256]{1,0:T(4,128)} fusion(f32[8,256]{1,0:T(8,128)S(1)} %fusion.2), kind=kLoop, calls=%fused_computation.8 | loop fusion | flops 768 | bytes 9216 | tf_op jit(solution)/shard_map/add | solution.py:442
  (11 shorter events, 0.0 us)
Async XLA Ops:
  0.6 0.7 %copy-start.7 = (s32[2048]{0:T(1024)S(1)}, s32[2048]{0:T(1024)}, u32[]{:S(2)}) copy-start(s32[2048]{0:T(1024)} %param.28) | copy-start | bytes 24580
  1.3 1.2 %copy-start = (bf16[256,2048]{1,0:T(8,128)(2,1)S(1)}, bf16[256,2048]{1,0:T(8,128)(2,1)}, u32[]{:S(2)}) copy-start(bf16[256,2048]{1,0:T(8,128)(2,1)} %edge.1) | copy-start | bytes 3145732
  2.6 0.8 %copy-start.2 = (f32[3,2048]{1,0:T(4,128)S(1)}, f32[3,2048]{1,0:T(4,128)}, u32[]{:S(2)}) copy-start(f32[3,2048]{1,0:T(4,128)} %vector.5) | copy-start | bytes 73732
  3.3 0.9 %copy-start.4 = (bf16[256,256]{1,0:T(8,128)(2,1)S(1)}, bf16[256,256]{1,0:T(8,128)(2,1)}, u32[]{:S(2)}) copy-start(bf16[256,256]{1,0:T(8,128)(2,1)} %node.1) | copy-start | bytes 393220
  4.2 0.8 %copy-start.8 = (bf16[256,64]{0,1:T(8,128)(2,1)S(1)}, bf16[256,64]{0,1:T(8,128)(2,1)}, u32[]{:S(2)}) copy-start(bf16[256,64]{0,1:T(8,128)(2,1)} %param.20) | copy-start | bytes 98308
  5.0 0.8 %copy-start.9 = (bf16[256,64]{0,1:T(8,128)(2,1)S(1)}, bf16[256,64]{0,1:T(8,128)(2,1)}, u32[]{:S(2)}) copy-start(bf16[256,64]{0,1:T(8,128)(2,1)} %param.21) | copy-start | bytes 98308
  5.7 0.8 %copy-start.10 = (bf16[256,64]{0,1:T(8,128)(2,1)S(1)}, bf16[256,64]{0,1:T(8,128)(2,1)}, u32[]{:S(2)}) copy-start(bf16[256,64]{0,1:T(8,128)(2,1)} %param.22) | copy-start | bytes 98308
  6.5 0.7 %copy-start.11 = (s32[4,4,256]{2,1,0:T(4,128)S(1)}, s32[4,4,256]{2,1,0:T(4,128)}, u32[]{:S(2)}) copy-start(s32[4,4,256]{2,1,0:T(4,128)} %edge_send.1) | copy-start | bytes 49156
  7.2 0.7 %copy-start.13 = (s32[4,4,64]{2,1,0:T(4,128)S(1)}, s32[4,4,64]{2,1,0:T(4,128)}, u32[]{:S(2)}) copy-start(s32[4,4,64]{2,1,0:T(4,128)} %node_send.1) | copy-start | bytes 12292
  7.9 0.7 %copy-start.14 = (s32[2048]{0:T(1024)S(1)}, s32[2048]{0:T(1024)}, u32[]{:S(2)}) copy-start(s32[2048]{0:T(1024)} %param.29) | copy-start | bytes 24580
  8.6 4.4 %copy-start.3 = (f32[3,2048]{1,0:T(4,128)S(1)}, f32[3,2048]{1,0:T(4,128)}, u32[]{:S(2)}) copy-start(f32[3,2048]{1,0:T(4,128)} %vector.5) | copy-start | bytes 73732
  8.6 4.4 %copy-start.12 = (bf16[128,64]{0,1:T(8,128)(2,1)S(1)}, bf16[128,64]{0,1:T(8,128)(2,1)}, u32[]{:S(2)}) copy-start(bf16[128,64]{0,1:T(8,128)(2,1)} %param.23) | copy-start | bytes 49156
  9.8 3.9 %collective-permute-start = (bf16[144,256]{1,0:T(8,128)(2,1)S(1)}, bf16[144,256]{1,0:T(8,128)(2,1)S(1)}, u32[]{:S(2)}, u32[]{:S(2)}) collective-permute-start(bf16[144,256]{1,0:T(8,128)(2,1)S(1)} %get-tuple-element.23), channel_id=1, source_target_pairs={{0,4},{4,0},{8,12},{12,8},{1,5},{5,1},{9,13},{13,9},{2,6},{6,2},{1... | collective-permute-start | bytes 221192 | tf_op jit(solution)/shard_map/ppermute | solution.py:337
  10.3 5.5 %collective-permute-start.1 = (bf16[144,256]{1,0:T(8,128)(2,1)S(1)}, bf16[144,256]{1,0:T(8,128)(2,1)S(1)}, u32[]{:S(2)}, u32[]{:S(2)}) collective-permute-start(bf16[144,256]{1,0:T(8,128)(2,1)S(1)} %get-tuple-element.24), channel_id=1, source_target_pairs={{0,8},{4,12},{8,0},{12,4},{1,9},{5,13},{9,1},{13,5},{2,10},{6,14},... | collective-permute-start | bytes 221192 | tf_op jit(solution)/shard_map/ppermute | solution.py:337
  12.9 4.2 %collective-permute-start.2 = (bf16[144,256]{1,0:T(8,128)(2,1)S(1)}, bf16[144,256]{1,0:T(8,128)(2,1)S(1)}, u32[]{:S(2)}, u32[]{:S(2)}) collective-permute-start(bf16[144,256]{1,0:T(8,128)(2,1)S(1)} %get-tuple-element.25), channel_id=1, source_target_pairs={{0,12},{4,8},{8,4},{12,0},{1,13},{5,9},{9,5},{13,1},{2,14},{6,10},... | collective-permute-start | bytes 221192 | tf_op jit(solution)/shard_map/ppermute | solution.py:337
  13.0 4.2 %copy-start.1 = (bf16[16,8192]{1,0:T(8,128)(2,1)S(1)}, bf16[16,8192]{1,0:T(8,128)(2,1)}, u32[]{:S(2)}) copy-start(bf16[16,8192]{1,0:T(8,128)(2,1)} %basis.1) | copy-start | bytes 786436
  13.0 4.2 %copy-start.5 = (s32[8192]{0:T(1024)S(1)}, s32[8192]{0:T(1024)}, u32[]{:S(2)}) copy-start(s32[8192]{0:T(1024)} %param.30) | copy-start | bytes 98308
  13.0 4.2 %copy-start.6 = (s32[8192]{0:T(1024)S(1)}, s32[8192]{0:T(1024)}, u32[]{:S(2)}) copy-start(s32[8192]{0:T(1024)} %param.31) | copy-start | bytes 98308
  17.1 0.7 %copy-start.15 = (bf16[16,64]{1,0:T(8,128)(2,1)S(1)}, bf16[16,64]{1,0:T(8,128)(2,1)}, u32[]{:S(2)}) copy-start(bf16[16,64]{1,0:T(8,128)(2,1)} %w_angle.1) | copy-start | bytes 6148
  17.1 0.7 %copy-start.16 = (f32[64]{0:T(128)S(1)}, f32[64]{0:T(128)}, u32[]{:S(2)}) copy-start(f32[64]{0:T(128)} %param.25) | copy-start | bytes 772
  30.9 5.8 %collective-permute-start.5 = (f32[4,8,256]{2,1,0:T(8,128)S(1)}, f32[4,8,256]{2,1,0:T(8,128)S(1)}, u32[]{:S(2)}, u32[]{:S(2)}) collective-permute-start(f32[4,8,256]{2,1,0:T(8,128)S(1)} %get-tuple-element.28), channel_id=1, source_target_pairs={{0,3},{1,2},{2,1},{3,0},{4,7},{5,6},{6,5},{7,4},{8,11},{9,10},{10,... | collective-permute-start | bytes 98312 | tf_op jit(solution)/shard_map/ppermute | solution.py:337
  34.7 4.8 %collective-permute-start.4 = (f32[4,8,256]{2,1,0:T(8,128)S(1)}, f32[4,8,256]{2,1,0:T(8,128)S(1)}, u32[]{:S(2)}, u32[]{:S(2)}) collective-permute-start(f32[4,8,256]{2,1,0:T(8,128)S(1)} %get-tuple-element.28), channel_id=1, source_target_pairs={{0,2},{1,3},{2,0},{3,1},{4,6},{5,7},{6,4},{7,5},{8,10},{9,11},{10,... | collective-permute-start | bytes 98312 | tf_op jit(solution)/shard_map/ppermute | solution.py:337
  34.7 4.8 %collective-permute-start.3 = (f32[4,8,256]{2,1,0:T(8,128)S(1)}, f32[4,8,256]{2,1,0:T(8,128)S(1)}, u32[]{:S(2)}, u32[]{:S(2)}) collective-permute-start(f32[4,8,256]{2,1,0:T(8,128)S(1)} %get-tuple-element.28), channel_id=1, source_target_pairs={{0,1},{1,0},{2,3},{3,2},{4,5},{5,4},{6,7},{7,6},{8,9},{9,8},{10,11... | collective-permute-start | bytes 98312 | tf_op jit(solution)/shard_map/ppermute | solution.py:337
  39.6 2.2 %collective-permute-start.6 = (f32[8,256]{1,0:T(8,128)S(1)}, f32[8,256]{1,0:T(8,128)S(1)}, u32[]{:S(2)}, u32[]{:S(2)}) collective-permute-start(f32[8,256]{1,0:T(8,128)S(1)} %get-tuple-element.29), channel_id=1, source_target_pairs={{0,4},{4,0},{8,12},{12,8},{1,5},{5,1},{9,13},{13,9},{2,6},{6,2},{1... | collective-permute-start | bytes 24584 | tf_op jit(solution)/shard_map/ppermute | solution.py:337
  39.7 3.1 %collective-permute-start.8 = (f32[8,256]{1,0:T(8,128)S(1)}, f32[8,256]{1,0:T(8,128)S(1)}, u32[]{:S(2)}, u32[]{:S(2)}) collective-permute-start(f32[8,256]{1,0:T(8,128)S(1)} %get-tuple-element.30), channel_id=1, source_target_pairs={{0,12},{4,8},{8,4},{12,0},{1,13},{5,9},{9,5},{13,1},{2,14},{6,10},... | collective-permute-start | bytes 24584 | tf_op jit(solution)/shard_map/ppermute | solution.py:337
  41.1 3.7 %collective-permute-start.7 = (f32[8,256]{1,0:T(8,128)S(1)}, f32[8,256]{1,0:T(8,128)S(1)}, u32[]{:S(2)}, u32[]{:S(2)}) collective-permute-start(f32[8,256]{1,0:T(8,128)S(1)} %get-tuple-element.31), channel_id=1, source_target_pairs={{0,8},{4,12},{8,0},{12,4},{1,9},{5,13},{9,1},{13,5},{2,10},{6,14},... | collective-permute-start | bytes 24584 | tf_op jit(solution)/shard_map/ppermute | solution.py:337

commit v3 on v2

--- a/solution.py
+++ b/solution.py
@@ -16,7 +16,7 @@
 TERM = 8
 BF = jnp.bfloat16
 F32 = jnp.float32
-VMEM_LIMIT = 40 * 1024 * 1024
+VMEM_LIMIT = 24 * 1024 * 1024
 
 
 def sigmoid(values):
@@ -70,51 +70,54 @@
     return dot_nn(weight, values.astype(BF)), dot_nn(weight, slopes.astype(BF)), lengths
 
 
+def fetch(sources, places, sems):
+    copies = [pltpu.make_async_copy(a, b, sems.at[i]) for i, (a, b) in enumerate(zip(sources, places))]
+    for copy in copies:
+        copy.start()
+    return copies
+
+
 def squared_length(vector):
     return vector[0:1] * vector[0:1] + vector[1:2] * vector[1:2] + vector[2:3] * vector[2:3]
 
 
-def prep_kernel(
-    node,
-    edge,
-    vector,
-    w_source,
-    w_target,
-    w_edge,
-    node_send,
-    edge_send,
-    target,
-    source,
-    part_out,
-    misc_out,
-    own_node_out,
-    own_edge_out,
-    *sends,
-):
+def prep_kernel(peers, *refs):
+    sources = refs[:10]
+    part_out, misc_out, target_hot, own_node_out, own_edge_out = refs[10:15]
+    sends = refs[15 : 15 + peers]
+    places = refs[15 + peers : -1]
+    sems = refs[-1]
+    edge_source, edge = sources[9], places[9]
+    edges = edge.shape[1]
+    high_count = 4
+    low_count = edges // high_count
+    pieces = [slice(h * low_count, (h + 1) * low_count) for h in range(high_count)]
+    copies = fetch(
+        list(sources[:9]) + [edge_source.at[:, cols] for cols in pieces],
+        list(places[:9]) + [edge.at[:, cols] for cols in pieces],
+        sems,
+    )
+    node, w_source, w_target, w_edge, vector, node_send, edge_send, target, source = places[:9]
     me = lax.axis_index("graph")
-    peers = len(sends)
     channels = w_source.shape[0]
     first_chan = pl.multiple_of(lax.axis_index("chan") * channels, channels)
-    edges = edge.shape[1]
     cap = node_send.shape[2]
-    high_count = 4
-    low_count = edges // high_count
+    for copy in copies[:9]:
+        copy.wait()
+    own_node_out[...] = node[pl.ds(first_chan, channels), :]
     atoms = node[...]
-    own_node_out[...] = node[pl.ds(first_chan, channels), :]
-    own_edge_out[...] = edge[pl.ds(first_chan, channels), :]
     proj_src = dot_nn(w_source[...], atoms).astype(BF)
     dst_high, dst_low = halves(dot_nn(w_target[...], atoms))
     dst_table = jnp.concatenate([dst_high, dst_low], axis=0)
     own_nodes = jnp.concatenate([node_send[q, pl.ds(me, 1), :] for q in range(peers)], axis=0)
     own_nodes = own_nodes.astype(F32).astype(BF)
     parts = []
-    for h in range(high_count):
-        cols = slice(h * low_count, (h + 1) * low_count)
+    for h, cols in enumerate(pieces):
         dst = target[:, cols]
         src = source[:, cols]
-        rows = dot_nn(dst_table, one_hot(dst, atoms.shape[1]))
-        part = rows[:channels] + rows[channels:] + dot_nn(w_edge[...], edge[:, cols])
-        part_out[:, cols] = part
+        hot = one_hot(dst, atoms.shape[1])
+        target_hot[:, cols] = hot
+        rows = dot_nn(dst_table, hot)
         src_peer = src // cap
         by_peer = dot_nn(own_nodes, one_hot(src - src_peer * cap, cap))
         src_node = choose(by_peer, src_peer, peers)
@@ -135,6 +138,10 @@
             axis=0,
         )
         misc_out[:, cols] = misc
+        copies[9 + h].wait()
+        part = rows[:channels] + rows[channels:] + dot_nn(w_edge[...], edge[:, cols])
+        part_out[:, cols] = part
+        own_edge_out[:, cols] = edge[pl.ds(first_chan, channels), cols]
         parts.append(jnp.concatenate([part.astype(BF), misc.astype(BF)], axis=0))
     table = jnp.concatenate(parts, axis=0)
     for d in range(peers):
@@ -145,14 +152,39 @@
         sends[d][channels:] = picked.astype(BF)
 
 
-def local_kernel(vector, w_radial, radial_out, rate_out):
+def local_kernel(ecap, misc, *refs):
+    sources = refs[:7]
+    radial, rate, unit, angular, place_in, place_out, source_hot, radial_weight, energy_column = refs[7:16]
+    places = refs[16:23]
+    sems = refs[23]
+    copies = fetch(sources, places, sems)
+    vector, w_radial, w_angle, w_energy, trip_in, trip_out, basis = places
+    me = lax.axis_index("graph")
     edges = vector.shape[1]
-    width = min(512, edges)
+    trips = basis.shape[1]
+    channels = w_radial.shape[0]
+    width = 512
     for start in range(0, edges, width):
         cols = slice(start, start + width)
-        radial, rate, _ = radial_terms(squared_length(vector[:, cols]), w_radial[...])
-        radial_out[:, cols] = radial
-        rate_out[:, cols] = rate
+        source_hot[:, cols] = one_hot(misc[10:11, cols].astype(jnp.int32), source_hot.shape[0])
+    for copy in copies:
+        copy.wait()
+    radial_weight[...] = w_radial[...]
+    lines = lax.broadcasted_iota(jnp.int32, (channels, channels), 0)
+    diagonal = lines == lax.broadcasted_iota(jnp.int32, (channels, channels), 1)
+    energy_column[...] = jnp.sum(jnp.where(diagonal, w_energy[...], 0.0), axis=1, keepdims=True)
+    for start in range(0, edges, width):
+        cols = slice(start, start + width)
+        vec = vector[:, cols]
+        rows, slopes, lengths = radial_terms(squared_length(vec), w_radial[...])
+        radial[:, cols] = rows
+        rate[:, cols] = slopes
+        unit[:, cols] = vec / lengths
+    for start in range(0, trips, width):
+        cols = slice(start, start + width)
+        angular[:, cols] = dot_tn(w_angle[...], basis[:, cols])
+        place_in[:, cols] = jnp.bitwise_xor(trip_in[:, cols], me * ecap)
+        place_out[:, cols] = trip_out[:, cols]
 
 
 def main_kernel(
@@ -161,27 +193,27 @@
     scale,
     part,
     misc,
+    target_hot,
+    node,
+    edge,
     radial,
     rate,
-    vector,
-    node,
-    edge,
-    basis,
+    unit,
+    angular,
+    place_in,
+    place_out,
+    source_hot,
     w_radial,
-    w_angle,
     w_energy,
-    trip_in,
-    trip_out,
-    target,
     *refs,
 ):
     received = refs[:peers]
     node_out, edge_out, force_out = refs[peers : peers + 3]
-    message, own_rate, slot_rate, slot_table, angular, gather_sum, grad_table, edge_grad, slot_sum, moves = refs[peers + 3 :]
+    message, own_rate, slot_rate, slot_table, gather_sum, grad_table, edge_grad, slot_sum, moves = refs[peers + 3 :]
     me = lax.axis_index("graph")
     channels, edges = part.shape
     nodes = node.shape[1]
-    trips = basis.shape[1]
+    trips = angular.shape[1]
     groups = slot_table.shape[0] // channels
     low_in = slot_table.shape[1]
     low_out = edges // groups
@@ -191,14 +223,12 @@
 
     src_table = jnp.concatenate([received[d][:channels] for d in range(peers)], axis=0)
 
-    def src_rows(src_node, src_peer):
-        rows = dot_nn(src_table, one_hot(src_node, nodes))
-        return choose(rows, jnp.bitwise_xor(src_peer, me), peers)
+    def src_rows(hot, src_peer):
+        return choose(dot_nn(src_table, hot), jnp.bitwise_xor(src_peer, me), peers)
 
     for start in range(0, edges, step):
         cols = slice(start, start + step)
-        rows = src_rows(misc[10:11, cols].astype(jnp.int32), misc[11:12, cols].astype(jnp.int32))
-        preact = rows + part[:, cols]
+        preact = src_rows(source_hot[:, cols], misc[11:12, cols].astype(jnp.int32)) + part[:, cols]
         active = preact * sigmoid(preact)
         message[:, cols] = (active * radial[:, cols]).astype(BF)
         own_rate[:, cols] = active * rate[:, cols]
@@ -211,7 +241,7 @@
         src_node = rest[10:11].astype(jnp.int32)
         src_peer = rest[11:12].astype(jnp.int32)
         slot_radial, slot_slope, lengths = radial_terms(squared_length(vec), w_radial[...])
-        preact = src_rows(src_node, src_peer) + extra[:channels]
+        preact = src_rows(one_hot(src_node, nodes), src_peer) + extra[:channels]
         active = preact * sigmoid(preact)
         place = d * ecap
         low = place % low_in
@@ -221,29 +251,20 @@
         slot_rate[:, cols] = active * slot_slope
         slots.append((vec / lengths, src_node, src_peer, rest[9:10].astype(jnp.int32)))
 
-    def split_in(cols):
-        place = jnp.bitwise_xor(trip_in[:, cols], me * ecap)
-        high = place // low_in
-        return high, one_hot(place - high * low_in, low_in)
-
-    def split_out(cols):
-        place = trip_out[:, cols]
-        high = place // low_out
-        return high, one_hot(place - high * low_out, low_out)
+    def split(place, low_count):
+        high = place // low_count
+        return high, one_hot(place - high * low_count, low_count)
 
     gather_sum[...] = jnp.zeros_like(gather_sum)
-    weight = w_angle[...]
 
     def forward(turn, carry):
         total = None
         for sub in range(turn_width // width):
             cols = pl.ds(pl.multiple_of(turn * turn_width + sub * width, width), width)
-            high_in, hot_in = split_in(cols)
-            high_out, hot_out = split_out(cols)
-            angle = dot_tn(weight, basis[:, cols])
-            angular[:, cols] = angle
-            term = (choose(dot_nn(slot_table[...], hot_in), high_in, groups) * angle).astype(BF)
-            more = dot_nt(hot_out, expand(term, high_out, groups))
+            high_in, hot_in = split(place_in[:, cols], low_in)
+            high_out, hot_out = split(place_out[:, cols], low_out)
+            rows = choose(dot_nn(slot_table[...], hot_in), high_in, groups)
+            more = dot_nt(hot_out, expand((rows * angular[:, cols]).astype(BF), high_out, groups))
             total = more if total is None else total + more
         gather_sum[...] += total
         return carry
@@ -255,26 +276,21 @@
     for g in range(groups):
         cols = slice(g * low_out, (g + 1) * low_out)
         value = gathered[g * channels : (g + 1) * channels]
-        own_edge = edge[:, cols].astype(F32)
-        fresh = own_edge + message[:, cols].astype(F32) + value * sigmoid(value)
+        fresh = edge[:, cols].astype(F32) + message[:, cols].astype(F32) + value * sigmoid(value)
         edge_out[:, cols] = fresh.astype(BF)
         high, low = halves(fresh)
-        sums = dot_nt(jnp.concatenate([high, low], axis=0), one_hot(target[:, cols], nodes))
+        sums = dot_nt(jnp.concatenate([high, low], axis=0), target_hot[:, cols])
         atom_sum += sums[:channels] + sums[channels:]
-    lines = lax.broadcasted_iota(jnp.int32, (channels, channels), 0)
-    diagonal = lines == lax.broadcasted_iota(jnp.int32, (channels, channels), 1)
-    energy = jnp.sum(jnp.where(diagonal, w_energy[...], 0.0), axis=1, keepdims=True)
     node_new = node[...].astype(F32) + scale * atom_sum
     node_out[...] = node_new.astype(BF)
     sig = sigmoid(node_new)
-    grad_node = energy * (sig * (1.0 + node_new * (1.0 - sig))) * scale
+    grad_node = w_energy[...] * (sig * (1.0 + node_new * (1.0 - sig))) * scale
     high, low = halves(grad_node)
     grad_pair = jnp.concatenate([high, low], axis=0)
-    pushes = []
     for g in range(groups):
         cols = slice(g * low_out, (g + 1) * low_out)
         value = gathered[g * channels : (g + 1) * channels]
-        rows = dot_nn(grad_pair, one_hot(target[:, cols], nodes))
+        rows = dot_nn(grad_pair, target_hot[:, cols])
         grad_edge = rows[:channels] + rows[channels:]
         sig = sigmoid(value)
         grad_table[g * channels : (g + 1) * channels, :] = (
@@ -288,10 +304,10 @@
         total = None
         for sub in range(turn_width // width):
             cols = pl.ds(pl.multiple_of(turn * turn_width + sub * width, width), width)
-            high_in, hot_in = split_in(cols)
-            high_out, hot_out = split_out(cols)
-            term = (choose(dot_nn(grad_table[...], hot_out), high_out, groups) * angular[:, cols]).astype(BF)
-            more = dot_nt(hot_in, expand(term, high_in, groups))
+            high_in, hot_in = split(place_in[:, cols], low_in)
+            high_out, hot_out = split(place_out[:, cols], low_out)
+            rows = choose(dot_nn(grad_table[...], hot_out), high_out, groups)
+            more = dot_nt(hot_in, expand((rows * angular[:, cols]).astype(BF), high_in, groups))
             total = more if total is None else total + more
         slot_sum[...] += total
         return carry
@@ -306,14 +322,11 @@
 
     for start in range(0, edges, step):
         cols = slice(start, start + step)
-        vec = vector[:, cols]
-        terms = push_terms(vec * (edge_grad[:, cols] / jnp.sqrt(1.0 + squared_length(vec))))
+        terms = push_terms(unit[:, cols] * edge_grad[:, cols])
         src_peer = jnp.bitwise_xor(misc[11:12, cols].astype(jnp.int32), me)
-        moves[...] += dot_nt(
-            expand(terms, src_peer, peers).astype(BF), one_hot(misc[10:11, cols].astype(jnp.int32), nodes)
-        )
+        moves[...] += dot_nt(expand(terms, src_peer, peers).astype(BF), source_hot[:, cols])
         moves[:TERM] -= dot_nt(
-            jnp.concatenate([terms, jnp.zeros_like(terms)], axis=0).astype(BF), one_hot(target[:, cols], nodes)
+            jnp.concatenate([terms, jnp.zeros_like(terms)], axis=0).astype(BF), target_hot[:, cols]
         )[:TERM]
     slot_grad = slot_sum[...].T
     for d in range(peers):
@@ -321,8 +334,8 @@
         place = d * ecap
         low = place % low_in
         grads = slot_grad[(place // low_in) * channels : (place // low_in + 1) * channels, low : low + ecap]
-        unit, src_node, src_peer, dst_node = slots[d]
-        terms = push_terms(unit * jnp.sum(grads * slot_rate[:, cols], axis=0, keepdims=True))
+        slot_unit, src_node, src_peer, dst_node = slots[d]
+        terms = push_terms(slot_unit * jnp.sum(grads * slot_rate[:, cols], axis=0, keepdims=True))
         moves[...] += dot_nt(
             expand(terms, jnp.bitwise_xor(src_peer, me), peers).astype(BF), one_hot(src_node, nodes)
         )
@@ -374,43 +387,89 @@
     groups = 256 // channels
     low_in = peers * ecap // groups
     low_out = edges // groups
-    target = edge_target.reshape(1, edges)
-    source = edge_source.reshape(1, edges)
+    shape = pltpu.VMEM
     params = pltpu.CompilerParams(vmem_limit_bytes=VMEM_LIMIT)
-    part, misc, own_node, own_edge, *sends = pl.pallas_call(
-        prep_kernel,
+
+    def far(count):
+        return [pl.BlockSpec(memory_space=pltpu.HBM)] * count
+
+    def near(count):
+        return [pl.BlockSpec(memory_space=pltpu.VMEM)] * count
+
+    def buffers(arrays):
+        return [pltpu.VMEM(a.shape, a.dtype) for a in arrays]
+
+    inputs = [
+        node_embed,
+        w_source.T,
+        w_target.T,
+        w_edge.T,
+        edge_vector,
+        node_send,
+        edge_send,
+        edge_target.reshape(1, edges),
+        edge_source.reshape(1, edges),
+        edge_embed,
+    ]
+    part, misc, target_hot, own_node, own_edge, *sends = pl.pallas_call(
+        functools.partial(prep_kernel, peers),
         name="prep",
+        in_specs=far(len(inputs)),
+        out_specs=near(5 + peers),
         out_shape=[
-            jax.ShapeDtypeStruct((channels, edges), F32),
-            jax.ShapeDtypeStruct((MISC, edges), F32),
-            jax.ShapeDtypeStruct((channels, nodes), BF),
-            jax.ShapeDtypeStruct((channels, edges), BF),
+            shape((channels, edges), F32),
+            shape((MISC, edges), F32),
+            shape((nodes, edges), BF),
+            shape((channels, nodes), BF),
+            shape((channels, edges), BF),
         ]
-        + [jax.ShapeDtypeStruct((2 * channels + MISC, ecap), BF)] * peers,
+        + [shape((2 * channels + MISC, ecap), BF)] * peers,
+        scratch_shapes=buffers(inputs) + [pltpu.SemaphoreType.DMA((13,))],
         compiler_params=params,
-    )(node_embed, edge_embed, edge_vector, w_source.T, w_target.T, w_edge.T, node_send, edge_send, target, source)
+    )(*[pltpu.with_memory_space_constraint(a, pltpu.HBM) for a in inputs])
     received = [sends[0]] + [exchange(sends[d], "graph", d) for d in range(1, peers)]
-    radial, rate = pl.pallas_call(
-        local_kernel,
+    inputs = [
+        edge_vector,
+        w_radial.T,
+        w_angle,
+        w_energy.reshape(1, channels),
+        triplet_in.reshape(1, trips),
+        triplet_out.reshape(1, trips),
+        triplet_basis,
+    ]
+    local = pl.pallas_call(
+        functools.partial(local_kernel, ecap),
         name="local",
-        out_shape=[jax.ShapeDtypeStruct((channels, edges), F32)] * 2,
+        in_specs=near(1) + far(len(inputs)),
+        out_specs=near(9),
+        out_shape=[
+            shape((channels, edges), F32),
+            shape((channels, edges), F32),
+            shape((3, edges), F32),
+            shape((channels, trips), F32),
+            shape((1, trips), jnp.int32),
+            shape((1, trips), jnp.int32),
+            shape((nodes, edges), BF),
+            shape((channels, w_radial.shape[0]), BF),
+            shape((channels, 1), F32),
+        ],
+        scratch_shapes=buffers(inputs) + [pltpu.SemaphoreType.DMA((7,))],
         compiler_params=params,
-        cost_estimate=pl.CostEstimate(flops=2**28, bytes_accessed=2**21, transcendentals=2**18),
-    )(edge_vector, w_radial.T)
+        cost_estimate=pl.CostEstimate(flops=2**30, bytes_accessed=2**23, transcendentals=2**18),
+    )(misc, *[pltpu.with_memory_space_constraint(a, pltpu.HBM) for a in inputs])
     node_out, edge_out, force = pl.pallas_call(
         functools.partial(main_kernel, peers, ecap, math.sqrt(NODE_DEV / EDGE_DEV)),
         name="main",
         out_shape=[
             jax.ShapeDtypeStruct((channels, nodes), BF),
             jax.ShapeDtypeStruct((channels, edges), BF),
-            jax.ShapeDtypeStruct((peers, TERM, nodes), F32),
+            shape((peers, TERM, nodes), F32),
         ],
         scratch_shapes=[
             pltpu.VMEM((channels, edges), BF),
             pltpu.VMEM((channels, edges), F32),
             pltpu.VMEM((channels, peers * ecap), F32),
             pltpu.VMEM((groups * channels, low_in), BF),
-            pltpu.VMEM((channels, trips), F32),
             pltpu.VMEM((low_out, groups * channels), F32),
             pltpu.VMEM((groups * channels, low_out), BF),
             pltpu.VMEM((1, edges), F32),
@@ -418,23 +477,7 @@
             pltpu.VMEM((peers * TERM, nodes), F32),
         ],
         compiler_params=params,
-    )(
-        part,
-        misc,
-        radial,
-        rate,
-        edge_vector,
-        own_node,
-        own_edge,
-        triplet_basis,
-        w_radial.T,
-        w_angle,
-        w_energy.reshape(1, channels),
-        triplet_in.reshape(1, trips),
-        triplet_out.reshape(1, trips),
-        target,
-        *received,
-    )
+    )(part, misc, target_hot, own_node, own_edge, *local, *received)
     force = add_over(force, "chan")
     mine = force[0]
     for d in range(1, peers):

time: 46 us -> 38.4 us (0.83); the launches traced: 45.3 us -> 38.3 us
  local copies, waits for them, and re-layouts: 8.65 us -> 0.01 us
  Pallas kernels: 14.9 us -> 18 us
  waiting for transfers between devices: 10.6 us -> 9.21 us
    unnamed x34 -> x0, local copies, waits for them, and re-layouts: 8.65 us -> none
    pallas_call x2, Pallas kernels: 1.81 us -> 4.97 us  [the longest x1 2.9 us: shards(): pl.pallas_call(functools.partial(prep_kernel, peers), name='prep', in_spe...]
    ppermute x9, waiting for transfers between devices: 10.6 us -> 9.21 us  [exchange(): return lax.ppermute(values, axis, [(i, i ^ distance) for i in range(count)])]
  transfers between devices with their start and end apart: 9 -> 9, of which waited for: 6 -> 6; matrix products, arithmetic and copies ran while one was open for 0% -> 0% of each run, Pallas kernels for 1% -> 5%
where the time goes in v3:
time: 38.4 us; the launch traced here: 38.3 us
  Pallas kernels  18 us (47%)
  starting transfers between devices  9.81 us (26%)
  waiting for transfers between devices  9.21 us (24%)
  between operations  0.68 us (2%)
  other arithmetic  0.62 us (2%)
    pallas_call x1, Pallas kernels, shards(): pl.pallas_call(functools.partial(main_kernel, peers, ecap, math.sqrt(NODE...  13 us
    ppermute x9, starting transfers between devices, exchange(): return lax.ppermute(values, axis, [(i, i ^ distance) for i in range(count)])  9.81 us
    ppermute x9, waiting for transfers between devices, exchange(): return lax.ppermute(values, axis, [(i, i ^ distance) for i in range(count)])  9.21 us
    pallas_call x1, Pallas kernels, shards(): pl.pallas_call(functools.partial(prep_kernel, peers), name='prep', in_spe...  2.9 us
    pallas_call x1, Pallas kernels, shards(): pl.pallas_call(functools.partial(local_kernel, ecap), name='local', in_sp...  2.06 us
  transfers between devices with their start and end apart: 9, of which 6 were waited for; matrix products, arithmetic and copies ran while one was open for 0% of the time, Pallas kernels for 5%

profile of v3, /device:TPU:0, one launch (start us, length us, event | category | flops | bytes accessed | tf_op | source)
XLA Modules:
  0.0 38.3 jit_solution(4180344362828766736)
XLA Ops:
  0.6 2.9 %prep.1 = (f32[64,2048]{1,0:T(8,128)S(1)}, f32[16,2048]{1,0:T(8,128)S(1)}, bf16[256,2048]{1,0:T(8,128)(2,1)S(1)}, bf16[64,256]{1,0:T(8,128)(2,1)S(1)}, bf16[64,2...) custom-call(bf16[256,256]{1,0:T(8,128)(2,1)} %refs_0_.2, ...), custom_call_target="tpu_custom_call" | custom-call | tf_op jit(solution)/shard_map/prep/pallas_call | solution.py:414
  3.5 0.5 %collective-permute-start = (bf16[144,256]{1,0:T(8,128)(2,1)S(1)}, bf16[144,256]{1,0:T(8,128)(2,1)S(1)}, u32[]{:S(2)}, u32[]{:S(2)}) collective-permute-start(bf16[144,256]{1,0:T(8,128)(2,1)S(1)} %get-tuple-element.39), channel_id=1, source_target_pairs={{0,4},{4,0},{8,12},{12,8},{1,5},{5,1},{9,13},{13,9},{2,6},{6,2},{1... | collective-permute-start | bytes 221192 | tf_op jit(solution)/shard_map/ppermute | solution.py:350
  4.1 2.6 %collective-permute-start.1 = (bf16[144,256]{1,0:T(8,128)(2,1)S(1)}, bf16[144,256]{1,0:T(8,128)(2,1)S(1)}, u32[]{:S(2)}, u32[]{:S(2)}) collective-permute-start(bf16[144,256]{1,0:T(8,128)(2,1)S(1)} %get-tuple-element.40), channel_id=1, source_target_pairs={{0,8},{4,12},{8,0},{12,4},{1,9},{5,13},{9,1},{13,5},{2,10},{6,14},... | collective-permute-start | bytes 221192 | tf_op jit(solution)/shard_map/ppermute | solution.py:350
  6.7 0.1 collective-permute-start.2
  6.7 2.1 %local.1 = (f32[64,2048]{1,0:T(8,128)S(1)}, f32[64,2048]{1,0:T(8,128)S(1)}, f32[3,2048]{1,0:T(4,128)S(1)}, f32[64,8192]{1,0:T(8,128)S(1)}, s32[1,8192]{1,0:T(1,1...) custom-call(f32[16,2048]{1,0:T(8,128)S(1)} %get-tuple-element.25.mis, ...), custom_call_target="tpu_custom_call" | custom-call | flops 1073741824 | bytes 8388608 | tf_op jit(solution)/shard_map/local/pallas_call | solution.py:440
  8.8 0.0 collective-permute-done.refs_1_
  8.8 0.7 %collective-permute-done.1.refs_2_ = bf16[144,256]{1,0:T(8,128)(2,1)S(1)} collective-permute-done((bf16[144,256]{1,0:T(8,128)(2,1)S(1)}, bf16[144,256]{1,0:T(8,128)(2,1)S(1)}, u32[]{:S(2)}, u32[]{:S(2)}) %collective-permute-start.1) | collective-permute-done | bytes 73760 | tf_op jit(solution)/shard_map/ppermute | solution.py:350
  9.5 1.4 %collective-permute-done.2.refs_3_ = bf16[144,256]{1,0:T(8,128)(2,1)S(1)} collective-permute-done((bf16[144,256]{1,0:T(8,128)(2,1)S(1)}, bf16[144,256]{1,0:T(8,128)(2,1)S(1)}, u32[]{:S(2)}, u32[]{:S(2)}) %collective-permute-start.2) | collective-permute-done | bytes 73760 | tf_op jit(solution)/shard_map/ppermute | solution.py:350
  10.9 13.0 %main.1 = (bf16[64,256]{1,0:T(8,128)(2,1)}, bf16[64,2048]{1,0:T(8,128)(2,1)}, f32[4,8,256]{2,1,0:T(8,128)S(1)}) custom-call(f32[64,2048]{1,0:T(8,128)S(1)} %get-tuple-element.24.part, f32[16,2048]{1,0:T(8,128)S(1)} %get-tuple-element.25.misc, bf16[256,2048]{1,0:T(8,128)(2,1)S(1)} %get-tuple-element.26.target_hot, ...), custom_call_target="tpu_custom_call" | custom-call | tf_op jit(solution)/shard_map/main/pallas_call | solution.py:460
  23.9 3.8 %collective-permute-start.5 = (f32[4,8,256]{2,1,0:T(8,128)S(1)}, f32[4,8,256]{2,1,0:T(8,128)S(1)}, u32[]{:S(2)}, u32[]{:S(2)}) collective-permute-start(f32[4,8,256]{2,1,0:T(8,128)S(1)} %get-tuple-element.44), channel_id=1, source_target_pairs={{0,3},{1,2},{2,1},{3,0},{4,7},{5,6},{6,5},{7,4},{8,11},{9,10},{10,... | collective-permute-start | bytes 98312 | tf_op jit(solution)/shard_map/ppermute | solution.py:350
  27.7 0.0 collective-permute-start.4
  27.7 0.6 %collective-permute-start.3 = (f32[4,8,256]{2,1,0:T(8,128)S(1)}, f32[4,8,256]{2,1,0:T(8,128)S(1)}, u32[]{:S(2)}, u32[]{:S(2)}) collective-permute-start(f32[4,8,256]{2,1,0:T(8,128)S(1)} %get-tuple-element.44), channel_id=1, source_target_pairs={{0,1},{1,0},{2,3},{3,2},{4,5},{5,4},{6,7},{7,6},{8,9},{9,8},{10,11... | collective-permute-start | bytes 98312 | tf_op jit(solution)/shard_map/ppermute | solution.py:350
  28.3 1.4 %collective-permute-done.5 = f32[4,8,256]{2,1,0:T(8,128)S(1)} collective-permute-done((f32[4,8,256]{2,1,0:T(8,128)S(1)}, f32[4,8,256]{2,1,0:T(8,128)S(1)}, u32[]{:S(2)}, u32[]{:S(2)}) %collective-permute-start.5) | collective-permute-done | bytes 32800 | tf_op jit(solution)/shard_map/ppermute | solution.py:350
  29.7 2.9 %collective-permute-done.4 = f32[4,8,256]{2,1,0:T(8,128)S(1)} collective-permute-done((f32[4,8,256]{2,1,0:T(8,128)S(1)}, f32[4,8,256]{2,1,0:T(8,128)S(1)}, u32[]{:S(2)}, u32[]{:S(2)}) %collective-permute-start.4) | collective-permute-done | bytes 32800 | tf_op jit(solution)/shard_map/ppermute | solution.py:350
  32.5 0.0 collective-permute-done.3
  32.6 0.1 collective-permute-start.6
  32.6 1.4 %collective-permute-start.8 = (f32[8,256]{1,0:T(8,128)S(1)}, f32[8,256]{1,0:T(8,128)S(1)}, u32[]{:S(2)}, u32[]{:S(2)}) collective-permute-start(f32[8,256]{1,0:T(8,128)S(1)} %get-tuple-element.46), channel_id=1, source_target_pairs={{0,12},{4,8},{8,4},{12,0},{1,13},{5,9},{9,5},{13,1},{2,14},{6,10},... | collective-permute-start | bytes 24584 | tf_op jit(solution)/shard_map/ppermute | solution.py:350
  34.0 0.8 %collective-permute-start.7 = (f32[8,256]{1,0:T(8,128)S(1)}, f32[8,256]{1,0:T(8,128)S(1)}, u32[]{:S(2)}, u32[]{:S(2)}) collective-permute-start(f32[8,256]{1,0:T(8,128)S(1)} %get-tuple-element.47), channel_id=1, source_target_pairs={{0,8},{4,12},{8,0},{12,4},{1,9},{5,13},{9,1},{13,5},{2,10},{6,14},... | collective-permute-start | bytes 24584 | tf_op jit(solution)/shard_map/ppermute | solution.py:350
  34.8 0.0 collective-permute-done.6
  34.8 1.0 %collective-permute-done.8 = f32[8,256]{1,0:T(8,128)S(1)} collective-permute-done((f32[8,256]{1,0:T(8,128)S(1)}, f32[8,256]{1,0:T(8,128)S(1)}, u32[]{:S(2)}, u32[]{:S(2)}) %collective-permute-start.8) | collective-permute-done | bytes 8224 | tf_op jit(solution)/shard_map/ppermute | solution.py:350
  35.8 1.9 %collective-permute-done.7 = f32[8,256]{1,0:T(8,128)S(1)} collective-permute-done((f32[8,256]{1,0:T(8,128)S(1)}, f32[8,256]{1,0:T(8,128)S(1)}, u32[]{:S(2)}, u32[]{:S(2)}) %collective-permute-start.7) | collective-permute-done | bytes 8224 | tf_op jit(solution)/shard_map/ppermute | solution.py:350
  37.7 0.6 %slice_add_fusion = f32[3,256]{1,0:T(4,128)} fusion(f32[8,256]{1,0:T(8,128)S(1)} %fusion.2), kind=kLoop, calls=%fused_computation.8 | loop fusion | flops 768 | bytes 9216 | tf_op jit(solution)/shard_map/add | solution.py:485
  (3 shorter events, 0.0 us)
Async XLA Ops:
  3.5 5.3 %collective-permute-start = (bf16[144,256]{1,0:T(8,128)(2,1)S(1)}, bf16[144,256]{1,0:T(8,128)(2,1)S(1)}, u32[]{:S(2)}, u32[]{:S(2)}) collective-permute-start(bf16[144,256]{1,0:T(8,128)(2,1)S(1)} %get-tuple-element.39), channel_id=1, source_target_pairs={{0,4},{4,0},{8,12},{12,8},{1,5},{5,1},{9,13},{13,9},{2,6},{6,2},{1... | collective-permute-start | bytes 221192 | tf_op jit(solution)/shard_map/ppermute | solution.py:350
  4.1 5.4 %collective-permute-start.1 = (bf16[144,256]{1,0:T(8,128)(2,1)S(1)}, bf16[144,256]{1,0:T(8,128)(2,1)S(1)}, u32[]{:S(2)}, u32[]{:S(2)}) collective-permute-start(bf16[144,256]{1,0:T(8,128)(2,1)S(1)} %get-tuple-element.40), channel_id=1, source_target_pairs={{0,8},{4,12},{8,0},{12,4},{1,9},{5,13},{9,1},{13,5},{2,10},{6,14},... | collective-permute-start | bytes 221192 | tf_op jit(solution)/shard_map/ppermute | solution.py:350
  6.7 4.2 %collective-permute-start.2 = (bf16[144,256]{1,0:T(8,128)(2,1)S(1)}, bf16[144,256]{1,0:T(8,128)(2,1)S(1)}, u32[]{:S(2)}, u32[]{:S(2)}) collective-permute-start(bf16[144,256]{1,0:T(8,128)(2,1)S(1)} %get-tuple-element.41), channel_id=1, source_target_pairs={{0,12},{4,8},{8,4},{12,0},{1,13},{5,9},{9,5},{13,1},{2,14},{6,10},... | collective-permute-start | bytes 221192 | tf_op jit(solution)/shard_map/ppermute | solution.py:350
  23.9 5.8 %collective-permute-start.5 = (f32[4,8,256]{2,1,0:T(8,128)S(1)}, f32[4,8,256]{2,1,0:T(8,128)S(1)}, u32[]{:S(2)}, u32[]{:S(2)}) collective-permute-start(f32[4,8,256]{2,1,0:T(8,128)S(1)} %get-tuple-element.44), channel_id=1, source_target_pairs={{0,3},{1,2},{2,1},{3,0},{4,7},{5,6},{6,5},{7,4},{8,11},{9,10},{10,... | collective-permute-start | bytes 98312 | tf_op jit(solution)/shard_map/ppermute | solution.py:350
  27.7 4.8 %collective-permute-start.4 = (f32[4,8,256]{2,1,0:T(8,128)S(1)}, f32[4,8,256]{2,1,0:T(8,128)S(1)}, u32[]{:S(2)}, u32[]{:S(2)}) collective-permute-start(f32[4,8,256]{2,1,0:T(8,128)S(1)} %get-tuple-element.44), channel_id=1, source_target_pairs={{0,2},{1,3},{2,0},{3,1},{4,6},{5,7},{6,4},{7,5},{8,10},{9,11},{10,... | collective-permute-start | bytes 98312 | tf_op jit(solution)/shard_map/ppermute | solution.py:350
  27.7 4.8 %collective-permute-start.3 = (f32[4,8,256]{2,1,0:T(8,128)S(1)}, f32[4,8,256]{2,1,0:T(8,128)S(1)}, u32[]{:S(2)}, u32[]{:S(2)}) collective-permute-start(f32[4,8,256]{2,1,0:T(8,128)S(1)} %get-tuple-element.44), channel_id=1, source_target_pairs={{0,1},{1,0},{2,3},{3,2},{4,5},{5,4},{6,7},{7,6},{8,9},{9,8},{10,11... | collective-permute-start | bytes 98312 | tf_op jit(solution)/shard_map/ppermute | solution.py:350
  32.6 2.2 %collective-permute-start.6 = (f32[8,256]{1,0:T(8,128)S(1)}, f32[8,256]{1,0:T(8,128)S(1)}, u32[]{:S(2)}, u32[]{:S(2)}) collective-permute-start(f32[8,256]{1,0:T(8,128)S(1)} %get-tuple-element.45), channel_id=1, source_target_pairs={{0,4},{4,0},{8,12},{12,8},{1,5},{5,1},{9,13},{13,9},{2,6},{6,2},{1... | collective-permute-start | bytes 24584 | tf_op jit(solution)/shard_map/ppermute | solution.py:350
  32.6 3.1 %collective-permute-start.8 = (f32[8,256]{1,0:T(8,128)S(1)}, f32[8,256]{1,0:T(8,128)S(1)}, u32[]{:S(2)}, u32[]{:S(2)}) collective-permute-start(f32[8,256]{1,0:T(8,128)S(1)} %get-tuple-element.46), channel_id=1, source_target_pairs={{0,12},{4,8},{8,4},{12,0},{1,13},{5,9},{9,5},{13,1},{2,14},{6,10},... | collective-permute-start | bytes 24584 | tf_op jit(solution)/shard_map/ppermute | solution.py:350
  34.0 3.7 %collective-permute-start.7 = (f32[8,256]{1,0:T(8,128)S(1)}, f32[8,256]{1,0:T(8,128)S(1)}, u32[]{:S(2)}, u32[]{:S(2)}) collective-permute-start(f32[8,256]{1,0:T(8,128)S(1)} %get-tuple-element.47), channel_id=1, source_target_pairs={{0,8},{4,12},{8,0},{12,4},{1,9},{5,13},{9,1},{13,5},{2,10},{6,14},... | collective-permute-start | bytes 24584 | tf_op jit(solution)/shard_map/ppermute | solution.py:350

commit v4 on v3

--- a/solution.py
+++ b/solution.py
@@ -17,6 +17,11 @@
 BF = jnp.bfloat16
 F32 = jnp.float32
 VMEM_LIMIT = 24 * 1024 * 1024
+GIN_F, GOUT_F, GOUT_B, GIN_B = 1, 2, 1, 1
+WF = 2048
+WB = 2048
+TURN_F = 8192
+TURN_B = 8192
 
 
 def sigmoid(values):
@@ -36,8 +41,9 @@
 
 
 def one_hot(row, count):
-    lines = lax.broadcasted_iota(jnp.int32, (count, row.shape[1]), 0)
-    return jnp.where(lines == row, 1.0, 0.0).astype(BF)
+    lines = lax.broadcasted_iota(jnp.int16, (count, row.shape[1]), 0)
+    one = jnp.ones((count, row.shape[1]), BF)
+    return jnp.where(lines == row.astype(jnp.int16), one, jnp.zeros_like(one))
 
 
 def choose(stacked, group, groups):
@@ -187,6 +193,25 @@
         place_out[:, cols] = trip_out[:, cols]
 
 
+def keep(table, start, values):
+    channels, count = values.shape
+    low = table.shape[1]
+    piece = min(low, count)
+    for at in range(0, count, piece):
+        group, off = divmod(start + at, low)
+        table[group * channels : (group + 1) * channels, off : off + piece] = values[:, at : at + piece]
+
+
+def part_of(table, channels, start, count):
+    low = table.shape[1]
+    piece = min(low, count)
+    out = []
+    for at in range(start, start + count, piece):
+        group, off = divmod(at, low)
+        out.append(table[group * channels : (group + 1) * channels, off : off + piece])
+    return jnp.concatenate(out, axis=1) if len(out) > 1 else out[0]
+
+
 def main_kernel(
     peers,
     ecap,
@@ -214,12 +239,11 @@
     channels, edges = part.shape
     nodes = node.shape[1]
     trips = angular.shape[1]
-    groups = slot_table.shape[0] // channels
-    low_in = slot_table.shape[1]
-    low_out = edges // groups
+    get_in, low_in = slot_table.shape[0] // channels, slot_table.shape[1]
+    put_out, low_put = gather_sum.shape[1] // channels, gather_sum.shape[0]
+    get_out, low_get = grad_table.shape[0] // channels, grad_table.shape[1]
+    put_in, low_back = slot_sum.shape[1] // channels, slot_sum.shape[0]
     step = 512
-    width = min(1024, trips)
-    turn_width = min(4096, trips)
 
     src_table = jnp.concatenate([received[d][:channels] for d in range(peers)], axis=0)
 
@@ -243,11 +267,7 @@
         slot_radial, slot_slope, lengths = radial_terms(squared_length(vec), w_radial[...])
         preact = src_rows(one_hot(src_node, nodes), src_peer) + extra[:channels]
         active = preact * sigmoid(preact)
-        place = d * ecap
-        low = place % low_in
-        slot_table[(place // low_in) * channels : (place // low_in + 1) * channels, low : low + ecap] = (
-            active * slot_radial
-        ).astype(BF)
+        keep(slot_table, d * ecap, (active * slot_radial).astype(BF))
         slot_rate[:, cols] = active * slot_slope
         slots.append((vec / lengths, src_node, src_peer, rest[9:10].astype(jnp.int32)))
 
@@ -255,27 +275,31 @@
         high = place // low_count
         return high, one_hot(place - high * low_count, low_count)
 
-    gather_sum[...] = jnp.zeros_like(gather_sum)
-
-    def forward(turn, carry):
-        total = None
-        for sub in range(turn_width // width):
-            cols = pl.ds(pl.multiple_of(turn * turn_width + sub * width, width), width)
-            high_in, hot_in = split(place_in[:, cols], low_in)
-            high_out, hot_out = split(place_out[:, cols], low_out)
-            rows = choose(dot_nn(slot_table[...], hot_in), high_in, groups)
-            more = dot_nt(hot_out, expand((rows * angular[:, cols]).astype(BF), high_out, groups))
-            total = more if total is None else total + more
-        gather_sum[...] += total
-        return carry
-
-    lax.fori_loop(0, trips // turn_width, forward, 0)
+    def sweep(total, table, get_place, get_groups, put_place, put_groups, width, turn_width):
+        width, turn_width = min(width, trips), min(turn_width, trips)
+        total[...] = jnp.zeros_like(total)
+
+        def turn(number, carry):
+            found = None
+            for sub in range(turn_width // width):
+                cols = pl.ds(pl.multiple_of(number * turn_width + sub * width, width), width)
+                high_get, hot_get = split(get_place[:, cols], table.shape[1])
+                high_put, hot_put = split(put_place[:, cols], total.shape[0])
+                term = choose(dot_nn(table[...], hot_get), high_get, get_groups) * angular[:, cols]
+                more = dot_nt(hot_put, expand(term.astype(BF), high_put, put_groups))
+                found = more if found is None else found + more
+            total[...] += found
+            return carry
+
+        lax.fori_loop(0, trips // turn_width, turn, 0)
+
+    sweep(gather_sum, slot_table, place_in, get_in, place_out, put_out, WF, TURN_F)
 
     gathered = gather_sum[...].T
     atom_sum = jnp.zeros((channels, nodes), F32)
-    for g in range(groups):
-        cols = slice(g * low_out, (g + 1) * low_out)
-        value = gathered[g * channels : (g + 1) * channels]
+    for start in range(0, edges, step):
+        cols = slice(start, start + step)
+        value = part_of(gathered, channels, start, step)
         fresh = edge[:, cols].astype(F32) + message[:, cols].astype(F32) + value * sigmoid(value)
         edge_out[:, cols] = fresh.astype(BF)
         high, low = halves(fresh)
@@ -287,32 +311,16 @@
     grad_node = w_energy[...] * (sig * (1.0 + node_new * (1.0 - sig))) * scale
     high, low = halves(grad_node)
     grad_pair = jnp.concatenate([high, low], axis=0)
-    for g in range(groups):
-        cols = slice(g * low_out, (g + 1) * low_out)
-        value = gathered[g * channels : (g + 1) * channels]
+    for start in range(0, edges, step):
+        cols = slice(start, start + step)
+        value = part_of(gathered, channels, start, step)
         rows = dot_nn(grad_pair, target_hot[:, cols])
         grad_edge = rows[:channels] + rows[channels:]
         sig = sigmoid(value)
-        grad_table[g * channels : (g + 1) * channels, :] = (
-            grad_edge * (sig * (1.0 + value * (1.0 - sig)))
-        ).astype(BF)
+        keep(grad_table, start, (grad_edge * (sig * (1.0 + value * (1.0 - sig)))).astype(BF))
         edge_grad[:, cols] = jnp.sum(grad_edge * own_rate[:, cols], axis=0, keepdims=True)
 
-    slot_sum[...] = jnp.zeros_like(slot_sum)
-
-    def backward(turn, carry):
-        total = None
-        for sub in range(turn_width // width):
-            cols = pl.ds(pl.multiple_of(turn * turn_width + sub * width, width), width)
-            high_in, hot_in = split(place_in[:, cols], low_in)
-            high_out, hot_out = split(place_out[:, cols], low_out)
-            rows = choose(dot_nn(grad_table[...], hot_out), high_out, groups)
-            more = dot_nt(hot_in, expand((rows * angular[:, cols]).astype(BF), high_in, groups))
-            total = more if total is None else total + more
-        slot_sum[...] += total
-        return carry
-
-    lax.fori_loop(0, trips // turn_width, backward, 0)
+    sweep(slot_sum, grad_table, place_out, get_out, place_in, put_in, WB, TURN_B)
 
     moves[...] = jnp.zeros_like(moves)
 
@@ -331,9 +339,7 @@
     slot_grad = slot_sum[...].T
     for d in range(peers):
         cols = slice(d * ecap, (d + 1) * ecap)
-        place = d * ecap
-        low = place % low_in
-        grads = slot_grad[(place // low_in) * channels : (place // low_in + 1) * channels, low : low + ecap]
+        grads = part_of(slot_grad, channels, d * ecap, ecap)
         slot_unit, src_node, src_peer, dst_node = slots[d]
         terms = push_terms(slot_unit * jnp.sum(grads * slot_rate[:, cols], axis=0, keepdims=True))
         moves[...] += dot_nt(
@@ -385,8 +391,8 @@
     trips = triplet_basis.shape[1]
     ecap = edge_send.shape[2]
     groups = 256 // channels
-    low_in = peers * ecap // groups
-    low_out = edges // groups
+    slots = peers * ecap
+    tables = [GIN_F * groups, GOUT_F * groups, GOUT_B * groups, GIN_B * groups]
     shape = pltpu.VMEM
     params = pltpu.CompilerParams(vmem_limit_bytes=VMEM_LIMIT)
 
@@ -468,12 +474,12 @@
         scratch_shapes=[
             pltpu.VMEM((channels, edges), BF),
             pltpu.VMEM((channels, edges), F32),
-            pltpu.VMEM((channels, peers * ecap), F32),
-            pltpu.VMEM((groups * channels, low_in), BF),
-            pltpu.VMEM((low_out, groups * channels), F32),
-            pltpu.VMEM((groups * channels, low_out), BF),
+            pltpu.VMEM((channels, slots), F32),
+            pltpu.VMEM((tables[0] * channels, slots // tables[0]), BF),
+            pltpu.VMEM((edges // tables[1], tables[1] * channels), F32),
+            pltpu.VMEM((tables[2] * channels, edges // tables[2]), BF),
             pltpu.VMEM((1, edges), F32),
-            pltpu.VMEM((low_in, groups * channels), F32),
+            pltpu.VMEM((slots // tables[3], tables[3] * channels), F32),
             pltpu.VMEM((peers * TERM, nodes), F32),
         ],
         compiler_params=params,

time: 38.4 us -> 35.3 us (0.919)
  Pallas kernels: 18 us -> 14.8 us
    pallas_call x1, Pallas kernels: 13 us -> 10 us  [shards(): pl.pallas_call(functools.partial(main_kernel, peers, ecap, math.sqrt(NODE...]
  transfers between devices with their start and end apart: 9 -> 9, of which waited for: 6 -> 6; matrix products, arithmetic and copies ran while one was open for 0% -> 0% of each run, Pallas kernels for 5% -> 6%
where the time goes in v4:
time: 35.3 us; the launch traced here: 35.1 us
  Pallas kernels  14.8 us (42%)
  starting transfers between devices  9.78 us (28%)
  waiting for transfers between devices  9.24 us (26%)
  between operations  0.68 us (2%)
  other arithmetic  0.62 us (2%)
    pallas_call x1, Pallas kernels, shards(): pl.pallas_call(functools.partial(main_kernel, peers, ecap, math.sqrt(NODE...  10 us
    ppermute x9, starting transfers between devices, exchange(): return lax.ppermute(values, axis, [(i, i ^ distance) for i in range(count)])  9.78 us
    ppermute x9, waiting for transfers between devices, exchange(): return lax.ppermute(values, axis, [(i, i ^ distance) for i in range(count)])  9.24 us
    pallas_call x1, Pallas kernels, shards(): pl.pallas_call(functools.partial(prep_kernel, peers), name='prep', in_spe...  2.72 us
    pallas_call x1, Pallas kernels, shards(): pl.pallas_call(functools.partial(local_kernel, ecap), name='local', in_sp...  2.07 us
  transfers between devices with their start and end apart: 9, of which 6 were waited for; matrix products, arithmetic and copies ran while one was open for 0% of the time, Pallas kernels for 6%

profile of v4, /device:TPU:0, one launch (start us, length us, event | category | flops | bytes accessed | tf_op | source)
XLA Modules:
  0.0 35.1 jit_solution(12647124890780089636)
XLA Ops:
  0.6 2.7 %prep.1 = (f32[64,2048]{1,0:T(8,128)S(1)}, f32[16,2048]{1,0:T(8,128)S(1)}, bf16[256,2048]{1,0:T(8,128)(2,1)S(1)}, bf16[64,256]{1,0:T(8,128)(2,1)S(1)}, bf16[64,2...) custom-call(bf16[256,256]{1,0:T(8,128)(2,1)} %refs_0_.2, ...), custom_call_target="tpu_custom_call" | custom-call | tf_op jit(solution)/shard_map/prep/pallas_call | solution.py:420
  3.4 0.5 %collective-permute-start = (bf16[144,256]{1,0:T(8,128)(2,1)S(1)}, bf16[144,256]{1,0:T(8,128)(2,1)S(1)}, u32[]{:S(2)}, u32[]{:S(2)}) collective-permute-start(bf16[144,256]{1,0:T(8,128)(2,1)S(1)} %get-tuple-element.39), channel_id=1, source_target_pairs={{0,4},{4,0},{8,12},{12,8},{1,5},{5,1},{9,13},{13,9},{2,6},{6,2},{1... | collective-permute-start | bytes 221192 | tf_op jit(solution)/shard_map/ppermute | solution.py:356
  3.9 2.6 %collective-permute-start.1 = (bf16[144,256]{1,0:T(8,128)(2,1)S(1)}, bf16[144,256]{1,0:T(8,128)(2,1)S(1)}, u32[]{:S(2)}, u32[]{:S(2)}) collective-permute-start(bf16[144,256]{1,0:T(8,128)(2,1)S(1)} %get-tuple-element.40), channel_id=1, source_target_pairs={{0,8},{4,12},{8,0},{12,4},{1,9},{5,13},{9,1},{13,5},{2,10},{6,14},... | collective-permute-start | bytes 221192 | tf_op jit(solution)/shard_map/ppermute | solution.py:356
  6.5 0.1 collective-permute-start.2
  6.5 2.1 %local.1 = (f32[64,2048]{1,0:T(8,128)S(1)}, f32[64,2048]{1,0:T(8,128)S(1)}, f32[3,2048]{1,0:T(4,128)S(1)}, f32[64,8192]{1,0:T(8,128)S(1)}, s32[1,8192]{1,0:T(1,1...) custom-call(f32[16,2048]{1,0:T(8,128)S(1)} %get-tuple-element.25.mis, ...), custom_call_target="tpu_custom_call" | custom-call | flops 1073741824 | bytes 8388608 | tf_op jit(solution)/shard_map/local/pallas_call | solution.py:446
  8.6 0.0 collective-permute-done.refs_1_
  8.6 0.7 %collective-permute-done.1.refs_2_ = bf16[144,256]{1,0:T(8,128)(2,1)S(1)} collective-permute-done((bf16[144,256]{1,0:T(8,128)(2,1)S(1)}, bf16[144,256]{1,0:T(8,128)(2,1)S(1)}, u32[]{:S(2)}, u32[]{:S(2)}) %collective-permute-start.1) | collective-permute-done | bytes 73760 | tf_op jit(solution)/shard_map/ppermute | solution.py:356
  9.3 1.4 %collective-permute-done.2.refs_3_ = bf16[144,256]{1,0:T(8,128)(2,1)S(1)} collective-permute-done((bf16[144,256]{1,0:T(8,128)(2,1)S(1)}, bf16[144,256]{1,0:T(8,128)(2,1)S(1)}, u32[]{:S(2)}, u32[]{:S(2)}) %collective-permute-start.2) | collective-permute-done | bytes 73760 | tf_op jit(solution)/shard_map/ppermute | solution.py:356
  10.7 10.0 %main.1 = (bf16[64,256]{1,0:T(8,128)(2,1)}, bf16[64,2048]{1,0:T(8,128)(2,1)}, f32[4,8,256]{2,1,0:T(8,128)S(1)}) custom-call(f32[64,2048]{1,0:T(8,128)S(1)} %get-tuple-element.24.part, f32[16,2048]{1,0:T(8,128)S(1)} %get-tuple-element.25.misc, bf16[256,2048]{1,0:T(8,128)(2,1)S(1)} %get-tuple-element.26.target_hot, ...), custom_call_target="tpu_custom_call" | custom-call | tf_op jit(solution)/shard_map/main/pallas_call | solution.py:466
  20.7 3.8 %collective-permute-start.5 = (f32[4,8,256]{2,1,0:T(8,128)S(1)}, f32[4,8,256]{2,1,0:T(8,128)S(1)}, u32[]{:S(2)}, u32[]{:S(2)}) collective-permute-start(f32[4,8,256]{2,1,0:T(8,128)S(1)} %get-tuple-element.44), channel_id=1, source_target_pairs={{0,3},{1,2},{2,1},{3,0},{4,7},{5,6},{6,5},{7,4},{8,11},{9,10},{10,... | collective-permute-start | bytes 98312 | tf_op jit(solution)/shard_map/ppermute | solution.py:356
  24.5 0.0 collective-permute-start.4
  24.5 0.6 %collective-permute-start.3 = (f32[4,8,256]{2,1,0:T(8,128)S(1)}, f32[4,8,256]{2,1,0:T(8,128)S(1)}, u32[]{:S(2)}, u32[]{:S(2)}) collective-permute-start(f32[4,8,256]{2,1,0:T(8,128)S(1)} %get-tuple-element.44), channel_id=1, source_target_pairs={{0,1},{1,0},{2,3},{3,2},{4,5},{5,4},{6,7},{7,6},{8,9},{9,8},{10,11... | collective-permute-start | bytes 98312 | tf_op jit(solution)/shard_map/ppermute | solution.py:356
  25.1 1.4 %collective-permute-done.5 = f32[4,8,256]{2,1,0:T(8,128)S(1)} collective-permute-done((f32[4,8,256]{2,1,0:T(8,128)S(1)}, f32[4,8,256]{2,1,0:T(8,128)S(1)}, u32[]{:S(2)}, u32[]{:S(2)}) %collective-permute-start.5) | collective-permute-done | bytes 32800 | tf_op jit(solution)/shard_map/ppermute | solution.py:356
  26.5 2.9 %collective-permute-done.4 = f32[4,8,256]{2,1,0:T(8,128)S(1)} collective-permute-done((f32[4,8,256]{2,1,0:T(8,128)S(1)}, f32[4,8,256]{2,1,0:T(8,128)S(1)}, u32[]{:S(2)}, u32[]{:S(2)}) %collective-permute-start.4) | collective-permute-done | bytes 32800 | tf_op jit(solution)/shard_map/ppermute | solution.py:356
  29.3 0.0 collective-permute-done.3
  29.4 0.1 collective-permute-start.6
  29.5 1.4 %collective-permute-start.8 = (f32[8,256]{1,0:T(8,128)S(1)}, f32[8,256]{1,0:T(8,128)S(1)}, u32[]{:S(2)}, u32[]{:S(2)}) collective-permute-start(f32[8,256]{1,0:T(8,128)S(1)} %get-tuple-element.46), channel_id=1, source_target_pairs={{0,12},{4,8},{8,4},{12,0},{1,13},{5,9},{9,5},{13,1},{2,14},{6,10},... | collective-permute-start | bytes 24584 | tf_op jit(solution)/shard_map/ppermute | solution.py:356
  30.9 0.7 %collective-permute-start.7 = (f32[8,256]{1,0:T(8,128)S(1)}, f32[8,256]{1,0:T(8,128)S(1)}, u32[]{:S(2)}, u32[]{:S(2)}) collective-permute-start(f32[8,256]{1,0:T(8,128)S(1)} %get-tuple-element.47), channel_id=1, source_target_pairs={{0,8},{4,12},{8,0},{12,4},{1,9},{5,13},{9,1},{13,5},{2,10},{6,14},... | collective-permute-start | bytes 24584 | tf_op jit(solution)/shard_map/ppermute | solution.py:356
  31.6 0.0 collective-permute-done.6
  31.6 1.0 %collective-permute-done.8 = f32[8,256]{1,0:T(8,128)S(1)} collective-permute-done((f32[8,256]{1,0:T(8,128)S(1)}, f32[8,256]{1,0:T(8,128)S(1)}, u32[]{:S(2)}, u32[]{:S(2)}) %collective-permute-start.8) | collective-permute-done | bytes 8224 | tf_op jit(solution)/shard_map/ppermute | solution.py:356
  32.6 1.9 %collective-permute-done.7 = f32[8,256]{1,0:T(8,128)S(1)} collective-permute-done((f32[8,256]{1,0:T(8,128)S(1)}, f32[8,256]{1,0:T(8,128)S(1)}, u32[]{:S(2)}, u32[]{:S(2)}) %collective-permute-start.7) | collective-permute-done | bytes 8224 | tf_op jit(solution)/shard_map/ppermute | solution.py:356
  34.5 0.6 %slice_add_fusion = f32[3,256]{1,0:T(4,128)} fusion(f32[8,256]{1,0:T(8,128)S(1)} %fusion.2), kind=kLoop, calls=%fused_computation.8 | loop fusion | flops 768 | bytes 9216 | tf_op jit(solution)/shard_map/add | solution.py:491
  (3 shorter events, 0.0 us)
Async XLA Ops:
  3.4 5.3 %collective-permute-start = (bf16[144,256]{1,0:T(8,128)(2,1)S(1)}, bf16[144,256]{1,0:T(8,128)(2,1)S(1)}, u32[]{:S(2)}, u32[]{:S(2)}) collective-permute-start(bf16[144,256]{1,0:T(8,128)(2,1)S(1)} %get-tuple-element.39), channel_id=1, source_target_pairs={{0,4},{4,0},{8,12},{12,8},{1,5},{5,1},{9,13},{13,9},{2,6},{6,2},{1... | collective-permute-start | bytes 221192 | tf_op jit(solution)/shard_map/ppermute | solution.py:356
  3.9 5.4 %collective-permute-start.1 = (bf16[144,256]{1,0:T(8,128)(2,1)S(1)}, bf16[144,256]{1,0:T(8,128)(2,1)S(1)}, u32[]{:S(2)}, u32[]{:S(2)}) collective-permute-start(bf16[144,256]{1,0:T(8,128)(2,1)S(1)} %get-tuple-element.40), channel_id=1, source_target_pairs={{0,8},{4,12},{8,0},{12,4},{1,9},{5,13},{9,1},{13,5},{2,10},{6,14},... | collective-permute-start | bytes 221192 | tf_op jit(solution)/shard_map/ppermute | solution.py:356
  6.5 4.2 %collective-permute-start.2 = (bf16[144,256]{1,0:T(8,128)(2,1)S(1)}, bf16[144,256]{1,0:T(8,128)(2,1)S(1)}, u32[]{:S(2)}, u32[]{:S(2)}) collective-permute-start(bf16[144,256]{1,0:T(8,128)(2,1)S(1)} %get-tuple-element.41), channel_id=1, source_target_pairs={{0,12},{4,8},{8,4},{12,0},{1,13},{5,9},{9,5},{13,1},{2,14},{6,10},... | collective-permute-start | bytes 221192 | tf_op jit(solution)/shard_map/ppermute | solution.py:356
  20.7 5.8 %collective-permute-start.5 = (f32[4,8,256]{2,1,0:T(8,128)S(1)}, f32[4,8,256]{2,1,0:T(8,128)S(1)}, u32[]{:S(2)}, u32[]{:S(2)}) collective-permute-start(f32[4,8,256]{2,1,0:T(8,128)S(1)} %get-tuple-element.44), channel_id=1, source_target_pairs={{0,3},{1,2},{2,1},{3,0},{4,7},{5,6},{6,5},{7,4},{8,11},{9,10},{10,... | collective-permute-start | bytes 98312 | tf_op jit(solution)/shard_map/ppermute | solution.py:356
  24.5 4.8 %collective-permute-start.4 = (f32[4,8,256]{2,1,0:T(8,128)S(1)}, f32[4,8,256]{2,1,0:T(8,128)S(1)}, u32[]{:S(2)}, u32[]{:S(2)}) collective-permute-start(f32[4,8,256]{2,1,0:T(8,128)S(1)} %get-tuple-element.44), channel_id=1, source_target_pairs={{0,2},{1,3},{2,0},{3,1},{4,6},{5,7},{6,4},{7,5},{8,10},{9,11},{10,... | collective-permute-start | bytes 98312 | tf_op jit(solution)/shard_map/ppermute | solution.py:356
  24.5 4.8 %collective-permute-start.3 = (f32[4,8,256]{2,1,0:T(8,128)S(1)}, f32[4,8,256]{2,1,0:T(8,128)S(1)}, u32[]{:S(2)}, u32[]{:S(2)}) collective-permute-start(f32[4,8,256]{2,1,0:T(8,128)S(1)} %get-tuple-element.44), channel_id=1, source_target_pairs={{0,1},{1,0},{2,3},{3,2},{4,5},{5,4},{6,7},{7,6},{8,9},{9,8},{10,11... | collective-permute-start | bytes 98312 | tf_op jit(solution)/shard_map/ppermute | solution.py:356
  29.4 2.2 %collective-permute-start.6 = (f32[8,256]{1,0:T(8,128)S(1)}, f32[8,256]{1,0:T(8,128)S(1)}, u32[]{:S(2)}, u32[]{:S(2)}) collective-permute-start(f32[8,256]{1,0:T(8,128)S(1)} %get-tuple-element.45), channel_id=1, source_target_pairs={{0,4},{4,0},{8,12},{12,8},{1,5},{5,1},{9,13},{13,9},{2,6},{6,2},{1... | collective-permute-start | bytes 24584 | tf_op jit(solution)/shard_map/ppermute | solution.py:356
  29.5 3.1 %collective-permute-start.8 = (f32[8,256]{1,0:T(8,128)S(1)}, f32[8,256]{1,0:T(8,128)S(1)}, u32[]{:S(2)}, u32[]{:S(2)}) collective-permute-start(f32[8,256]{1,0:T(8,128)S(1)} %get-tuple-element.46), channel_id=1, source_target_pairs={{0,12},{4,8},{8,4},{12,0},{1,13},{5,9},{9,5},{13,1},{2,14},{6,10},... | collective-permute-start | bytes 24584 | tf_op jit(solution)/shard_map/ppermute | solution.py:356
  30.9 3.7 %collective-permute-start.7 = (f32[8,256]{1,0:T(8,128)S(1)}, f32[8,256]{1,0:T(8,128)S(1)}, u32[]{:S(2)}, u32[]{:S(2)}) collective-permute-start(f32[8,256]{1,0:T(8,128)S(1)} %get-tuple-element.47), channel_id=1, source_target_pairs={{0,8},{4,12},{8,0},{12,4},{1,9},{5,13},{9,1},{13,5},{2,10},{6,14},... | collective-permute-start | bytes 24584 | tf_op jit(solution)/shard_map/ppermute | solution.py:356

commit v5 on v4

--- a/solution.py
+++ b/solution.py
@@ -17,6 +17,7 @@
 BF = jnp.bfloat16
 F32 = jnp.float32
 VMEM_LIMIT = 24 * 1024 * 1024
+GRAPH_ORDER, CHAN_ORDER = "213", "123"
 GIN_F, GOUT_F, GOUT_B, GIN_B = 1, 2, 1, 1
 WF = 2048
 WB = 2048
@@ -99,31 +100,25 @@
     low_count = edges // high_count
     pieces = [slice(h * low_count, (h + 1) * low_count) for h in range(high_count)]
     copies = fetch(
-        list(sources[:9]) + [edge_source.at[:, cols] for cols in pieces],
-        list(places[:9]) + [edge.at[:, cols] for cols in pieces],
+        list(sources[4:9]) + list(sources[:4]) + [edge_source.at[:, cols] for cols in pieces],
+        list(places[4:9]) + list(places[:4]) + [edge.at[:, cols] for cols in pieces],
         sems,
     )
+    copies = copies[5:9] + copies[:5] + copies[9:]
     node, w_source, w_target, w_edge, vector, node_send, edge_send, target, source = places[:9]
     me = lax.axis_index("graph")
     channels = w_source.shape[0]
     first_chan = pl.multiple_of(lax.axis_index("chan") * channels, channels)
     cap = node_send.shape[2]
-    for copy in copies[:9]:
+    for copy in copies[4:9]:
         copy.wait()
-    own_node_out[...] = node[pl.ds(first_chan, channels), :]
-    atoms = node[...]
-    proj_src = dot_nn(w_source[...], atoms).astype(BF)
-    dst_high, dst_low = halves(dot_nn(w_target[...], atoms))
-    dst_table = jnp.concatenate([dst_high, dst_low], axis=0)
     own_nodes = jnp.concatenate([node_send[q, pl.ds(me, 1), :] for q in range(peers)], axis=0)
     own_nodes = own_nodes.astype(F32).astype(BF)
-    parts = []
-    for h, cols in enumerate(pieces):
+    miscs = []
+    for cols in pieces:
         dst = target[:, cols]
         src = source[:, cols]
-        hot = one_hot(dst, atoms.shape[1])
-        target_hot[:, cols] = hot
-        rows = dot_nn(dst_table, hot)
+        target_hot[:, cols] = one_hot(dst, target_hot.shape[0])
         src_peer = src // cap
         by_peer = dot_nn(own_nodes, one_hot(src - src_peer * cap, cap))
         src_node = choose(by_peer, src_peer, peers)
@@ -144,18 +139,32 @@
             axis=0,
         )
         misc_out[:, cols] = misc
+        miscs.append(misc.astype(BF))
+    picks = []
+    for d in range(peers):
+        chosen = edge_send[me, pl.ds(jnp.bitwise_xor(me, d), 1), :]
+        high = jnp.where(chosen < 0, -1, chosen // low_count)
+        picks.append((high, one_hot(chosen % low_count, low_count)))
+    for copy in copies[:4]:
+        copy.wait()
+    own_node_out[...] = node[pl.ds(first_chan, channels), :]
+    atoms = node[...]
+    proj_src = dot_nn(w_source[...], atoms).astype(BF)
+    dst_high, dst_low = halves(dot_nn(w_target[...], atoms))
+    dst_table = jnp.concatenate([dst_high, dst_low], axis=0)
+    for d in range(peers):
+        sends[d][:channels] = proj_src
+    parts = []
+    for h, cols in enumerate(pieces):
+        rows = dot_nn(dst_table, target_hot[:, cols])
         copies[9 + h].wait()
         part = rows[:channels] + rows[channels:] + dot_nn(w_edge[...], edge[:, cols])
         part_out[:, cols] = part
         own_edge_out[:, cols] = edge[pl.ds(first_chan, channels), cols]
-        parts.append(jnp.concatenate([part.astype(BF), misc.astype(BF)], axis=0))
+        parts.append(jnp.concatenate([part.astype(BF), miscs[h]], axis=0))
     table = jnp.concatenate(parts, axis=0)
-    for d in range(peers):
-        chosen = edge_send[me, pl.ds(jnp.bitwise_xor(me, d), 1), :]
-        high = jnp.where(chosen < 0, -1, chosen // low_count)
-        picked = choose(dot_nn(table, one_hot(chosen % low_count, low_count)), high, high_count)
-        sends[d][:channels] = proj_src
-        sends[d][channels:] = picked.astype(BF)
+    for d, (high, hot) in enumerate(picks):
+        sends[d][channels:] = choose(dot_nn(table, hot), high, high_count).astype(BF)
 
 
 def local_kernel(ecap, misc, *refs):
@@ -243,7 +252,7 @@
     put_out, low_put = gather_sum.shape[1] // channels, gather_sum.shape[0]
     get_out, low_get = grad_table.shape[0] // channels, grad_table.shape[1]
     put_in, low_back = slot_sum.shape[1] // channels, slot_sum.shape[0]
-    step = 512
+    step = 256
 
     src_table = jnp.concatenate([received[d][:channels] for d in range(peers)], axis=0)
 
@@ -277,21 +286,19 @@
 
     def sweep(total, table, get_place, get_groups, put_place, put_groups, width, turn_width):
         width, turn_width = min(width, trips), min(turn_width, trips)
-        total[...] = jnp.zeros_like(total)
-
-        def turn(number, carry):
+
+        def turn(number):
             found = None
             for sub in range(turn_width // width):
-                cols = pl.ds(pl.multiple_of(number * turn_width + sub * width, width), width)
+                cols = slice(number * turn_width + sub * width, number * turn_width + (sub + 1) * width)
                 high_get, hot_get = split(get_place[:, cols], table.shape[1])
                 high_put, hot_put = split(put_place[:, cols], total.shape[0])
                 term = choose(dot_nn(table[...], hot_get), high_get, get_groups) * angular[:, cols]
                 more = dot_nt(hot_put, expand(term.astype(BF), high_put, put_groups))
                 found = more if found is None else found + more
-            total[...] += found
-            return carry
-
-        lax.fori_loop(0, trips // turn_width, turn, 0)
+            return found
+
+        total[...] = functools.reduce(jnp.add, [turn(number) for number in range(trips // turn_width)])
 
     sweep(gather_sum, slot_table, place_in, get_in, place_out, put_out, WF, TURN_F)
 
@@ -348,7 +355,13 @@
         moves[d * TERM : (d + 1) * TERM] -= dot_nt(
             jnp.concatenate([terms, jnp.zeros_like(terms)], axis=0).astype(BF), one_hot(dst_node, nodes)
         )[:TERM]
-    force_out[...] = moves[...].reshape(force_out.shape)
+    half = nodes // 2
+    rows = []
+    for d in range(peers):
+        place = d * TERM
+        both = moves[place : place + 3] + moves[place + 3 : place + 6]
+        rows += [both[:, :half], both[:, half:]]
+    force_out[...] = jnp.concatenate(rows, axis=0)
 
 
 def exchange(values, axis, distance):
@@ -359,8 +372,10 @@
 def add_over(values, axis):
     count = lax.axis_size(axis)
     if count <= 4:
-        others = [exchange(values, axis, d) for d in range(1, count)]
-        return functools.reduce(jnp.add, others, values)
+        total = values
+        for d in sorted(range(1, count), key=lambda d: CHAN_ORDER.find(str(d))):
+            total = total + exchange(values, axis, d)
+        return total
     for bit in range(count.bit_length() - 1):
         values = values + exchange(values, axis, 1 << bit)
     return values
@@ -469,7 +484,7 @@
         out_shape=[
             jax.ShapeDtypeStruct((channels, nodes), BF),
             jax.ShapeDtypeStruct((channels, edges), BF),
-            shape((peers, TERM, nodes), F32),
+            shape((peers * 6, nodes // 2), F32),
         ],
         scratch_shapes=[
             pltpu.VMEM((channels, edges), BF),
@@ -484,11 +499,11 @@
         ],
         compiler_params=params,
     )(part, misc, target_hot, own_node, own_edge, *local, *received)
-    force = add_over(force, "chan")
-    mine = force[0]
-    for d in range(1, peers):
-        mine = mine + exchange(force[d], "graph", d)
-    return node_out, edge_out, mine[0:3] + mine[3:6]
+    mine = force[:6]
+    for d in sorted(range(1, peers), key=lambda d: GRAPH_ORDER.find(str(d))):
+        mine = mine + exchange(force[6 * d : 6 * d + 6], "graph", d)
+    mine = add_over(mine, "chan")
+    return node_out, edge_out, jnp.concatenate([mine[:3], mine[3:]], axis=1)
 
 
 def solution(mesh):

time: 35.3 us -> 34.1 us (0.966)
  waiting for transfers between devices: 9.24 us -> 8.21 us
    ppermute x9, waiting for transfers between devices: 9.24 us -> 8.21 us  [exchange(): return lax.ppermute(values, axis, [(i, i ^ distance) for i in range(count)])]
    add x3 -> x2, other arithmetic: 0.62 us -> 0.01 us  [the longest x1 0.01 us: shards(): mine = mine + exchange(force[6 * d:6 * d + 6], 'graph', d)]
    concatenate x0 -> x1, other arithmetic: none -> 0.6 us  [shards(): return (node_out, edge_out, jnp.concatenate([mine[:3], mine[3:]], axis=1))]
where the time goes in v5:
time: 34.1 us; the launch traced here: 33.9 us
  Pallas kernels  14.7 us (43%)
  starting transfers between devices  9.77 us (29%)
  waiting for transfers between devices  8.21 us (24%)
  between operations  0.68 us (2%)
  other arithmetic  0.61 us (2%)
    pallas_call x1, Pallas kernels, shards(): pl.pallas_call(functools.partial(main_kernel, peers, ecap, math.sqrt(NODE...  10.1 us
    ppermute x9, starting transfers between devices, exchange(): return lax.ppermute(values, axis, [(i, i ^ distance) for i in range(count)])  9.77 us
    ppermute x9, waiting for transfers between devices, exchange(): return lax.ppermute(values, axis, [(i, i ^ distance) for i in range(count)])  8.21 us
    pallas_call x1, Pallas kernels, shards(): pl.pallas_call(functools.partial(prep_kernel, peers), name='prep', in_spe...  2.52 us
    pallas_call x1, Pallas kernels, shards(): pl.pallas_call(functools.partial(local_kernel, ecap), name='local', in_sp...  2.06 us
  transfers between devices with their start and end apart: 9, of which 6 were waited for; matrix products, arithmetic and copies ran while one was open for 0% of the time, Pallas kernels for 6%

profile of v5, /device:TPU:0, one launch (start us, length us, event | category | flops | bytes accessed | tf_op | source)
XLA Modules:
  0.0 33.9 jit_solution(13601573596981462662)
XLA Ops:
  0.6 2.5 %prep.1 = (f32[64,2048]{1,0:T(8,128)S(1)}, f32[16,2048]{1,0:T(8,128)S(1)}, bf16[256,2048]{1,0:T(8,128)(2,1)S(1)}, bf16[64,256]{1,0:T(8,128)(2,1)S(1)}, bf16[64,2...) custom-call(bf16[256,256]{1,0:T(8,128)(2,1)} %refs_0_.2, ...), custom_call_target="tpu_custom_call" | custom-call | tf_op jit(solution)/shard_map/prep/pallas_call | solution.py:435
  3.2 0.5 %collective-permute-start = (bf16[144,256]{1,0:T(8,128)(2,1)S(1)}, bf16[144,256]{1,0:T(8,128)(2,1)S(1)}, u32[]{:S(2)}, u32[]{:S(2)}) collective-permute-start(bf16[144,256]{1,0:T(8,128)(2,1)S(1)} %get-tuple-element.39), channel_id=1, source_target_pairs={{0,4},{4,0},{8,12},{12,8},{1,5},{5,1},{9,13},{13,9},{2,6},{6,2},{1... | collective-permute-start | bytes 221192 | tf_op jit(solution)/shard_map/ppermute | solution.py:369
  3.7 2.6 %collective-permute-start.1 = (bf16[144,256]{1,0:T(8,128)(2,1)S(1)}, bf16[144,256]{1,0:T(8,128)(2,1)S(1)}, u32[]{:S(2)}, u32[]{:S(2)}) collective-permute-start(bf16[144,256]{1,0:T(8,128)(2,1)S(1)} %get-tuple-element.40), channel_id=1, source_target_pairs={{0,8},{4,12},{8,0},{12,4},{1,9},{5,13},{9,1},{13,5},{2,10},{6,14},... | collective-permute-start | bytes 221192 | tf_op jit(solution)/shard_map/ppermute | solution.py:369
  6.3 0.1 collective-permute-start.2
  6.3 2.1 %local.1 = (f32[64,2048]{1,0:T(8,128)S(1)}, f32[64,2048]{1,0:T(8,128)S(1)}, f32[3,2048]{1,0:T(4,128)S(1)}, f32[64,8192]{1,0:T(8,128)S(1)}, s32[1,8192]{1,0:T(1,1...) custom-call(f32[16,2048]{1,0:T(8,128)S(1)} %get-tuple-element.25.mis, ...), custom_call_target="tpu_custom_call" | custom-call | flops 1073741824 | bytes 8388608 | tf_op jit(solution)/shard_map/local/pallas_call | solution.py:461
  8.4 0.0 collective-permute-done.refs_1_
  8.4 0.7 %collective-permute-done.1.refs_2_ = bf16[144,256]{1,0:T(8,128)(2,1)S(1)} collective-permute-done((bf16[144,256]{1,0:T(8,128)(2,1)S(1)}, bf16[144,256]{1,0:T(8,128)(2,1)S(1)}, u32[]{:S(2)}, u32[]{:S(2)}) %collective-permute-start.1) | collective-permute-done | bytes 73760 | tf_op jit(solution)/shard_map/ppermute | solution.py:369
  9.1 1.4 %collective-permute-done.2.refs_3_ = bf16[144,256]{1,0:T(8,128)(2,1)S(1)} collective-permute-done((bf16[144,256]{1,0:T(8,128)(2,1)S(1)}, bf16[144,256]{1,0:T(8,128)(2,1)S(1)}, u32[]{:S(2)}, u32[]{:S(2)}) %collective-permute-start.2) | collective-permute-done | bytes 73760 | tf_op jit(solution)/shard_map/ppermute | solution.py:369
  10.5 10.1 %main.1 = (bf16[64,256]{1,0:T(8,128)(2,1)}, bf16[64,2048]{1,0:T(8,128)(2,1)}, f32[24,128]{1,0:T(8,128)S(1)}) custom-call(f32[64,2048]{1,0:T(8,128)S(1)} %get-tuple-element.24.part, f32[16,2048]{1,0:T(8,128)S(1)} %get-tuple-element.25.misc, bf16[256,2048]{1,0:T(8,128)(2,1)S(1)} %get-tuple-element.26.target_hot, bf16[64,256]{1,0:T(8,128)(2,1)S(1)} %get-tuple-element.27.node, ...), custom_call_target="tpu_custom_call" | custom-call | tf_op jit(solution)/shard_map/main/pallas_call | solution.py:481
  20.6 1.6 %collective-permute-start.3 = (f32[6,128]{1,0:T(8,128)S(1)}, f32[6,128]{1,0:T(8,128)S(1)}, u32[]{:S(2)}, u32[]{:S(2)}) collective-permute-start(f32[6,128]{1,0:T(8,128)S(1)} %get-tuple-element.45), channel_id=1, source_target_pairs={{0,8},{4,12},{8,0},{12,4},{1,9},{5,13},{9,1},{13,5},{2,10},{6,14},... | collective-permute-start | bytes 9224 | tf_op jit(solution)/shard_map/ppermute | solution.py:369
  22.1 0.0 collective-permute-start.5
  22.1 0.6 %collective-permute-start.4 = (f32[6,128]{1,0:T(8,128)S(1)}, f32[6,128]{1,0:T(8,128)S(1)}, u32[]{:S(2)}, u32[]{:S(2)}) collective-permute-start(f32[6,128]{1,0:T(8,128)S(1)} %get-tuple-element.47), channel_id=1, source_target_pairs={{0,4},{4,0},{8,12},{12,8},{1,5},{5,1},{9,13},{13,9},{2,6},{6,2},{1... | collective-permute-start | bytes 9224 | tf_op jit(solution)/shard_map/ppermute | solution.py:369
  22.7 1.5 %collective-permute-done.3 = f32[6,128]{1,0:T(8,128)S(1)} collective-permute-done((f32[6,128]{1,0:T(8,128)S(1)}, f32[6,128]{1,0:T(8,128)S(1)}, u32[]{:S(2)}, u32[]{:S(2)}) %collective-permute-start.3) | collective-permute-done | bytes 3104 | tf_op jit(solution)/shard_map/ppermute | solution.py:369
  24.2 1.0 %collective-permute-done.5 = f32[6,128]{1,0:T(8,128)S(1)} collective-permute-done((f32[6,128]{1,0:T(8,128)S(1)}, f32[6,128]{1,0:T(8,128)S(1)}, u32[]{:S(2)}, u32[]{:S(2)}) %collective-permute-start.5) | collective-permute-done | bytes 3104 | tf_op jit(solution)/shard_map/ppermute | solution.py:369
  25.2 0.0 collective-permute-done.4
  25.2 3.6 %collective-permute-start.8 = (f32[6,128]{1,0:T(8,128)S(1)}, f32[6,128]{1,0:T(8,128)S(1)}, u32[]{:S(2)}, u32[]{:S(2)}) collective-permute-start(f32[6,128]{1,0:T(8,128)S(1)} %add_add_fusion.1), channel_id=1, source_target_pairs={{0,3},{1,2},{2,1},{3,0},{4,7},{5,6},{6,5},{7,4},{8,11},{9,10},{10,... | collective-permute-start | bytes 9224 | tf_op jit(solution)/shard_map/ppermute | solution.py:369
  28.8 0.0 collective-permute-start.7
  28.8 0.8 %collective-permute-start.6 = (f32[6,128]{1,0:T(8,128)S(1)}, f32[6,128]{1,0:T(8,128)S(1)}, u32[]{:S(2)}, u32[]{:S(2)}) collective-permute-start(f32[6,128]{1,0:T(8,128)S(1)} %add_add_fusion.1), channel_id=1, source_target_pairs={{0,1},{1,0},{2,3},{3,2},{4,5},{5,4},{6,7},{7,6},{8,9},{9,8},{10,11... | collective-permute-start | bytes 9224 | tf_op jit(solution)/shard_map/ppermute | solution.py:369
  29.6 1.0 %collective-permute-done.8 = f32[6,128]{1,0:T(8,128)S(1)} collective-permute-done((f32[6,128]{1,0:T(8,128)S(1)}, f32[6,128]{1,0:T(8,128)S(1)}, u32[]{:S(2)}, u32[]{:S(2)}) %collective-permute-start.8) | collective-permute-done | bytes 3104 | tf_op jit(solution)/shard_map/ppermute | solution.py:369
  30.7 2.7 %collective-permute-done.7 = f32[6,128]{1,0:T(8,128)S(1)} collective-permute-done((f32[6,128]{1,0:T(8,128)S(1)}, f32[6,128]{1,0:T(8,128)S(1)}, u32[]{:S(2)}, u32[]{:S(2)}) %collective-permute-start.7) | collective-permute-done | bytes 3104 | tf_op jit(solution)/shard_map/ppermute | solution.py:369
  33.3 0.0 collective-permute-done.6
  33.4 0.6 %pad_maximum_fusion = f32[3,256]{1,0:T(4,128)} fusion(f32[3,128]{1,0:T(4,128)S(1)} %get-tuple-element.49, f32[3,128]{1,0:T(4,128)S(1)} %get-tuple-element.48), kind=kLoop, calls=%fused_computation | loop fusion | flops 768 | bytes 6144 | tf_op jit(solution)/shard_map/concatenate | solution.py:506
  (4 shorter events, 0.0 us)
Async XLA Ops:
  3.2 5.3 %collective-permute-start = (bf16[144,256]{1,0:T(8,128)(2,1)S(1)}, bf16[144,256]{1,0:T(8,128)(2,1)S(1)}, u32[]{:S(2)}, u32[]{:S(2)}) collective-permute-start(bf16[144,256]{1,0:T(8,128)(2,1)S(1)} %get-tuple-element.39), channel_id=1, source_target_pairs={{0,4},{4,0},{8,12},{12,8},{1,5},{5,1},{9,13},{13,9},{2,6},{6,2},{1... | collective-permute-start | bytes 221192 | tf_op jit(solution)/shard_map/ppermute | solution.py:369
  3.7 5.4 %collective-permute-start.1 = (bf16[144,256]{1,0:T(8,128)(2,1)S(1)}, bf16[144,256]{1,0:T(8,128)(2,1)S(1)}, u32[]{:S(2)}, u32[]{:S(2)}) collective-permute-start(bf16[144,256]{1,0:T(8,128)(2,1)S(1)} %get-tuple-element.40), channel_id=1, source_target_pairs={{0,8},{4,12},{8,0},{12,4},{1,9},{5,13},{9,1},{13,5},{2,10},{6,14},... | collective-permute-start | bytes 221192 | tf_op jit(solution)/shard_map/ppermute | solution.py:369
  6.3 4.2 %collective-permute-start.2 = (bf16[144,256]{1,0:T(8,128)(2,1)S(1)}, bf16[144,256]{1,0:T(8,128)(2,1)S(1)}, u32[]{:S(2)}, u32[]{:S(2)}) collective-permute-start(bf16[144,256]{1,0:T(8,128)(2,1)S(1)} %get-tuple-element.41), channel_id=1, source_target_pairs={{0,12},{4,8},{8,4},{12,0},{1,13},{5,9},{9,5},{13,1},{2,14},{6,10},... | collective-permute-start | bytes 221192 | tf_op jit(solution)/shard_map/ppermute | solution.py:369
  20.6 3.6 %collective-permute-start.3 = (f32[6,128]{1,0:T(8,128)S(1)}, f32[6,128]{1,0:T(8,128)S(1)}, u32[]{:S(2)}, u32[]{:S(2)}) collective-permute-start(f32[6,128]{1,0:T(8,128)S(1)} %get-tuple-element.45), channel_id=1, source_target_pairs={{0,8},{4,12},{8,0},{12,4},{1,9},{5,13},{9,1},{13,5},{2,10},{6,14},... | collective-permute-start | bytes 9224 | tf_op jit(solution)/shard_map/ppermute | solution.py:369
  22.1 3.0 %collective-permute-start.5 = (f32[6,128]{1,0:T(8,128)S(1)}, f32[6,128]{1,0:T(8,128)S(1)}, u32[]{:S(2)}, u32[]{:S(2)}) collective-permute-start(f32[6,128]{1,0:T(8,128)S(1)} %get-tuple-element.46), channel_id=1, source_target_pairs={{0,12},{4,8},{8,4},{12,0},{1,13},{5,9},{9,5},{13,1},{2,14},{6,10},... | collective-permute-start | bytes 9224 | tf_op jit(solution)/shard_map/ppermute | solution.py:369
  22.1 3.0 %collective-permute-start.4 = (f32[6,128]{1,0:T(8,128)S(1)}, f32[6,128]{1,0:T(8,128)S(1)}, u32[]{:S(2)}, u32[]{:S(2)}) collective-permute-start(f32[6,128]{1,0:T(8,128)S(1)} %get-tuple-element.47), channel_id=1, source_target_pairs={{0,4},{4,0},{8,12},{12,8},{1,5},{5,1},{9,13},{13,9},{2,6},{6,2},{1... | collective-permute-start | bytes 9224 | tf_op jit(solution)/shard_map/ppermute | solution.py:369
  25.2 5.5 %collective-permute-start.8 = (f32[6,128]{1,0:T(8,128)S(1)}, f32[6,128]{1,0:T(8,128)S(1)}, u32[]{:S(2)}, u32[]{:S(2)}) collective-permute-start(f32[6,128]{1,0:T(8,128)S(1)} %add_add_fusion.1), channel_id=1, source_target_pairs={{0,3},{1,2},{2,1},{3,0},{4,7},{5,6},{6,5},{7,4},{8,11},{9,10},{10,... | collective-permute-start | bytes 9224 | tf_op jit(solution)/shard_map/ppermute | solution.py:369
  28.8 4.5 %collective-permute-start.7 = (f32[6,128]{1,0:T(8,128)S(1)}, f32[6,128]{1,0:T(8,128)S(1)}, u32[]{:S(2)}, u32[]{:S(2)}) collective-permute-start(f32[6,128]{1,0:T(8,128)S(1)} %add_add_fusion.1), channel_id=1, source_target_pairs={{0,2},{1,3},{2,0},{3,1},{4,6},{5,7},{6,4},{7,5},{8,10},{9,11},{10,... | collective-permute-start | bytes 9224 | tf_op jit(solution)/shard_map/ppermute | solution.py:369
  28.8 4.5 %collective-permute-start.6 = (f32[6,128]{1,0:T(8,128)S(1)}, f32[6,128]{1,0:T(8,128)S(1)}, u32[]{:S(2)}, u32[]{:S(2)}) collective-permute-start(f32[6,128]{1,0:T(8,128)S(1)} %add_add_fusion.1), channel_id=1, source_target_pairs={{0,1},{1,0},{2,3},{3,2},{4,5},{5,4},{6,7},{7,6},{8,9},{9,8},{10,11... | collective-permute-start | bytes 9224 | tf_op jit(solution)/shard_map/ppermute | solution.py:369

commit v6 on v5

--- a/solution.py
+++ b/solution.py
@@ -202,6 +202,19 @@
         place_out[:, cols] = trip_out[:, cols]
 
 
+def push_terms(push):
+    high = push.astype(BF).astype(F32)
+    return jnp.concatenate([high, push - high, jnp.zeros((TERM - 6, push.shape[1]), F32)], axis=0)
+
+
+def late_kernel(unit, edge_grad, target_hot, out):
+    terms = push_terms(unit[...] * edge_grad[...])
+    sums = dot_nt(jnp.concatenate([terms, jnp.zeros_like(terms)], axis=0).astype(BF), target_hot[...])
+    both = -(sums[:3] + sums[3:6])
+    half = both.shape[1] // 2
+    out[...] = jnp.concatenate([both[:, :half], both[:, half:]], axis=0)
+
+
 def keep(table, start, values):
     channels, count = values.shape
     low = table.shape[1]
@@ -242,8 +255,8 @@
     *refs,
 ):
     received = refs[:peers]
-    node_out, edge_out, force_out = refs[peers : peers + 3]
-    message, own_rate, slot_rate, slot_table, gather_sum, grad_table, edge_grad, slot_sum, moves = refs[peers + 3 :]
+    node_out, edge_out, force_out, edge_grad = refs[peers : peers + 4]
+    message, own_rate, slot_rate, slot_table, gather_sum, grad_table, slot_sum, moves = refs[peers + 4 :]
     me = lax.axis_index("graph")
     channels, edges = part.shape
     nodes = node.shape[1]
@@ -293,7 +306,12 @@
                 cols = slice(number * turn_width + sub * width, number * turn_width + (sub + 1) * width)
                 high_get, hot_get = split(get_place[:, cols], table.shape[1])
                 high_put, hot_put = split(put_place[:, cols], total.shape[0])
-                term = choose(dot_nn(table[...], hot_get), high_get, get_groups) * angular[:, cols]
+                wide = dot_nn(table[...], hot_get)
+                rows = wide.shape[0] // get_groups
+                picked = wide[:rows]
+                for g in range(1, get_groups):
+                    picked = jnp.where(high_get == g, wide[g * rows : (g + 1) * rows], picked)
+                term = picked * angular[:, cols]
                 more = dot_nt(hot_put, expand(term.astype(BF), high_put, put_groups))
                 found = more if found is None else found + more
             return found
@@ -329,20 +347,9 @@
 
     sweep(slot_sum, grad_table, place_out, get_out, place_in, put_in, WB, TURN_B)
 
-    moves[...] = jnp.zeros_like(moves)
-
-    def push_terms(push):
-        high = push.astype(BF).astype(F32)
-        return jnp.concatenate([high, push - high, jnp.zeros((TERM - 6, push.shape[1]), F32)], axis=0)
-
-    for start in range(0, edges, step):
-        cols = slice(start, start + step)
-        terms = push_terms(unit[:, cols] * edge_grad[:, cols])
-        src_peer = jnp.bitwise_xor(misc[11:12, cols].astype(jnp.int32), me)
-        moves[...] += dot_nt(expand(terms, src_peer, peers).astype(BF), source_hot[:, cols])
-        moves[:TERM] -= dot_nt(
-            jnp.concatenate([terms, jnp.zeros_like(terms)], axis=0).astype(BF), target_hot[:, cols]
-        )[:TERM]
+    src_peer = jnp.bitwise_xor(misc[11:12, :].astype(jnp.int32), me)
+    terms = push_terms(unit[...] * edge_grad[...])
+    moves[...] = dot_nt(expand(terms, src_peer, peers).astype(BF), source_hot[...])
     slot_grad = slot_sum[...].T
     for d in range(peers):
         cols = slice(d * ecap, (d + 1) * ecap)
@@ -478,13 +485,14 @@
         compiler_params=params,
         cost_estimate=pl.CostEstimate(flops=2**30, bytes_accessed=2**23, transcendentals=2**18),
     )(misc, *[pltpu.with_memory_space_constraint(a, pltpu.HBM) for a in inputs])
-    node_out, edge_out, force = pl.pallas_call(
+    node_out, edge_out, force, edge_grad = pl.pallas_call(
         functools.partial(main_kernel, peers, ecap, math.sqrt(NODE_DEV / EDGE_DEV)),
         name="main",
         out_shape=[
             jax.ShapeDtypeStruct((channels, nodes), BF),
             jax.ShapeDtypeStruct((channels, edges), BF),
             shape((peers * 6, nodes // 2), F32),
+            shape((1, edges), F32),
         ],
         scratch_shapes=[
             pltpu.VMEM((channels, edges), BF),
@@ -493,13 +501,20 @@
             pltpu.VMEM((tables[0] * channels, slots // tables[0]), BF),
             pltpu.VMEM((edges // tables[1], tables[1] * channels), F32),
             pltpu.VMEM((tables[2] * channels, edges // tables[2]), BF),
-            pltpu.VMEM((1, edges), F32),
             pltpu.VMEM((slots // tables[3], tables[3] * channels), F32),
             pltpu.VMEM((peers * TERM, nodes), F32),
         ],
         compiler_params=params,
     )(part, misc, target_hot, own_node, own_edge, *local, *received)
-    mine = force[:6]
+    unit = local[2]
+    late = pl.pallas_call(
+        late_kernel,
+        name="late",
+        out_shape=shape((6, nodes // 2), F32),
+        compiler_params=params,
+        cost_estimate=pl.CostEstimate(flops=2**28, bytes_accessed=2**21, transcendentals=0),
+    )(unit, edge_grad, target_hot)
+    mine = force[:6] + late
     for d in sorted(range(1, peers), key=lambda d: GRAPH_ORDER.find(str(d))):
         mine = mine + exchange(force[6 * d : 6 * d + 6], "graph", d)
     mine = add_over(mine, "chan")

time: 34.1 us -> 33.8 us (level)
  waiting for transfers between devices: 8.21 us -> 7.83 us
    ppermute x9, waiting for transfers between devices: 8.21 us -> 7.83 us  [exchange(): return lax.ppermute(values, axis, [(i, i ^ distance) for i in range(count)])]
    pallas_call x0 -> x1, Pallas kernels: none -> 0.38 us  [shards(): pl.pallas_call(late_kernel, name='late', out_shape=shape((6, nodes // 2),...]
  transfers between devices with their start and end apart: 9 -> 9, of which waited for: 6 -> 6; matrix products, arithmetic and copies ran while one was open for 0% -> 0% of each run, Pallas kernels for 6% -> 7%
where the time goes in v6:
time: 33.8 us; the launch traced here: 33.7 us
  Pallas kernels  14.8 us (44%)
  starting transfers between devices  9.77 us (29%)
  waiting for transfers between devices  7.83 us (23%)
  between operations  0.68 us (2%)
  other arithmetic  0.61 us (2%)
    pallas_call x1, Pallas kernels, shards(): pl.pallas_call(functools.partial(main_kernel, peers, ecap, math.sqrt(NODE...  9.8 us
    ppermute x9, starting transfers between devices, exchange(): return lax.ppermute(values, axis, [(i, i ^ distance) for i in range(count)])  9.77 us
    ppermute x9, waiting for transfers between devices, exchange(): return lax.ppermute(values, axis, [(i, i ^ distance) for i in range(count)])  7.83 us
    pallas_call x1, Pallas kernels, shards(): pl.pallas_call(functools.partial(prep_kernel, peers), name='prep', in_spe...  2.52 us
    pallas_call x1, Pallas kernels, shards(): pl.pallas_call(functools.partial(local_kernel, ecap), name='local', in_sp...  2.06 us
  transfers between devices with their start and end apart: 9, of which 6 were waited for; matrix products, arithmetic and copies ran while one was open for 0% of the time, Pallas kernels for 7%

profile of v6, /device:TPU:0, one launch (start us, length us, event | category | flops | bytes accessed | tf_op | source)
XLA Modules:
  0.0 33.7 jit_solution(4054729860361843025)
XLA Ops:
  0.6 2.5 %prep.1 = (f32[64,2048]{1,0:T(8,128)S(1)}, f32[16,2048]{1,0:T(8,128)S(1)}, bf16[256,2048]{1,0:T(8,128)(2,1)S(1)}, bf16[64,256]{1,0:T(8,128)(2,1)S(1)}, bf16[64,2...) custom-call(bf16[256,256]{1,0:T(8,128)(2,1)} %refs_0_.2, ...), custom_call_target="tpu_custom_call" | custom-call | tf_op jit(solution)/shard_map/prep/pallas_call | solution.py:442
  3.2 0.5 %collective-permute-start = (bf16[144,256]{1,0:T(8,128)(2,1)S(1)}, bf16[144,256]{1,0:T(8,128)(2,1)S(1)}, u32[]{:S(2)}, u32[]{:S(2)}) collective-permute-start(bf16[144,256]{1,0:T(8,128)(2,1)S(1)} %get-tuple-element.40), channel_id=1, source_target_pairs={{0,4},{4,0},{8,12},{12,8},{1,5},{5,1},{9,13},{13,9},{2,6},{6,2},{1... | collective-permute-start | bytes 221192 | tf_op jit(solution)/shard_map/ppermute | solution.py:376
  3.7 2.6 %collective-permute-start.1 = (bf16[144,256]{1,0:T(8,128)(2,1)S(1)}, bf16[144,256]{1,0:T(8,128)(2,1)S(1)}, u32[]{:S(2)}, u32[]{:S(2)}) collective-permute-start(bf16[144,256]{1,0:T(8,128)(2,1)S(1)} %get-tuple-element.41), channel_id=1, source_target_pairs={{0,8},{4,12},{8,0},{12,4},{1,9},{5,13},{9,1},{13,5},{2,10},{6,14},... | collective-permute-start | bytes 221192 | tf_op jit(solution)/shard_map/ppermute | solution.py:376
  6.3 0.1 collective-permute-start.2
  6.3 2.1 %local.1 = (f32[64,2048]{1,0:T(8,128)S(1)}, f32[64,2048]{1,0:T(8,128)S(1)}, f32[3,2048]{1,0:T(4,128)S(1)}, f32[64,8192]{1,0:T(8,128)S(1)}, s32[1,8192]{1,0:T(1,1...) custom-call(f32[16,2048]{1,0:T(8,128)S(1)} %get-tuple-element.26.mis, ...), custom_call_target="tpu_custom_call" | custom-call | flops 1073741824 | bytes 8388608 | tf_op jit(solution)/shard_map/local/pallas_call | solution.py:468
  8.4 0.0 collective-permute-done.refs_1_
  8.4 0.7 %collective-permute-done.1.refs_2_ = bf16[144,256]{1,0:T(8,128)(2,1)S(1)} collective-permute-done((bf16[144,256]{1,0:T(8,128)(2,1)S(1)}, bf16[144,256]{1,0:T(8,128)(2,1)S(1)}, u32[]{:S(2)}, u32[]{:S(2)}) %collective-permute-start.1) | collective-permute-done | bytes 73760 | tf_op jit(solution)/shard_map/ppermute | solution.py:376
  9.1 1.4 %collective-permute-done.2.refs_3_ = bf16[144,256]{1,0:T(8,128)(2,1)S(1)} collective-permute-done((bf16[144,256]{1,0:T(8,128)(2,1)S(1)}, bf16[144,256]{1,0:T(8,128)(2,1)S(1)}, u32[]{:S(2)}, u32[]{:S(2)}) %collective-permute-start.2) | collective-permute-done | bytes 73760 | tf_op jit(solution)/shard_map/ppermute | solution.py:376
  10.5 9.8 %main.1 = (bf16[64,256]{1,0:T(8,128)(2,1)}, bf16[64,2048]{1,0:T(8,128)(2,1)}, f32[24,128]{1,0:T(8,128)S(1)}, f32[1,2048]{1,0:T(1,128)S(1)}) custom-call(f32[64,2048]{1,0:T(8,128)S(1)} %get-tuple-element.25.part, f32[16,2048]{1,0:T(8,128)S(1)} %get-tuple-element.26.misc, bf16[256,2048]{1,0:T(8,128)(2,1)S(1)} %get-tuple-element.27.target_hot, ...), custom_call_target="tpu_custom_call" | custom-call | tf_op jit(solution)/shard_map/main/pallas_call | solution.py:488
  20.3 1.5 %collective-permute-start.3 = (f32[6,128]{1,0:T(8,128)S(1)}, f32[6,128]{1,0:T(8,128)S(1)}, u32[]{:S(2)}, u32[]{:S(2)}) collective-permute-start(f32[6,128]{1,0:T(8,128)S(1)} %get-tuple-element.47), channel_id=1, source_target_pairs={{0,8},{4,12},{8,0},{12,4},{1,9},{5,13},{9,1},{13,5},{2,10},{6,14},... | collective-permute-start | bytes 9224 | tf_op jit(solution)/shard_map/ppermute | solution.py:376
  21.9 0.0 collective-permute-start.5
  21.9 0.6 %collective-permute-start.4 = (f32[6,128]{1,0:T(8,128)S(1)}, f32[6,128]{1,0:T(8,128)S(1)}, u32[]{:S(2)}, u32[]{:S(2)}) collective-permute-start(f32[6,128]{1,0:T(8,128)S(1)} %get-tuple-element.49), channel_id=1, source_target_pairs={{0,4},{4,0},{8,12},{12,8},{1,5},{5,1},{9,13},{13,9},{2,6},{6,2},{1... | collective-permute-start | bytes 9224 | tf_op jit(solution)/shard_map/ppermute | solution.py:376
  22.4 0.4 %late.1 = f32[6,128]{1,0:T(8,128)S(1)} custom-call(f32[3,2048]{1,0:T(4,128)S(1)} %get-tuple-element.32.unit, f32[1,2048]{1,0:T(1,128)S(1)} %get-tuple-element.46.edge_grad, bf16[256,2048]{1,0:T(8,128)(2,1)S(1)} %get-tuple-element.27.target_hot), custom_call_target="tpu_custom_call" | custom-call | flops 268435456 | bytes 2097152 | tf_op jit(solution)/shard_map/late/pallas_call | solution.py:510
  22.8 1.1 %collective-permute-done.3 = f32[6,128]{1,0:T(8,128)S(1)} collective-permute-done((f32[6,128]{1,0:T(8,128)S(1)}, f32[6,128]{1,0:T(8,128)S(1)}, u32[]{:S(2)}, u32[]{:S(2)}) %collective-permute-start.3) | collective-permute-done | bytes 3104 | tf_op jit(solution)/shard_map/ppermute | solution.py:376
  23.9 1.0 %collective-permute-done.5 = f32[6,128]{1,0:T(8,128)S(1)} collective-permute-done((f32[6,128]{1,0:T(8,128)S(1)}, f32[6,128]{1,0:T(8,128)S(1)}, u32[]{:S(2)}, u32[]{:S(2)}) %collective-permute-start.5) | collective-permute-done | bytes 3104 | tf_op jit(solution)/shard_map/ppermute | solution.py:376
  24.9 0.0 collective-permute-done.4
  24.9 3.6 %collective-permute-start.8 = (f32[6,128]{1,0:T(8,128)S(1)}, f32[6,128]{1,0:T(8,128)S(1)}, u32[]{:S(2)}, u32[]{:S(2)}) collective-permute-start(f32[6,128]{1,0:T(8,128)S(1)} %add_add_fusion.1), channel_id=1, source_target_pairs={{0,3},{1,2},{2,1},{3,0},{4,7},{5,6},{6,5},{7,4},{8,11},{9,10},{10,... | collective-permute-start | bytes 9224 | tf_op jit(solution)/shard_map/ppermute | solution.py:376
  28.5 0.0 collective-permute-start.7
  28.5 0.8 %collective-permute-start.6 = (f32[6,128]{1,0:T(8,128)S(1)}, f32[6,128]{1,0:T(8,128)S(1)}, u32[]{:S(2)}, u32[]{:S(2)}) collective-permute-start(f32[6,128]{1,0:T(8,128)S(1)} %add_add_fusion.1), channel_id=1, source_target_pairs={{0,1},{1,0},{2,3},{3,2},{4,5},{5,4},{6,7},{7,6},{8,9},{9,8},{10,11... | collective-permute-start | bytes 9224 | tf_op jit(solution)/shard_map/ppermute | solution.py:376
  29.3 1.0 %collective-permute-done.8 = f32[6,128]{1,0:T(8,128)S(1)} collective-permute-done((f32[6,128]{1,0:T(8,128)S(1)}, f32[6,128]{1,0:T(8,128)S(1)}, u32[]{:S(2)}, u32[]{:S(2)}) %collective-permute-start.8) | collective-permute-done | bytes 3104 | tf_op jit(solution)/shard_map/ppermute | solution.py:376
  30.4 2.7 %collective-permute-done.7 = f32[6,128]{1,0:T(8,128)S(1)} collective-permute-done((f32[6,128]{1,0:T(8,128)S(1)}, f32[6,128]{1,0:T(8,128)S(1)}, u32[]{:S(2)}, u32[]{:S(2)}) %collective-permute-start.7) | collective-permute-done | bytes 3104 | tf_op jit(solution)/shard_map/ppermute | solution.py:376
  33.0 0.0 collective-permute-done.6
  33.1 0.6 %pad_maximum_fusion = f32[3,256]{1,0:T(4,128)} fusion(f32[3,128]{1,0:T(4,128)S(1)} %get-tuple-element.51, f32[3,128]{1,0:T(4,128)S(1)} %get-tuple-element.50), kind=kLoop, calls=%fused_computation | loop fusion | flops 768 | bytes 6144 | tf_op jit(solution)/shard_map/concatenate | solution.py:521
  (4 shorter events, 0.0 us)
Async XLA Ops:
  3.2 5.3 %collective-permute-start = (bf16[144,256]{1,0:T(8,128)(2,1)S(1)}, bf16[144,256]{1,0:T(8,128)(2,1)S(1)}, u32[]{:S(2)}, u32[]{:S(2)}) collective-permute-start(bf16[144,256]{1,0:T(8,128)(2,1)S(1)} %get-tuple-element.40), channel_id=1, source_target_pairs={{0,4},{4,0},{8,12},{12,8},{1,5},{5,1},{9,13},{13,9},{2,6},{6,2},{1... | collective-permute-start | bytes 221192 | tf_op jit(solution)/shard_map/ppermute | solution.py:376
  3.7 5.4 %collective-permute-start.1 = (bf16[144,256]{1,0:T(8,128)(2,1)S(1)}, bf16[144,256]{1,0:T(8,128)(2,1)S(1)}, u32[]{:S(2)}, u32[]{:S(2)}) collective-permute-start(bf16[144,256]{1,0:T(8,128)(2,1)S(1)} %get-tuple-element.41), channel_id=1, source_target_pairs={{0,8},{4,12},{8,0},{12,4},{1,9},{5,13},{9,1},{13,5},{2,10},{6,14},... | collective-permute-start | bytes 221192 | tf_op jit(solution)/shard_map/ppermute | solution.py:376
  6.3 4.2 %collective-permute-start.2 = (bf16[144,256]{1,0:T(8,128)(2,1)S(1)}, bf16[144,256]{1,0:T(8,128)(2,1)S(1)}, u32[]{:S(2)}, u32[]{:S(2)}) collective-permute-start(bf16[144,256]{1,0:T(8,128)(2,1)S(1)} %get-tuple-element.42), channel_id=1, source_target_pairs={{0,12},{4,8},{8,4},{12,0},{1,13},{5,9},{9,5},{13,1},{2,14},{6,10},... | collective-permute-start | bytes 221192 | tf_op jit(solution)/shard_map/ppermute | solution.py:376
  20.3 3.6 %collective-permute-start.3 = (f32[6,128]{1,0:T(8,128)S(1)}, f32[6,128]{1,0:T(8,128)S(1)}, u32[]{:S(2)}, u32[]{:S(2)}) collective-permute-start(f32[6,128]{1,0:T(8,128)S(1)} %get-tuple-element.47), channel_id=1, source_target_pairs={{0,8},{4,12},{8,0},{12,4},{1,9},{5,13},{9,1},{13,5},{2,10},{6,14},... | collective-permute-start | bytes 9224 | tf_op jit(solution)/shard_map/ppermute | solution.py:376
  21.9 3.0 %collective-permute-start.5 = (f32[6,128]{1,0:T(8,128)S(1)}, f32[6,128]{1,0:T(8,128)S(1)}, u32[]{:S(2)}, u32[]{:S(2)}) collective-permute-start(f32[6,128]{1,0:T(8,128)S(1)} %get-tuple-element.48), channel_id=1, source_target_pairs={{0,12},{4,8},{8,4},{12,0},{1,13},{5,9},{9,5},{13,1},{2,14},{6,10},... | collective-permute-start | bytes 9224 | tf_op jit(solution)/shard_map/ppermute | solution.py:376
  21.9 3.0 %collective-permute-start.4 = (f32[6,128]{1,0:T(8,128)S(1)}, f32[6,128]{1,0:T(8,128)S(1)}, u32[]{:S(2)}, u32[]{:S(2)}) collective-permute-start(f32[6,128]{1,0:T(8,128)S(1)} %get-tuple-element.49), channel_id=1, source_target_pairs={{0,4},{4,0},{8,12},{12,8},{1,5},{5,1},{9,13},{13,9},{2,6},{6,2},{1... | collective-permute-start | bytes 9224 | tf_op jit(solution)/shard_map/ppermute | solution.py:376
  24.9 5.5 %collective-permute-start.8 = (f32[6,128]{1,0:T(8,128)S(1)}, f32[6,128]{1,0:T(8,128)S(1)}, u32[]{:S(2)}, u32[]{:S(2)}) collective-permute-start(f32[6,128]{1,0:T(8,128)S(1)} %add_add_fusion.1), channel_id=1, source_target_pairs={{0,3},{1,2},{2,1},{3,0},{4,7},{5,6},{6,5},{7,4},{8,11},{9,10},{10,... | collective-permute-start | bytes 9224 | tf_op jit(solution)/shard_map/ppermute | solution.py:376
  28.5 4.5 %collective-permute-start.7 = (f32[6,128]{1,0:T(8,128)S(1)}, f32[6,128]{1,0:T(8,128)S(1)}, u32[]{:S(2)}, u32[]{:S(2)}) collective-permute-start(f32[6,128]{1,0:T(8,128)S(1)} %add_add_fusion.1), channel_id=1, source_target_pairs={{0,2},{1,3},{2,0},{3,1},{4,6},{5,7},{6,4},{7,5},{8,10},{9,11},{10,... | collective-permute-start | bytes 9224 | tf_op jit(solution)/shard_map/ppermute | solution.py:376
  28.5 4.5 %collective-permute-start.6 = (f32[6,128]{1,0:T(8,128)S(1)}, f32[6,128]{1,0:T(8,128)S(1)}, u32[]{:S(2)}, u32[]{:S(2)}) collective-permute-start(f32[6,128]{1,0:T(8,128)S(1)} %add_add_fusion.1), channel_id=1, source_target_pairs={{0,1},{1,0},{2,3},{3,2},{4,5},{5,4},{6,7},{7,6},{8,9},{9,8},{10,11... | collective-permute-start | bytes 9224 | tf_op jit(solution)/shard_map/ppermute | solution.py:376

commit v7 on v6

--- a/solution.py
+++ b/solution.py
@@ -17,7 +17,7 @@
 BF = jnp.bfloat16
 F32 = jnp.float32
 VMEM_LIMIT = 24 * 1024 * 1024
-GRAPH_ORDER, CHAN_ORDER = "213", "123"
+GRAPH_ORDER, CHAN_ORDER = "213", "132"
 GIN_F, GOUT_F, GOUT_B, GIN_B = 1, 2, 1, 1
 WF = 2048
 WB = 2048

time: 33.8 us -> 33.7 us (level)
  no operation moved by 1% of the time
where the time goes in v7:
time: 33.7 us; the launch traced here: 33.5 us
  Pallas kernels  14.8 us (44%)
  starting transfers between devices  9.53 us (28%)
  waiting for transfers between devices  7.96 us (24%)
  between operations  0.68 us (2%)
  other arithmetic  0.61 us (2%)
    pallas_call x1, Pallas kernels, shards(): pl.pallas_call(functools.partial(main_kernel, peers, ecap, math.sqrt(NODE...  9.8 us
    ppermute x9, starting transfers between devices, exchange(): return lax.ppermute(values, axis, [(i, i ^ distance) for i in range(count)])  9.53 us
    ppermute x9, waiting for transfers between devices, exchange(): return lax.ppermute(values, axis, [(i, i ^ distance) for i in range(count)])  7.96 us
    pallas_call x1, Pallas kernels, shards(): pl.pallas_call(functools.partial(prep_kernel, peers), name='prep', in_spe...  2.52 us
    pallas_call x1, Pallas kernels, shards(): pl.pallas_call(functools.partial(local_kernel, ecap), name='local', in_sp...  2.06 us
  transfers between devices with their start and end apart: 9, of which 6 were waited for; matrix products, arithmetic and copies ran while one was open for 0% of the time, Pallas kernels for 7%

profile of v7, /device:TPU:0, one launch (start us, length us, event | category | flops | bytes accessed | tf_op | source)
XLA Modules:
  0.0 33.5 jit_solution(2132406700148783887)
XLA Ops:
  0.6 2.5 %prep.1 = (f32[64,2048]{1,0:T(8,128)S(1)}, f32[16,2048]{1,0:T(8,128)S(1)}, bf16[256,2048]{1,0:T(8,128)(2,1)S(1)}, bf16[64,256]{1,0:T(8,128)(2,1)S(1)}, bf16[64,2...) custom-call(bf16[256,256]{1,0:T(8,128)(2,1)} %refs_0_.2, ...), custom_call_target="tpu_custom_call" | custom-call | tf_op jit(solution)/shard_map/prep/pallas_call | solution.py:442
  3.2 0.5 %collective-permute-start = (bf16[144,256]{1,0:T(8,128)(2,1)S(1)}, bf16[144,256]{1,0:T(8,128)(2,1)S(1)}, u32[]{:S(2)}, u32[]{:S(2)}) collective-permute-start(bf16[144,256]{1,0:T(8,128)(2,1)S(1)} %get-tuple-element.40), channel_id=1, source_target_pairs={{0,4},{4,0},{8,12},{12,8},{1,5},{5,1},{9,13},{13,9},{2,6},{6,2},{1... | collective-permute-start | bytes 221192 | tf_op jit(solution)/shard_map/ppermute | solution.py:376
  3.7 2.6 %collective-permute-start.1 = (bf16[144,256]{1,0:T(8,128)(2,1)S(1)}, bf16[144,256]{1,0:T(8,128)(2,1)S(1)}, u32[]{:S(2)}, u32[]{:S(2)}) collective-permute-start(bf16[144,256]{1,0:T(8,128)(2,1)S(1)} %get-tuple-element.41), channel_id=1, source_target_pairs={{0,8},{4,12},{8,0},{12,4},{1,9},{5,13},{9,1},{13,5},{2,10},{6,14},... | collective-permute-start | bytes 221192 | tf_op jit(solution)/shard_map/ppermute | solution.py:376
  6.3 0.1 collective-permute-start.2
  6.3 2.1 %local.1 = (f32[64,2048]{1,0:T(8,128)S(1)}, f32[64,2048]{1,0:T(8,128)S(1)}, f32[3,2048]{1,0:T(4,128)S(1)}, f32[64,8192]{1,0:T(8,128)S(1)}, s32[1,8192]{1,0:T(1,1...) custom-call(f32[16,2048]{1,0:T(8,128)S(1)} %get-tuple-element.26.mis, ...), custom_call_target="tpu_custom_call" | custom-call | flops 1073741824 | bytes 8388608 | tf_op jit(solution)/shard_map/local/pallas_call | solution.py:468
  8.4 0.0 collective-permute-done.refs_1_
  8.4 0.7 %collective-permute-done.1.refs_2_ = bf16[144,256]{1,0:T(8,128)(2,1)S(1)} collective-permute-done((bf16[144,256]{1,0:T(8,128)(2,1)S(1)}, bf16[144,256]{1,0:T(8,128)(2,1)S(1)}, u32[]{:S(2)}, u32[]{:S(2)}) %collective-permute-start.1) | collective-permute-done | bytes 73760 | tf_op jit(solution)/shard_map/ppermute | solution.py:376
  9.1 1.4 %collective-permute-done.2.refs_3_ = bf16[144,256]{1,0:T(8,128)(2,1)S(1)} collective-permute-done((bf16[144,256]{1,0:T(8,128)(2,1)S(1)}, bf16[144,256]{1,0:T(8,128)(2,1)S(1)}, u32[]{:S(2)}, u32[]{:S(2)}) %collective-permute-start.2) | collective-permute-done | bytes 73760 | tf_op jit(solution)/shard_map/ppermute | solution.py:376
  10.5 9.8 %main.1 = (bf16[64,256]{1,0:T(8,128)(2,1)}, bf16[64,2048]{1,0:T(8,128)(2,1)}, f32[24,128]{1,0:T(8,128)S(1)}, f32[1,2048]{1,0:T(1,128)S(1)}) custom-call(f32[64,2048]{1,0:T(8,128)S(1)} %get-tuple-element.25.part, f32[16,2048]{1,0:T(8,128)S(1)} %get-tuple-element.26.misc, bf16[256,2048]{1,0:T(8,128)(2,1)S(1)} %get-tuple-element.27.target_hot, ...), custom_call_target="tpu_custom_call" | custom-call | tf_op jit(solution)/shard_map/main/pallas_call | solution.py:488
  20.3 1.5 %collective-permute-start.3 = (f32[6,128]{1,0:T(8,128)S(1)}, f32[6,128]{1,0:T(8,128)S(1)}, u32[]{:S(2)}, u32[]{:S(2)}) collective-permute-start(f32[6,128]{1,0:T(8,128)S(1)} %get-tuple-element.47), channel_id=1, source_target_pairs={{0,8},{4,12},{8,0},{12,4},{1,9},{5,13},{9,1},{13,5},{2,10},{6,14},... | collective-permute-start | bytes 9224 | tf_op jit(solution)/shard_map/ppermute | solution.py:376
  21.9 0.0 collective-permute-start.5
  21.9 0.6 %collective-permute-start.4 = (f32[6,128]{1,0:T(8,128)S(1)}, f32[6,128]{1,0:T(8,128)S(1)}, u32[]{:S(2)}, u32[]{:S(2)}) collective-permute-start(f32[6,128]{1,0:T(8,128)S(1)} %get-tuple-element.49), channel_id=1, source_target_pairs={{0,4},{4,0},{8,12},{12,8},{1,5},{5,1},{9,13},{13,9},{2,6},{6,2},{1... | collective-permute-start | bytes 9224 | tf_op jit(solution)/shard_map/ppermute | solution.py:376
  22.4 0.4 %late.1 = f32[6,128]{1,0:T(8,128)S(1)} custom-call(f32[3,2048]{1,0:T(4,128)S(1)} %get-tuple-element.32.unit, f32[1,2048]{1,0:T(1,128)S(1)} %get-tuple-element.46.edge_grad, bf16[256,2048]{1,0:T(8,128)(2,1)S(1)} %get-tuple-element.27.target_hot), custom_call_target="tpu_custom_call" | custom-call | flops 268435456 | bytes 2097152 | tf_op jit(solution)/shard_map/late/pallas_call | solution.py:510
  22.8 1.1 %collective-permute-done.3 = f32[6,128]{1,0:T(8,128)S(1)} collective-permute-done((f32[6,128]{1,0:T(8,128)S(1)}, f32[6,128]{1,0:T(8,128)S(1)}, u32[]{:S(2)}, u32[]{:S(2)}) %collective-permute-start.3) | collective-permute-done | bytes 3104 | tf_op jit(solution)/shard_map/ppermute | solution.py:376
  23.9 1.0 %collective-permute-done.5 = f32[6,128]{1,0:T(8,128)S(1)} collective-permute-done((f32[6,128]{1,0:T(8,128)S(1)}, f32[6,128]{1,0:T(8,128)S(1)}, u32[]{:S(2)}, u32[]{:S(2)}) %collective-permute-start.5) | collective-permute-done | bytes 3104 | tf_op jit(solution)/shard_map/ppermute | solution.py:376
  24.9 0.0 collective-permute-done.4
  24.9 2.6 %collective-permute-start.8 = (f32[6,128]{1,0:T(8,128)S(1)}, f32[6,128]{1,0:T(8,128)S(1)}, u32[]{:S(2)}, u32[]{:S(2)}) collective-permute-start(f32[6,128]{1,0:T(8,128)S(1)} %add_add_fusion.1), channel_id=1, source_target_pairs={{0,2},{1,3},{2,0},{3,1},{4,6},{5,7},{6,4},{7,5},{8,10},{9,11},{10,... | collective-permute-start | bytes 9224 | tf_op jit(solution)/shard_map/ppermute | solution.py:376
  27.5 1.3 %collective-permute-start.7 = (f32[6,128]{1,0:T(8,128)S(1)}, f32[6,128]{1,0:T(8,128)S(1)}, u32[]{:S(2)}, u32[]{:S(2)}) collective-permute-start(f32[6,128]{1,0:T(8,128)S(1)} %add_add_fusion.1), channel_id=1, source_target_pairs={{0,3},{1,2},{2,1},{3,0},{4,7},{5,6},{6,5},{7,4},{8,11},{9,10},{10,... | collective-permute-start | bytes 9224 | tf_op jit(solution)/shard_map/ppermute | solution.py:376
  28.9 0.2 collective-permute-start.6
  29.1 0.4 %collective-permute-done.8 = f32[6,128]{1,0:T(8,128)S(1)} collective-permute-done((f32[6,128]{1,0:T(8,128)S(1)}, f32[6,128]{1,0:T(8,128)S(1)}, u32[]{:S(2)}, u32[]{:S(2)}) %collective-permute-start.8) | collective-permute-done | bytes 3104 | tf_op jit(solution)/shard_map/ppermute | solution.py:376
  29.5 3.5 %collective-permute-done.7 = f32[6,128]{1,0:T(8,128)S(1)} collective-permute-done((f32[6,128]{1,0:T(8,128)S(1)}, f32[6,128]{1,0:T(8,128)S(1)}, u32[]{:S(2)}, u32[]{:S(2)}) %collective-permute-start.7) | collective-permute-done | bytes 3104 | tf_op jit(solution)/shard_map/ppermute | solution.py:376
  32.9 0.0 collective-permute-done.6
  32.9 0.6 %pad_maximum_fusion = f32[3,256]{1,0:T(4,128)} fusion(f32[3,128]{1,0:T(4,128)S(1)} %get-tuple-element.51, f32[3,128]{1,0:T(4,128)S(1)} %get-tuple-element.50), kind=kLoop, calls=%fused_computation | loop fusion | flops 768 | bytes 6144 | tf_op jit(solution)/shard_map/concatenate | solution.py:521
  (4 shorter events, 0.0 us)
Async XLA Ops:
  3.2 5.3 %collective-permute-start = (bf16[144,256]{1,0:T(8,128)(2,1)S(1)}, bf16[144,256]{1,0:T(8,128)(2,1)S(1)}, u32[]{:S(2)}, u32[]{:S(2)}) collective-permute-start(bf16[144,256]{1,0:T(8,128)(2,1)S(1)} %get-tuple-element.40), channel_id=1, source_target_pairs={{0,4},{4,0},{8,12},{12,8},{1,5},{5,1},{9,13},{13,9},{2,6},{6,2},{1... | collective-permute-start | bytes 221192 | tf_op jit(solution)/shard_map/ppermute | solution.py:376
  3.7 5.4 %collective-permute-start.1 = (bf16[144,256]{1,0:T(8,128)(2,1)S(1)}, bf16[144,256]{1,0:T(8,128)(2,1)S(1)}, u32[]{:S(2)}, u32[]{:S(2)}) collective-permute-start(bf16[144,256]{1,0:T(8,128)(2,1)S(1)} %get-tuple-element.41), channel_id=1, source_target_pairs={{0,8},{4,12},{8,0},{12,4},{1,9},{5,13},{9,1},{13,5},{2,10},{6,14},... | collective-permute-start | bytes 221192 | tf_op jit(solution)/shard_map/ppermute | solution.py:376
  6.3 4.2 %collective-permute-start.2 = (bf16[144,256]{1,0:T(8,128)(2,1)S(1)}, bf16[144,256]{1,0:T(8,128)(2,1)S(1)}, u32[]{:S(2)}, u32[]{:S(2)}) collective-permute-start(bf16[144,256]{1,0:T(8,128)(2,1)S(1)} %get-tuple-element.42), channel_id=1, source_target_pairs={{0,12},{4,8},{8,4},{12,0},{1,13},{5,9},{9,5},{13,1},{2,14},{6,10},... | collective-permute-start | bytes 221192 | tf_op jit(solution)/shard_map/ppermute | solution.py:376
  20.3 3.6 %collective-permute-start.3 = (f32[6,128]{1,0:T(8,128)S(1)}, f32[6,128]{1,0:T(8,128)S(1)}, u32[]{:S(2)}, u32[]{:S(2)}) collective-permute-start(f32[6,128]{1,0:T(8,128)S(1)} %get-tuple-element.47), channel_id=1, source_target_pairs={{0,8},{4,12},{8,0},{12,4},{1,9},{5,13},{9,1},{13,5},{2,10},{6,14},... | collective-permute-start | bytes 9224 | tf_op jit(solution)/shard_map/ppermute | solution.py:376
  21.9 3.0 %collective-permute-start.5 = (f32[6,128]{1,0:T(8,128)S(1)}, f32[6,128]{1,0:T(8,128)S(1)}, u32[]{:S(2)}, u32[]{:S(2)}) collective-permute-start(f32[6,128]{1,0:T(8,128)S(1)} %get-tuple-element.48), channel_id=1, source_target_pairs={{0,12},{4,8},{8,4},{12,0},{1,13},{5,9},{9,5},{13,1},{2,14},{6,10},... | collective-permute-start | bytes 9224 | tf_op jit(solution)/shard_map/ppermute | solution.py:376
  21.9 3.0 %collective-permute-start.4 = (f32[6,128]{1,0:T(8,128)S(1)}, f32[6,128]{1,0:T(8,128)S(1)}, u32[]{:S(2)}, u32[]{:S(2)}) collective-permute-start(f32[6,128]{1,0:T(8,128)S(1)} %get-tuple-element.49), channel_id=1, source_target_pairs={{0,4},{4,0},{8,12},{12,8},{1,5},{5,1},{9,13},{13,9},{2,6},{6,2},{1... | collective-permute-start | bytes 9224 | tf_op jit(solution)/shard_map/ppermute | solution.py:376
  24.9 4.6 %collective-permute-start.8 = (f32[6,128]{1,0:T(8,128)S(1)}, f32[6,128]{1,0:T(8,128)S(1)}, u32[]{:S(2)}, u32[]{:S(2)}) collective-permute-start(f32[6,128]{1,0:T(8,128)S(1)} %add_add_fusion.1), channel_id=1, source_target_pairs={{0,2},{1,3},{2,0},{3,1},{4,6},{5,7},{6,4},{7,5},{8,10},{9,11},{10,... | collective-permute-start | bytes 9224 | tf_op jit(solution)/shard_map/ppermute | solution.py:376
  27.5 5.4 %collective-permute-start.7 = (f32[6,128]{1,0:T(8,128)S(1)}, f32[6,128]{1,0:T(8,128)S(1)}, u32[]{:S(2)}, u32[]{:S(2)}) collective-permute-start(f32[6,128]{1,0:T(8,128)S(1)} %add_add_fusion.1), channel_id=1, source_target_pairs={{0,3},{1,2},{2,1},{3,0},{4,7},{5,6},{6,5},{7,4},{8,11},{9,10},{10,... | collective-permute-start | bytes 9224 | tf_op jit(solution)/shard_map/ppermute | solution.py:376
  28.9 4.1 %collective-permute-start.6 = (f32[6,128]{1,0:T(8,128)S(1)}, f32[6,128]{1,0:T(8,128)S(1)}, u32[]{:S(2)}, u32[]{:S(2)}) collective-permute-start(f32[6,128]{1,0:T(8,128)S(1)} %add_add_fusion.1), channel_id=1, source_target_pairs={{0,1},{1,0},{2,3},{3,2},{4,5},{5,4},{6,7},{7,6},{8,9},{9,8},{10,11... | collective-permute-start | bytes 9224 | tf_op jit(solution)/shard_map/ppermute | solution.py:376
